TPU v7x, 512 devices: a whole 4x4x16 slice. The times are simulated.
512 devices in a mesh: tile: 32 (over x, z_hi, core), dir: 16 (over y, z_lo).
Axes of the slice: x: 4, y: 4, z: 16 (z_hi: 4, z_lo: 4; z = z_hi * 4 + z_lo), core: 2. Of those that a mesh axis runs over, the one named last changes fastest.
Arguments:
- background_prev: float32 [64, 256, 128], P(None, 'tile'), may hold values from -6 to 6
- background_now: float32 [64, 256, 128], P(None, 'tile'), may hold values from -6 to 6
- stiffness: bfloat16 [64, 256, 128], P(None, 'tile'), may hold values from 0.039794922 to 0.19921875
- drift_terms: bfloat16 [3, 64, 256, 128], P(None, None, 'tile'), may hold values from -0.079589844 to 0.079589844
- born_prev: bfloat16 [64, 64, 256, 128], P('dir', None, 'tile'), may hold values from -6 to 6
- born_now: bfloat16 [64, 64, 256, 128], P('dir', None, 'tile'), may hold values from -6 to 6
- pieces: bfloat16 [64, 1024, 32, 128], P('dir', 'tile'), may hold values from -6 to 6
- piece_target: int32 [1024, 1], P('tile'), may hold values from 0 to 31; in each aligned block of 32 rows (0 to 31, 32 to 63, ...) at most 2 rows name the same one
- piece_block: int32 [1024], P('tile'), may hold values from 0 to 15
- wavelet: float32 [4], replicated, may hold values from -24 to 24
- source_cell: int32 [3], replicated, may hold values from 0 to 63
- receiver_z: int32 [256], replicated, may hold values from 0 to 63
- receiver_x: int32 [256], replicated, may hold values from 0 to 255
- receiver_y: int32 [256], replicated, may hold values from 0 to 127
Outputs:
- born_field: float32 [64, 64, 256, 128], P('dir', None, 'tile')
- traces: float32 [64, 4, 256], P('dir')
Inputs may be any that keep to these rules, and one draw needn't show every extreme that they name: `piece_target`: in each aligned block of 32 rows (the rows of one device) no tile is named by more than 2 rows; in some blocks a tile is named by exactly 2 rows.
All inputs are finite; a program needn't handle non-finite values.
Results may differ from a plain program's by a relative error of at most 0.0005.
Values may be sent and summed in bfloat16 or wider, within the bound.
No kernel may reach another device: no remote copies, remote signals or barrier semaphores. Data moves between devices by JAX's collectives and lax.ppermute only.
A program may use at most 128 MiB of HBM per device.

v0:
```python
import jax
import jax.numpy as jnp
from jax import lax
from jax.sharding import PartitionSpec as P

CX = 8
ITERS = 4
ZPARTS = 2
CAP = 2


SECOND_TAPS = (-205.0 / 72.0, 8.0 / 5.0, -1.0 / 5.0, 8.0 / 315.0, -1.0 / 560.0)
FIRST_TAPS = (0.0, 4.0 / 5.0, -1.0 / 5.0, 4.0 / 105.0, -1.0 / 280.0)


def padded_2(block, sides, width):
    for axis, dim in sides:
        count = lax.axis_size(axis)
        forward = [(i, i + 1) for i in range(count - 1)]
        backward = [(target, source) for source, target in forward]
        low = lax.ppermute(
            lax.slice_in_dim(block, block.shape[dim] - width, None, axis=dim), axis, forward
        )
        high = lax.ppermute(lax.slice_in_dim(block, 0, width, axis=dim), axis, backward)
        block = jnp.concatenate([low, block, high], axis=dim)
    return block


def shifted(padded, interior, spatial, offset):
    starts = [4, 4, 4]
    starts[spatial] = 4 + offset
    leading = padded.ndim - 3
    window = tuple(
        [slice(None)] * leading
        + [slice(starts[which], starts[which] + interior[which]) for which in range(3)]
    )
    return padded[window]


def operate(padded, stiff_wide, drift_wide):
    interior = stiff_wide.shape
    center = shifted(padded, interior, 0, 0)
    second = 3.0 * SECOND_TAPS[0] * center
    slopes = jnp.zeros_like(center)
    for spatial in range(3):
        gradient = jnp.zeros_like(center)
        for offset in range(1, 5):
            forward = shifted(padded, interior, spatial, offset)
            backward = shifted(padded, interior, spatial, -offset)
            second = second + SECOND_TAPS[offset] * (forward + backward)
            gradient = gradient + FIRST_TAPS[offset] * (forward - backward)
        slopes = slopes + drift_wide[spatial] * gradient
    return stiff_wide * second + slopes


def faces(born_present, background_part):
    return (padded_2(born_present, (("tile", 2),), 4), padded_2(background_part, (("tile", 2),), 4))


def assemble(pieces, piece_target, piece_block, tile_count):
    targets = piece_target[:, 0]
    row_count = targets.shape[0]
    positions = jnp.arange(row_count)
    before = (targets[:, None] == targets[None, :]) & (positions[None, :] < positions[:, None])
    arrival = jnp.sum(before.astype(jnp.int32), axis=1)
    slot_ids = targets * CAP + arrival
    placing = (slot_ids[:, None] == jnp.arange(tile_count * CAP)[None, :]).astype(jnp.bfloat16)
    outgoing = jnp.einsum(
        "krzy,rs->kszy", pieces, placing, preferred_element_type=jnp.float32
    ).astype(jnp.bfloat16)
    labels = jnp.dot(
        (piece_block + 1).astype(jnp.bfloat16)[None, :], placing, preferred_element_type=jnp.float32
    ).astype(jnp.bfloat16)
    incoming, arrived = (
        lax.all_to_all(outgoing, "tile", split_axis=1, concat_axis=1, tiled=True),
        lax.all_to_all(labels, "tile", split_axis=1, concat_axis=1, tiled=True),
    )
    wanted = (jnp.arange(ZPARTS * CX) + 1).astype(jnp.float32)
    picking = (
        (arrived[0][:, None].astype(jnp.float32) == wanted[None, :])
        .astype(jnp.bfloat16)
        .reshape(-1, ZPARTS, CX)
    )
    perturb = jnp.einsum("kszy,spx->kpzxy", incoming, picking, preferred_element_type=jnp.float32)
    return perturb.reshape(pieces.shape[0], ZPARTS * pieces.shape[2], CX, pieces.shape[3])


def local(
    background_prev,
    background_now,
    stiffness,
    drift_terms,
    born_prev,
    born_now,
    pieces,
    piece_target,
    piece_block,
    wavelet,
    source_cell,
    receiver_z,
    receiver_x,
    receiver_y,
):
    tile_count = lax.axis_size("tile")
    tile_place = lax.axis_index("tile")
    depth_cells, width_cells, height_cells = background_now.shape
    stiff_wide = stiffness.astype(jnp.float32)
    drift_wide = drift_terms.astype(jnp.float32)
    perturb = assemble(pieces, piece_target, piece_block, tile_count)
    across_axis = (tile_place * width_cells + jnp.arange(width_cells))[None, :, None]
    height_axis = jnp.arange(height_cells)[None, None, :]
    earlier_born = born_prev.astype(jnp.float32)
    current_born = born_now.astype(jnp.float32)
    local_x = receiver_x - tile_place * width_cells
    inside = ((local_x >= 0) & (local_x < width_cells)).astype(jnp.float32)
    flat_index = (
        receiver_z * width_cells + jnp.clip(local_x, 0, width_cells - 1)
    ) * height_cells + receiver_y
    slab_cells = depth_cells // lax.axis_size("dir")
    slab_start = lax.axis_index("dir") * slab_cells
    previous = lax.dynamic_slice_in_dim(background_prev, slab_start, slab_cells, 0)
    present = lax.dynamic_slice_in_dim(background_now, slab_start, slab_cells, 0)
    slab_stiff = lax.dynamic_slice_in_dim(stiff_wide, slab_start, slab_cells, 0)
    slab_drift = lax.dynamic_slice_in_dim(drift_wide, slab_start, slab_cells, 1)
    depth_axis = (slab_start + jnp.arange(slab_cells))[:, None, None]
    source_mask = (
        (depth_axis == source_cell[0])
        & (across_axis == source_cell[1])
        & (height_axis == source_cell[2])
    ).astype(jnp.float32)
    records = []
    for step_index in range(ITERS):
        deeper = padded_2(present[None], (("dir", 1),), 4)
        born_wide, back_wide = faces(current_born, deeper)
        local_accel = operate(
            jnp.pad(back_wide[0], ((0, 0), (0, 0), (4, 4))), slab_stiff, slab_drift
        )
        acceleration = lax.all_gather(local_accel, "dir", axis=0, tiled=True)
        previous, present = (
            present,
            2.0 * present - previous + local_accel + wavelet[step_index] * source_mask,
        )
        born_padded = jnp.pad(born_wide, ((0, 0), (4, 4), (0, 0), (4, 4)))
        following = (
            2.0 * current_born
            - earlier_born
            + operate(born_padded, stiff_wide, drift_wide)
            + perturb * acceleration
        )
        records.append(
            jnp.take(following.reshape(following.shape[0], -1), flat_index, axis=1)
            * inside[None, :]
        )
        earlier_born, current_born = (current_born, following)
    traces = lax.psum(jnp.stack(records, axis=1), "tile")
    return (current_born, traces)


def solution(mesh):
    placed = (
        P(None, "tile", None),
        P(None, "tile", None),
        P(None, "tile", None),
        P(None, None, "tile", None),
        P("dir", None, "tile", None),
        P("dir", None, "tile", None),
        P("dir", "tile", None, None),
        P("tile", None),
        P("tile"),
        P(),
        P(),
        P(),
        P(),
        P(),
    )
    return jax.shard_map(
        local,
        mesh=mesh,
        in_specs=placed,
        out_specs=(P("dir", None, "tile", None), P("dir", None, None)),
        check_vma=False,
    )
```

profile of v0, /device:TPU:1, one launch (start us, length us, event | category | flops | bytes accessed | tf_op | source)
XLA Modules:
  0.0 743.8 jit_solution(9172707135732427772)
XLA Ops:
  0.6 0.9 convert_reduce_fusion.1
  2.2 0.8 fusion.9
  3.8 19.2 %all-to-all-start = ((bf16[1,32,2]{2,0,1:T(2,128)(2,1)}), bf16[1,32,2]{2,0,1:T(2,128)(2,1)S(1)}, u32[]{:S(2)}, u32[]{:S(2)}) async-start(bf16[1,32,2]{2,0,1:T(2,128)(2,1)} %all_to_all.12), calls=%async_computation | async-start | bytes 32768 | tf_op jit(solution)/shard_map/all_to_all | solution.py:76
  23.1 0.8 convert_bitcast_fusion
  23.9 2.8 copy.42
  26.7 10.4 %all-to-all-done = bf16[1,32,2]{2,0,1:T(2,128)(2,1)S(1)} async-done(((bf16[1,32,2]{2,0,1:T(2,128)(2,1)}), bf16[1,32,2]{2,0,1:T(2,128)(2,1)S(1)}, u32[]{:S(2)}, u32[]{:S(2)}) %all-to-all-start) | async-done | bytes 160 | tf_op jit(solution)/shard_map/all_to_all | solution.py:76
  37.1 5.0 all-to-all-start.1
  42.8 1.3 collective-permute-start.3
  44.1 4.0 collective-permute-start.2
  48.1 1.1 fusion.119
  49.3 2.9 collective-permute-start.1
  52.1 7.0 collective-permute-start
  59.3 0.7 fusion.125
  62.0 0.9 slice_bitcast_fusion.2
  63.0 66.5 %collective-permute-done.3 = f32[1,4,8,128]{3,2,1,0:T(8,128)S(1)} collective-permute-done((f32[1,4,8,128]{3,2,1,0:T(8,128)S(1)}, f32[1,4,8,128]{3,2,1,0:T(8,128)S(1)}, u32[]{:S(2)}, u32[]{:S(2)}) %collective-permute-start.3) | collective-permute-done | bytes 16416 | tf_op jit(solution)/shard_map/ppermute | solution.py:24
  129.5 3.7 collective-permute-start.5
  133.2 23.6 %collective-permute-start.4 = (f32[1,12,4,128]{3,2,1,0:T(4,128)S(1)}, f32[1,12,4,128]{3,2,1,0:T(4,128)S(1)}, u32[]{:S(2)}, u32[]{:S(2)}) collective-permute-start(f32[1,12,4,128]{3,2,1,0:T(4,128)S(1)} %get-tuple-element.32), channel_id=1, source_target_pairs={{0,16},{16,32},{32,48},{48,64},{64,80},{80,96},{96,112},{112,128},... | collective-permute-start | bytes 73736 | tf_op jit(solution)/shard_map/ppermute | solution.py:21
  157.5 4.2 collective-permute-done.5
  161.7 1.5 fusion.39
  163.3 1.3 collective-permute-start.9
  164.6 4.0 collective-permute-start.8
  169.4 1.9 collective-permute-start.11
  171.4 8.9 %collective-permute-start.10 = (f32[1,12,4,128]{3,2,1,0:T(4,128)S(1)}, f32[1,12,4,128]{3,2,1,0:T(4,128)S(1)}, u32[]{:S(2)}, u32[]{:S(2)}) collective-permute-start(f32[1,12,4,128]{3,2,1,0:T(4,128)S(1)} %get-tuple-element.30), channel_id=1, source_target_pairs={{0,16},{16,32},{32,48},{48,64},{64,80},{80,96},{96,112},{112,128},... | collective-permute-start | bytes 73736 | tf_op jit(solution)/shard_map/ppermute | solution.py:21
  180.3 41.5 %all_gather.12 = f32[64,8,128]{2,1,0:T(8,128)} all-gather(f32[4,8,128]{2,1,0:T(8,128)S(1)} %get-tuple-element.14), channel_id=1, replica_groups=mesh['tile'=32,'dir'=16] {'dir'}, dimensions={0}, use_global_device_ids=true | all-gather | bytes 278528 | tf_op jit(solution)/shard_map/all_gather | solution.py:138
  221.8 1.5 fusion.108
  223.3 1.3 collective-permute-start.15
  224.6 4.0 collective-permute-start.14
  228.7 5.3 select_maximum_fusion.6
  233.9 3.0 fusion.6
  237.0 7.7 %multiply_add_fusion.3 = f32[4,64,8,128]{3,2,1,0:T(8,128)S(1)} fusion(f32[4,64,8,128]{3,2,1,0:T(8,128)S(1)} %bitcast.132, f32[4,72,16,136]{3,2,1,0:T(8,128)S(1)} %copy-done.2, f32[4,64,4,128]{3,2,1,0:T(4,128)S(1)} %copy-done.15, f32[4,64,8,128]{3,2,1,0:T(8,128)S(1)} %convert_element_type.62, f32[4,64,4,128]{3,2,1,0:T(4,128)} %collective-permute-done, ...), kind=kLoop, calls=%fused_computation.110 | loop fusion | flops 23855104 | bytes 22806528 | tf_op jit(solution)/shard_map/add | solution.py:145
  244.9 4.6 collective-permute-start.7
  249.5 7.4 collective-permute-start.6
  257.0 1.9 collective-permute-start.17
  258.9 7.5 %collective-permute-start.16 = (f32[1,12,4,128]{3,2,1,0:T(4,128)S(1)}, f32[1,12,4,128]{3,2,1,0:T(4,128)S(1)}, u32[]{:S(2)}, u32[]{:S(2)}) collective-permute-start(f32[1,12,4,128]{3,2,1,0:T(4,128)S(1)} %get-tuple-element.28), channel_id=1, source_target_pairs={{0,16},{16,32},{32,48},{48,64},{64,80},{80,96},{96,112},{112,128},... | collective-permute-start | bytes 73736 | tf_op jit(solution)/shard_map/ppermute | solution.py:21
  266.5 40.0 %all_gather.13 = f32[64,8,128]{2,1,0:T(8,128)S(1)} all-gather(f32[4,8,128]{2,1,0:T(8,128)S(1)} %get-tuple-element.12), channel_id=1, replica_groups=mesh['tile'=32,'dir'=16] {'dir'}, dimensions={0}, use_global_device_ids=true | all-gather | bytes 278528 | tf_op jit(solution)/shard_map/all_gather | solution.py:138
  306.6 2.7 select_maximum_fusion.4
  309.3 6.1 multiply_add_fusion.2
  315.6 6.9 collective-permute-start.13
  322.4 4.1 collective-permute-start.12
  326.5 2.2 fusion.42
  328.8 1.3 collective-permute-start.21
  330.1 4.5 collective-permute-start.20
  334.6 40.8 %all_gather.14 = f32[64,8,128]{2,1,0:T(8,128)S(1)} all-gather(f32[4,8,128]{2,1,0:T(8,128)S(1)} %get-tuple-element.10), channel_id=1, replica_groups=mesh['tile'=32,'dir'=16] {'dir'}, dimensions={0}, use_global_device_ids=true | all-gather | bytes 278528 | tf_op jit(solution)/shard_map/all_gather | solution.py:138
  375.5 5.0 collective-permute-start.23
  380.5 6.4 collective-permute-start.22
  386.9 2.7 select_maximum_fusion.2
  389.6 6.1 multiply_add_fusion.1
  395.7 1.0 copy-done.3
  396.7 1.1 fusion.116
  397.8 1.9 collective-permute-start.19
  399.7 7.6 %collective-permute-start.18 = (f32[4,64,4,128]{3,2,1,0:T(4,128)}, f32[4,64,4,128]{3,2,1,0:T(4,128)}, u32[]{:S(2)}, u32[]{:S(2)}) collective-permute-start(f32[4,64,4,128]{3,2,1,0:T(4,128)} %get-tuple-element.15), channel_id=1, source_target_pairs={{0,16},{16,32},{32,48},{48,64},{64,80},{80,96},{96,112},{112,128},... | collective-permute-start | bytes 1572872 | tf_op jit(solution)/shard_map/ppermute | solution.py:21
  407.3 0.9 fusion.56
  408.2 52.4 %all_gather.15 = f32[64,8,128]{2,1,0:T(8,128)} all-gather(f32[4,8,128]{2,1,0:T(8,128)S(1)} %fusion.56), channel_id=1, replica_groups=mesh['tile'=32,'dir'=16] {'dir'}, dimensions={0}, use_global_device_ids=true | all-gather | bytes 278528 | tf_op jit(solution)/shard_map/all_gather | solution.py:138
  460.6 16.0 %copy.45 = f32[4,64,8,128]{0,3,2,1:T(8,128)} copy(f32[4,64,8,128]{3,2,1,0:T(8,128)S(1)} %multiply_add_fusion.3) | data formatting | bytes 2097152 | tf_op jit(solution)/shard_map/add | solution.py:145
  476.6 11.3 %gather_fusion = f32[256,4]{1,0:T(8,128)S(1)} fusion(f32[4,65536]{0,1:T(8,128)} %bitcast.128, s32[1024]{0:T(1024)S(1)} %pad_clamp_fusion), kind=kCustom, calls=%fused_computation.clone | custom fusion | bytes 9216 | tf_op jit(solution)/shard_map/jit(_take)/gather | solution.py:151
  487.9 16.0 %copy.46 = f32[4,64,8,128]{0,3,2,1:T(8,128)} copy(f32[4,64,8,128]{3,2,1,0:T(8,128)S(1)} %multiply_add_fusion.2) | data formatting | bytes 2097152 | tf_op jit(solution)/shard_map/add | solution.py:145
  503.9 11.9 %gather_fusion.1 = f32[256,4]{1,0:T(8,128)} fusion(f32[4,65536]{0,1:T(8,128)} %bitcast.130, s32[1024]{0:T(1024)S(1)} %pad_clamp_fusion), kind=kCustom, calls=%fused_computation.1.clone | custom fusion | bytes 9216 | tf_op jit(solution)/shard_map/jit(_take)/gather | solution.py:151
  515.8 16.0 %copy.47 = f32[4,64,8,128]{0,3,2,1:T(8,128)} copy(f32[4,64,8,128]{3,2,1,0:T(8,128)S(1)} %copy-done.4) | data formatting | bytes 2097152 | tf_op jit(solution)/shard_map/add | solution.py:145
  531.7 11.9 %gather_fusion.2 = f32[256,4]{1,0:T(8,128)} fusion(f32[4,65536]{0,1:T(8,128)} %bitcast.131, s32[1024]{0:T(1024)S(1)} %pad_clamp_fusion), kind=kCustom, calls=%fused_computation.2.clone | custom fusion | bytes 9216 | tf_op jit(solution)/shard_map/jit(_take)/gather | solution.py:151
  543.6 3.8 select_maximum_fusion
  547.4 8.5 %multiply_add_fusion = f32[4,64,8,128]{3,2,1,0:T(8,128)} fusion(f32[4,64,8,128]{3,2,1,0:T(8,128)S(1)} %bitcast.135, f32[4,72,16,136]{3,2,1,0:T(8,128)S(1)} %select_maximum_fusion, f32[4,64,4,128]{3,2,1,0:T(4,128)} %collective-permute-done.19, f32[4,64,8,128]{3,2,1,0:T(8,128)S(1)} %copy-done.4, f32[4,64,4,128]{3,2,1,0:T(4,128)} %collective-permute-done.18, ...), kind=kLoop, calls=%fused_computation.107 | loop fusion | flops 23592960 | bytes 23330816 | tf_op jit(solution)/shard_map/add | solution.py:145
  555.9 16.9 %copy.48 = f32[4,64,8,128]{0,3,2,1:T(8,128)} copy(f32[4,64,8,128]{3,2,1,0:T(8,128)} %multiply_add_fusion) | data formatting | bytes 2097152 | tf_op jit(solution)/shard_map/add | solution.py:145
  572.8 11.3 %gather_fusion.3 = f32[256,4]{1,0:T(8,128)S(1)} fusion(f32[4,65536]{0,1:T(8,128)} %bitcast.129, s32[1024]{0:T(1024)S(1)} %pad_clamp_fusion), kind=kCustom, calls=%fused_computation.3.clone | custom fusion | bytes 9216 | tf_op jit(solution)/shard_map/jit(_take)/gather | solution.py:151
  584.6 159.1 %psum.7 = f32[4,4,256]{2,1,0:T(4,128)} all-reduce(f32[4,4,256]{2,1,0:T(4,128)S(1)} %pad_maximum_fusion.12), channel_id=1, replica_groups=mesh['tile'=32,'dir'=16] {'tile'}, use_global_device_ids=true, to_apply=%region_1.3 | all-reduce | flops 4096 | bytes 32768 | tf_op jit(solution)/shard_map/psum | solution.py:155
  (111 shorter events, 6.9 us)
Async XLA Ops:
  0.6 22.4 %copy-start = (bf16[4,32,32,128]{3,2,1,0:T(8,128)(2,1)S(1)}, bf16[4,32,32,128]{3,2,1,0:T(8,128)(2,1)}, u32[]{:S(2)}) copy-start(bf16[4,32,32,128]{3,2,1,0:T(8,128)(2,1)} %param.22) | copy-start | bytes 3145732
  3.8 33.3 %all-to-all-start = ((bf16[1,32,2]{2,0,1:T(2,128)(2,1)}), bf16[1,32,2]{2,0,1:T(2,128)(2,1)S(1)}, u32[]{:S(2)}, u32[]{:S(2)}) async-start(bf16[1,32,2]{2,0,1:T(2,128)(2,1)} %all_to_all.12), calls=%async_computation | async-start | bytes 32768 | tf_op jit(solution)/shard_map/all_to_all | solution.py:76
  23.9 24.2 %copy-start.5 = (bf16[4,64,8,128]{3,2,1,0:T(8,128)(2,1)S(1)}, bf16[4,64,8,128]{3,2,1,0:T(8,128)(2,1)}, u32[]{:S(2)}) copy-start(bf16[4,64,8,128]{3,2,1,0:T(8,128)(2,1)} %param.21) | copy-start | bytes 1572868
  23.9 35.3 %copy-start.17 = (bf16[3,64,8,128]{3,2,1,0:T(8,128)(2,1)S(1)}, bf16[3,64,8,128]{3,2,1,0:T(8,128)(2,1)}, u32[]{:S(2)}) copy-start(bf16[3,64,8,128]{3,2,1,0:T(8,128)(2,1)} %param.19) | copy-start | bytes 1179652
  26.7 32.6 %copy-start.21 = (s32[3]{0:T(128)S(1)}, s32[3]{0:T(128)}, u32[]{:S(2)}) copy-start(s32[3]{0:T(128)} %param.26) | copy-start | bytes 40
  26.7 34.6 %copy-start.22 = (f32[4]{0:T(128)S(1)}, f32[4]{0:T(128)}, u32[]{:S(2)}) copy-start(f32[4]{0:T(128)} %param.25) | copy-start | bytes 52
  26.7 35.3 %copy-start.23 = (s32[256]{0:T(256)S(1)}, s32[256]{0:T(256)}, u32[]{:S(2)}) copy-start(s32[256]{0:T(256)} %param.29) | copy-start | bytes 3076
  26.7 35.3 %copy-start.24 = (s32[256]{0:T(256)S(1)}, s32[256]{0:T(256)}, u32[]{:S(2)}) copy-start(s32[256]{0:T(256)} %param.28) | copy-start | bytes 3076
  26.7 35.3 %copy-start.25 = (s32[256]{0:T(256)S(1)}, s32[256]{0:T(256)}, u32[]{:S(2)}) copy-start(s32[256]{0:T(256)} %param.27) | copy-start | bytes 3076
  26.7 130.8 %copy-start.20 = (bf16[64,8,128]{2,1,0:T(8,128)(2,1)S(1)}, bf16[64,8,128]{2,1,0:T(8,128)(2,1)}, u32[]{:S(2)}) copy-start(bf16[64,8,128]{2,1,0:T(8,128)(2,1)} %param.18) | copy-start | bytes 393220
  37.1 196.8 %all-to-all-start.1 = ((bf16[4,64,32,128]{3,2,0,1:T(8,128)(2,1)}), bf16[4,64,32,128]{3,2,0,1:T(8,128)(2,1)}, u32[]{:S(2)}, u32[]{:S(2)}) async-start(bf16[4,64,32,128]{3,2,0,1:T(8,128)(2,1)} %copy.42), calls=%async_computation.1 | async-start | bytes 4194304 | tf_op jit(solution)/shard_map/all_to_all | solution.py:75
  42.8 86.6 %collective-permute-start.3 = (f32[1,4,8,128]{3,2,1,0:T(8,128)S(1)}, f32[1,4,8,128]{3,2,1,0:T(8,128)S(1)}, u32[]{:S(2)}, u32[]{:S(2)}) collective-permute-start(f32[1,4,8,128]{3,2,1,0:T(8,128)S(1)} %dynamic-slice_bitcast_fusion.3), channel_id=1, source_target_pairs={{1,0},{2,1},{3,2},{4,3},{5,4},{6,5},{7,6},{8,7},{9,8},{10,9},{11,1... | collective-permute-start | bytes 49160 | tf_op jit(solution)/shard_map/ppermute | solution.py:24
  44.1 85.3 %collective-permute-start.2 = (f32[1,4,8,128]{3,2,1,0:T(8,128)S(1)}, f32[1,4,8,128]{3,2,1,0:T(8,128)S(1)}, u32[]{:S(2)}, u32[]{:S(2)}) collective-permute-start(f32[1,4,8,128]{3,2,1,0:T(8,128)S(1)} %dynamic-slice_bitcast_fusion.3), channel_id=1, source_target_pairs={{0,1},{1,2},{2,3},{3,4},{4,5},{5,6},{6,7},{7,8},{8,9},{9,10},{10,1... | collective-permute-start | bytes 49160 | tf_op jit(solution)/shard_map/ppermute | solution.py:21
  49.3 179.4 %collective-permute-start.1 = (f32[4,64,4,128]{3,2,1,0:T(4,128)}, f32[4,64,4,128]{3,2,1,0:T(4,128)S(1)}, u32[]{:S(2)}, u32[]{:S(2)}) collective-permute-start(f32[4,64,4,128]{3,2,1,0:T(4,128)} %get-tuple-element.25), channel_id=1, source_target_pairs={{16,0},{32,16},{48,32},{64,48},{80,64},{96,80},{112,96},{128,112},... | collective-permute-start | bytes 1572872 | tf_op jit(solution)/shard_map/ppermute | solution.py:24
  52.1 176.5 %collective-permute-start = (f32[4,64,4,128]{3,2,1,0:T(4,128)}, f32[4,64,4,128]{3,2,1,0:T(4,128)}, u32[]{:S(2)}, u32[]{:S(2)}) collective-permute-start(f32[4,64,4,128]{3,2,1,0:T(4,128)} %get-tuple-element.24), channel_id=1, source_target_pairs={{0,16},{16,32},{32,48},{48,64},{64,80},{80,96},{96,112},{112,128},... | collective-permute-start | bytes 1572872 | tf_op jit(solution)/shard_map/ppermute | solution.py:21
  59.3 174.6 %copy-start.13 = (f32[3,64,8,128]{3,2,1,0:T(8,128)}, f32[3,64,8,128]{3,2,1,0:T(8,128)S(1)}, u32[]{:S(2)}) copy-start(f32[3,64,8,128]{3,2,1,0:T(8,128)S(1)} %convert_element_type.65) | copy-start | bytes 2359300
  129.5 32.2 %collective-permute-start.5 = (f32[1,12,4,128]{3,2,1,0:T(4,128)S(1)}, f32[1,12,4,128]{3,2,1,0:T(4,128)S(1)}, u32[]{:S(2)}, u32[]{:S(2)}) collective-permute-start(f32[1,12,4,128]{3,2,1,0:T(4,128)S(1)} %get-tuple-element.33), channel_id=1, source_target_pairs={{16,0},{32,16},{48,32},{64,48},{80,64},{96,80},{112,96},{128,112},... | collective-permute-start | bytes 73736 | tf_op jit(solution)/shard_map/ppermute | solution.py:24
  133.2 28.6 %collective-permute-start.4 = (f32[1,12,4,128]{3,2,1,0:T(4,128)S(1)}, f32[1,12,4,128]{3,2,1,0:T(4,128)S(1)}, u32[]{:S(2)}, u32[]{:S(2)}) collective-permute-start(f32[1,12,4,128]{3,2,1,0:T(4,128)S(1)} %get-tuple-element.32), channel_id=1, source_target_pairs={{0,16},{16,32},{32,48},{48,64},{64,80},{80,96},{96,112},{112,128},... | collective-permute-start | bytes 73736 | tf_op jit(solution)/shard_map/ppermute | solution.py:21
  163.3 5.5 collective-permute-start.9
  164.6 4.8 collective-permute-start.8
  169.4 52.3 %collective-permute-start.11 = (f32[1,12,4,128]{3,2,1,0:T(4,128)S(1)}, f32[1,12,4,128]{3,2,1,0:T(4,128)S(1)}, u32[]{:S(2)}, u32[]{:S(2)}) collective-permute-start(f32[1,12,4,128]{3,2,1,0:T(4,128)S(1)} %get-tuple-element.31), channel_id=1, source_target_pairs={{16,0},{32,16},{48,32},{64,48},{80,64},{96,80},{112,96},{128,112},... | collective-permute-start | bytes 73736 | tf_op jit(solution)/shard_map/ppermute | solution.py:24
  171.4 50.4 %collective-permute-start.10 = (f32[1,12,4,128]{3,2,1,0:T(4,128)S(1)}, f32[1,12,4,128]{3,2,1,0:T(4,128)S(1)}, u32[]{:S(2)}, u32[]{:S(2)}) collective-permute-start(f32[1,12,4,128]{3,2,1,0:T(4,128)S(1)} %get-tuple-element.30), channel_id=1, source_target_pairs={{0,16},{16,32},{32,48},{48,64},{64,80},{80,96},{96,112},{112,128},... | collective-permute-start | bytes 73736 | tf_op jit(solution)/shard_map/ppermute | solution.py:21
  223.3 33.6 %collective-permute-start.15 = (f32[1,4,8,128]{3,2,1,0:T(8,128)S(1)}, f32[1,4,8,128]{3,2,1,0:T(8,128)S(1)}, u32[]{:S(2)}, u32[]{:S(2)}) collective-permute-start(f32[1,4,8,128]{3,2,1,0:T(8,128)S(1)} %get-tuple-element.11), channel_id=1, source_target_pairs={{1,0},{2,1},{3,2},{4,3},{5,4},{6,5},{7,6},{8,7},{9,8},{10,9},{11,1... | collective-permute-start | bytes 49160 | tf_op jit(solution)/shard_map/ppermute | solution.py:24
  224.6 32.3 %collective-permute-start.14 = (f32[1,4,8,128]{3,2,1,0:T(8,128)S(1)}, f32[1,4,8,128]{3,2,1,0:T(8,128)S(1)}, u32[]{:S(2)}, u32[]{:S(2)}) collective-permute-start(f32[1,4,8,128]{3,2,1,0:T(8,128)S(1)} %get-tuple-element.11), channel_id=1, source_target_pairs={{0,1},{1,2},{2,3},{3,4},{4,5},{5,6},{6,7},{7,8},{8,9},{9,10},{10,1... | collective-permute-start | bytes 49160 | tf_op jit(solution)/shard_map/ppermute | solution.py:21
  228.6 5.3 copy-start.14
  233.9 3.1 copy-start.2
  233.9 3.1 copy-start.15
  244.7 64.6 %copy-start.6 = (bf16[4,64,8,128]{3,2,1,0:T(8,128)(2,1)S(1)}, bf16[4,64,8,128]{3,2,1,0:T(8,128)(2,1)}, u32[]{:S(2)}) copy-start(bf16[4,64,8,128]{3,2,1,0:T(8,128)(2,1)} %param.21) | copy-start | bytes 1572868
  244.7 64.6 %copy-start.7 = (f32[64,8,128]{2,1,0:T(8,128)S(1)}, f32[64,8,128]{2,1,0:T(8,128)}, u32[]{:S(2)}) copy-start(f32[64,8,128]{2,1,0:T(8,128)} %get-tuple-element.21) | copy-start | bytes 786436
  244.7 64.6 %copy-start.9 = (f32[64,8,128]{2,1,0:T(8,128)S(1)}, f32[64,8,128]{2,1,0:T(8,128)}, u32[]{:S(2)}) copy-start(f32[64,8,128]{2,1,0:T(8,128)} %get-tuple-element.22) | copy-start | bytes 786436
  244.7 64.6 %copy-start.11 = (f32[64,8,128]{2,1,0:T(8,128)S(1)}, f32[64,8,128]{2,1,0:T(8,128)}, u32[]{:S(2)}) copy-start(f32[64,8,128]{2,1,0:T(8,128)} %get-tuple-element.23) | copy-start | bytes 786436
  244.9 61.7 %collective-permute-start.7 = (f32[4,64,4,128]{3,2,1,0:T(4,128)S(1)}, f32[4,64,4,128]{3,2,1,0:T(4,128)S(1)}, u32[]{:S(2)}, u32[]{:S(2)}) collective-permute-start(f32[4,64,4,128]{3,2,1,0:T(4,128)S(1)} %get-tuple-element.20), channel_id=1, source_target_pairs={{16,0},{32,16},{48,32},{64,48},{80,64},{96,80},{112,96},{128,112},... | collective-permute-start | bytes 1572872 | tf_op jit(solution)/shard_map/ppermute | solution.py:24
  249.5 57.1 %collective-permute-start.6 = (f32[4,64,4,128]{3,2,1,0:T(4,128)S(1)}, f32[4,64,4,128]{3,2,1,0:T(4,128)S(1)}, u32[]{:S(2)}, u32[]{:S(2)}) collective-permute-start(f32[4,64,4,128]{3,2,1,0:T(4,128)S(1)} %get-tuple-element.19), channel_id=1, source_target_pairs={{0,16},{16,32},{32,48},{48,64},{64,80},{80,96},{96,112},{112,128},... | collective-permute-start | bytes 1572872 | tf_op jit(solution)/shard_map/ppermute | solution.py:21
  257.0 49.5 %collective-permute-start.17 = (f32[1,12,4,128]{3,2,1,0:T(4,128)S(1)}, f32[1,12,4,128]{3,2,1,0:T(4,128)S(1)}, u32[]{:S(2)}, u32[]{:S(2)}) collective-permute-start(f32[1,12,4,128]{3,2,1,0:T(4,128)S(1)} %get-tuple-element.29), channel_id=1, source_target_pairs={{16,0},{32,16},{48,32},{64,48},{80,64},{96,80},{112,96},{128,112},... | collective-permute-start | bytes 73736 | tf_op jit(solution)/shard_map/ppermute | solution.py:24
  258.9 47.6 %collective-permute-start.16 = (f32[1,12,4,128]{3,2,1,0:T(4,128)S(1)}, f32[1,12,4,128]{3,2,1,0:T(4,128)S(1)}, u32[]{:S(2)}, u32[]{:S(2)}) collective-permute-start(f32[1,12,4,128]{3,2,1,0:T(4,128)S(1)} %get-tuple-element.28), channel_id=1, source_target_pairs={{0,16},{16,32},{32,48},{48,64},{64,80},{80,96},{96,112},{112,128},... | collective-permute-start | bytes 73736 | tf_op jit(solution)/shard_map/ppermute | solution.py:21
  315.6 71.3 %collective-permute-start.13 = (f32[4,64,4,128]{3,2,1,0:T(4,128)S(1)}, f32[4,64,4,128]{3,2,1,0:T(4,128)S(1)}, u32[]{:S(2)}, u32[]{:S(2)}) collective-permute-start(f32[4,64,4,128]{3,2,1,0:T(4,128)S(1)} %get-tuple-element.18), channel_id=1, source_target_pairs={{16,0},{32,16},{48,32},{64,48},{80,64},{96,80},{112,96},{128,112},... | collective-permute-start | bytes 1572872 | tf_op jit(solution)/shard_map/ppermute | solution.py:24
  322.4 64.5 %collective-permute-start.12 = (f32[4,64,4,128]{3,2,1,0:T(4,128)S(1)}, f32[4,64,4,128]{3,2,1,0:T(4,128)S(1)}, u32[]{:S(2)}, u32[]{:S(2)}) collective-permute-start(f32[4,64,4,128]{3,2,1,0:T(4,128)S(1)} %get-tuple-element.17), channel_id=1, source_target_pairs={{0,16},{16,32},{32,48},{48,64},{64,80},{80,96},{96,112},{112,128},... | collective-permute-start | bytes 1572872 | tf_op jit(solution)/shard_map/ppermute | solution.py:21
  328.8 46.7 %collective-permute-start.21 = (f32[1,4,8,128]{3,2,1,0:T(8,128)S(1)}, f32[1,4,8,128]{3,2,1,0:T(8,128)S(1)}, u32[]{:S(2)}, u32[]{:S(2)}) collective-permute-start(f32[1,4,8,128]{3,2,1,0:T(8,128)S(1)} %get-tuple-element.9), channel_id=1, source_target_pairs={{1,0},{2,1},{3,2},{4,3},{5,4},{6,5},{7,6},{8,7},{9,8},{10,9},{11,1... | collective-permute-start | bytes 49160 | tf_op jit(solution)/shard_map/ppermute | solution.py:24
  330.1 45.4 %collective-permute-start.20 = (f32[1,4,8,128]{3,2,1,0:T(8,128)S(1)}, f32[1,4,8,128]{3,2,1,0:T(8,128)S(1)}, u32[]{:S(2)}, u32[]{:S(2)}) collective-permute-start(f32[1,4,8,128]{3,2,1,0:T(8,128)S(1)} %get-tuple-element.9), channel_id=1, source_target_pairs={{0,1},{1,2},{2,3},{3,4},{4,5},{5,6},{6,7},{7,8},{8,9},{9,10},{10,1... | collective-permute-start | bytes 49160 | tf_op jit(solution)/shard_map/ppermute | solution.py:21
  375.5 31.8 %collective-permute-start.23 = (f32[1,12,4,128]{3,2,1,0:T(4,128)S(1)}, f32[1,12,4,128]{3,2,1,0:T(4,128)S(1)}, u32[]{:S(2)}, u32[]{:S(2)}) collective-permute-start(f32[1,12,4,128]{3,2,1,0:T(4,128)S(1)} %get-tuple-element.27), channel_id=1, source_target_pairs={{16,0},{32,16},{48,32},{64,48},{80,64},{96,80},{112,96},{128,112},... | collective-permute-start | bytes 73736 | tf_op jit(solution)/shard_map/ppermute | solution.py:24
  380.5 26.8 %collective-permute-start.22 = (f32[1,12,4,128]{3,2,1,0:T(4,128)S(1)}, f32[1,12,4,128]{3,2,1,0:T(4,128)S(1)}, u32[]{:S(2)}, u32[]{:S(2)}) collective-permute-start(f32[1,12,4,128]{3,2,1,0:T(4,128)S(1)} %get-tuple-element.26), channel_id=1, source_target_pairs={{0,16},{16,32},{32,48},{48,64},{64,80},{80,96},{96,112},{112,128},... | collective-permute-start | bytes 73736 | tf_op jit(solution)/shard_map/ppermute | solution.py:21
  395.7 1.0 copy-start.3
  397.8 145.8 %collective-permute-start.19 = (f32[4,64,4,128]{3,2,1,0:T(4,128)}, f32[4,64,4,128]{3,2,1,0:T(4,128)}, u32[]{:S(2)}, u32[]{:S(2)}) collective-permute-start(f32[4,64,4,128]{3,2,1,0:T(4,128)} %get-tuple-element.16), channel_id=1, source_target_pairs={{16,0},{32,16},{48,32},{64,48},{80,64},{96,80},{112,96},{128,112},... | collective-permute-start | bytes 1572872 | tf_op jit(solution)/shard_map/ppermute | solution.py:24
  399.7 143.9 %collective-permute-start.18 = (f32[4,64,4,128]{3,2,1,0:T(4,128)}, f32[4,64,4,128]{3,2,1,0:T(4,128)}, u32[]{:S(2)}, u32[]{:S(2)}) collective-permute-start(f32[4,64,4,128]{3,2,1,0:T(4,128)} %get-tuple-element.15), channel_id=1, source_target_pairs={{0,16},{16,32},{32,48},{48,64},{64,80},{80,96},{96,112},{112,128},... | collective-permute-start | bytes 1572872 | tf_op jit(solution)/shard_map/ppermute | solution.py:21
  487.9 27.9 %copy-start.4 = (f32[4,64,8,128]{3,2,1,0:T(8,128)S(1)}, f32[4,64,8,128]{3,2,1,0:T(8,128)}, u32[]{:S(2)}) copy-start(f32[4,64,8,128]{3,2,1,0:T(8,128)} %copy-done.3) | copy-start | bytes 3145732
  543.6 3.8 copy-start.8
  543.6 3.8 copy-start.10
  543.6 3.8 copy-start.12
  543.6 3.8 copy-start.16
  555.9 28.2 %copy-start.18 = (f32[256,4]{1,0:T(8,128)S(1)}, f32[256,4]{1,0:T(8,128)}, u32[]{:S(2)}) copy-start(f32[256,4]{1,0:T(8,128)} %gather_fusion.1) | copy-start | bytes 12292
  555.9 28.2 %copy-start.19 = (f32[256,4]{1,0:T(8,128)S(1)}, f32[256,4]{1,0:T(8,128)}, u32[]{:S(2)}) copy-start(f32[256,4]{1,0:T(8,128)} %gather_fusion.2) | copy-start | bytes 12292
  555.9 187.8 %copy-start.1 = (bf16[4,32,32,128]{3,2,1,0:T(8,128)(2,1)S(1)}, bf16[4,32,32,128]{3,2,1,0:T(8,128)(2,1)}, u32[]{:S(2)}) copy-start(bf16[4,32,32,128]{3,2,1,0:T(8,128)(2,1)} %param.22) | copy-start | bytes 3145732
where the time goes:
time: 748 us; the launch traced here: 744 us
  blocking collectives  334 us (45%)
  starting transfers between devices  147 us (20%)
  local copies, waits for them, and re-layouts  122 us (16%)
  waiting for transfers between devices  81.9 us (11%)
  other arithmetic  52.8 us (7%)
    all_gather x4, blocking collectives, local(): acceleration = lax.all_gather(local_accel, 'dir', axis=0, tiled=True)  175 us
    psum x1, blocking collectives, local(): traces = lax.psum(jnp.stack(records, axis=1), 'tile')  159 us
    ppermute x12, starting transfers between devices, padded_2(): lax.ppermute(lax.slice_in_dim(block, block.shape[dim] - width, None, axis...  89 us
    ppermute x12, waiting for transfers between devices, padded_2(): lax.ppermute(lax.slice_in_dim(block, 0, width, axis=dim), axis, backward)  70.7 us
    add x4, local copies, waits for them, and re-layouts, local(): 2.0 * current_born - earlier_born  64.8 us
    gather x4, local copies, waits for them, and re-layouts, local(): jnp.take(following.reshape(following.shape[0], -1), flat_index, axis=1)  46.3 us
    ppermute x12, starting transfers between devices, padded_2(): lax.ppermute(lax.slice_in_dim(block, 0, width, axis=dim), axis, backward)  34 us
    add x4, other arithmetic, local(): 2.0 * current_born - earlier_born  28.4 us
  transfers between devices with their start and end apart: 26, of which 4 were waited for; matrix products, arithmetic and copies ran while one was open for 17% of the time, Pallas kernels for 0%

commit v1 on v0

v1 whole, which is shorter than its diff:
```python
import functools

import jax
import jax.numpy as jnp
import numpy as np
from jax import lax
from jax.experimental import pallas as pl
from jax.experimental.pallas import tpu as pltpu
from jax.sharding import PartitionSpec as P

ITERS = 4
CAP = 2
F = 5

CENTRE = -14350.0
SECOND = (0.0, 8064.0, -1008.0, 128.0, -9.0)
FIRST = (0.0, 672.0, -168.0, 32.0, -3.0)

BF = jnp.bfloat16
F32 = jnp.float32
VM = pltpu.VMEM
SM = pltpu.SMEM


def vspec():
    return pl.BlockSpec(memory_space=VM)


def sspec():
    return pl.BlockSpec(memory_space=SM)


def params():
    return pltpu.CompilerParams(vmem_limit_bytes=16 * 1024 * 1024)


def tap_matrix(ny):
    both = np.zeros((ny, 2 * ny), np.float32)
    for k in range(1, 5):
        for y in range(ny):
            for at, sign in ((y + k, 1.0), (y - k, -1.0)):
                if 0 <= at < ny:
                    both[at, y] = SECOND[k]
                    both[at, ny + y] = sign * FIRST[k]
    return np.concatenate([both, both], axis=0)


def pack_kernel(target, block, pieces, packed, count, label):
    directions, rows, zb, ny = pieces.shape
    tiles = packed.shape[0]

    def clear(t, c):
        count[t] = 0
        for a in range(CAP):
            label[t * CAP + a] = 0
        return c

    lax.fori_loop(0, tiles, clear, 0)

    def place(r, c):
        t = target[r]
        a = count[t]
        count[t] = a + 1
        label[t * CAP + a] = block[r] + 1
        for k in range(directions):
            at = pl.multiple_of((a * directions + k) * zb, zb)
            packed[t, pl.ds(at, zb), :] = pieces[k, r]
        return c

    lax.fori_loop(0, rows, place, 0)
    row_at = lax.broadcasted_iota(jnp.int32, (16, ny), 0)

    def name(t, c):
        held = jnp.zeros((16, ny), jnp.int32)
        for a in range(CAP):
            held = jnp.where(row_at == a, label[t * CAP + a], held)
        packed[t, CAP * directions * zb :, :] = held.astype(F32).astype(BF)
        return c

    lax.fori_loop(0, tiles, name, 0)


def pack(pieces, target, block, tiles):
    k, rows, zb, ny = pieces.shape
    return pl.pallas_call(
        pack_kernel,
        out_shape=jax.ShapeDtypeStruct((tiles, CAP * k * zb + 16, ny), pieces.dtype),
        in_specs=[sspec(), sspec(), vspec()],
        out_specs=vspec(),
        scratch_shapes=[SM((tiles,), jnp.int32), SM((tiles * CAP,), jnp.int32)],
        compiler_params=params(),
        name="pack",
    )(target, block, pieces)


def list_kernel(rz, rx, ry, where, *outs):
    row_in, y_in, at_in, row_by, y_by, at_by, count = outs
    first, planes, depth = where[0], where[1], where[2]

    def look(i, n):
        x = rx[i] - first
        inside = (x >= 0) & (x < planes)
        beside = (x >= -4) & (x < planes + 4) & jnp.logical_not(inside)

        @pl.when(inside)
        def _():
            row_in[n[0]] = x * depth + rz[i]
            y_in[n[0]] = ry[i]
            at_in[n[0]] = i

        @pl.when(beside)
        def _():
            row_by[n[1]] = (x + 4) * depth + rz[i]
            y_by[n[1]] = ry[i]
            at_by[n[1]] = i

        return n[0] + inside.astype(jnp.int32), n[1] + beside.astype(jnp.int32)

    count[0], count[1] = lax.fori_loop(0, rz.shape[0], look, (jnp.int32(0), jnp.int32(0)))


def list_receivers(rz, rx, ry, where):
    n = rz.shape[0]
    ints = jax.ShapeDtypeStruct((n,), jnp.int32)
    return pl.pallas_call(
        list_kernel,
        out_shape=(ints,) * 6 + (jax.ShapeDtypeStruct((2,), jnp.int32),),
        in_specs=[sspec()] * 4,
        out_specs=(sspec(),) * 7,
        compiler_params=params(),
        name="receivers",
    )(rz, rx, ry, where)


def at_receivers(rec, beside, read, into, gathered):
    rows, ys, ats = rec[3:6] if beside else rec[0:3]
    count = rec[6]
    for target in into:
        target[...] = jnp.zeros(target.shape, F32)
    for g in gathered:
        g[...] = jnp.zeros(g.shape, F32)
    lane = lax.broadcasted_iota(jnp.int32, gathered[0].shape, 1)

    def one(j, c):
        row, y, at = rows[j], ys[j], ats[j]
        read(row, gathered)
        to = at % 128
        for g, target in zip(gathered, into):
            moved = pltpu.roll(g[...], (to - y + 128) % 128, 1)
            target[at // 128] = target[at // 128] + jnp.where(lane == to, moved, 0.0)
        return c

    lax.fori_loop(0, count[1] if beside else count[0], one, 0)


def apply_own(cur, f, buf, ybuf, taps, coef, emit):
    nx, depth, ny = cur.shape[1:]
    for x in range(nx):
        u = cur[f, x]
        buf[4 + x, 8 : 8 + depth] = u
        top = u.astype(BF)
        rest = (u - top.astype(F32)).astype(BF)
        ybuf[x] = jnp.dot(
            jnp.concatenate([top, rest], axis=1), taps[...], preferred_element_type=F32
        )
    rows = 32

    def part(i, c):
        x, h = i // (depth // rows), i % (depth // rows)
        z0 = pl.multiple_of(h * rows, rows)
        at = 8 + z0

        def rd(px, dz):
            return buf[px, pl.ds(at + dz, rows), :]

        u = rd(4 + x, 0)
        y = ybuf[x, pl.ds(z0, rows), :]
        second = (3.0 * CENTRE) * u + y[:, :ny]
        gx = gz = None
        for k in range(1, 5):
            p, m = rd(4 + x + k, 0), rd(4 + x - k, 0)
            second = second + SECOND[k] * (p + m)
            g = FIRST[k] * (p - m)
            gx = g if gx is None else gx + g
            p, m = rd(4 + x, k), rd(4 + x, -k)
            second = second + SECOND[k] * (p + m)
            g = FIRST[k] * (p - m)
            gz = g if gz is None else gz + g

        def cf(which):
            return coef[which, x, pl.ds(z0, rows), :]

        value = cf(0) * second + cf(1) * gz + cf(2) * gx + cf(3) * y[:, ny:]
        emit(x, z0, rows, u, value)
        return c

    lax.fori_loop(0, nx * (depth // rows), part, 0)


def clear_edges(buf, depth):
    nx = buf.shape[0] - 8
    for x in range(4):
        buf[x] = jnp.zeros(buf.shape[1:], F32)
        buf[4 + nx + x] = jnp.zeros(buf.shape[1:], F32)
    zeros = jnp.zeros((8, buf.shape[2]), F32)
    for x in range(nx):
        buf[4 + x, 0:8] = zeros
        buf[4 + x, 8 + depth : 16 + depth] = zeros


def source_term(n, wav, src, x, z0, shape):
    z = lax.broadcasted_iota(jnp.int32, shape, 0) + z0
    y = lax.broadcasted_iota(jnp.int32, shape, 1)
    at = (z == src[0]) & (y == src[2])
    amount = jnp.where(x == src[1], wav[n], 0.0)
    return jnp.where(at, amount, 0.0)


def own_part(n, wav, src, cur, prev, coef, taps, part, acc, buf, ybuf):
    depth = cur.shape[2]
    clear_edges(buf, depth)
    for f in range(F):

        def emit(x, z0, rows, u, value, f=f):
            rs = pl.ds(z0, rows)
            new = 2.0 * u - prev[f, x, rs, :] + value
            if f == 0:
                acc[x, rs, :] = value
                new = new + source_term(n, wav, src, x, z0, u.shape)
            part[f, x, rs, :] = new

        apply_own(cur, f, buf, ybuf, taps, coef, emit)


def own_kernel(n, wav, src, cur, prev, coef, taps, part, acc, buf, ybuf):
    own_part(n, wav, src, cur, prev, coef, taps, part, acc, buf, ybuf)


def own_table_kernel(
    n, wav, src, *refs
):
    rec = refs[:7]
    cur, prev, coef, taps, perturb, part, acc, table, buf, ybuf, gathered, found = refs[7:]
    own_part(n, wav, src, cur, prev, coef, taps, part, acc, buf, ybuf)
    k, nx, depth, ny = perturb.shape

    def read(row, gs):
        x, z = row // depth, pl.ds(row % depth, 1)
        gs[0][0:1, :] = coef[0, x, z, :]
        gs[0][1:2, :] = coef[2, x, z, :]
        for j in range(k):
            gs[0][2 + j : 3 + j, :] = perturb[j, x, z, :]

    at_receivers(rec, False, read, [found], [gathered])
    left = found[...].reshape(16, 128)
    for term in range(3):
        rounded = left.astype(BF)
        table[16 * term : 16 * term + 16, :] = rounded
        left = left - rounded.astype(F32)
    table[48:64, :] = jnp.zeros((16, 128), BF)


def own_trace_kernel(n, wav, src, *refs):
    rec = refs[:7]
    (cur, prev, coef, taps, perturb, table_low, table_high) = refs[7:14]
    part, acc, traces, buf, ybuf, ga, gb, ta, tb = refs[14:]
    own_part(n, wav, src, cur, prev, coef, taps, part, acc, buf, ybuf)
    k, nx, depth, ny = perturb.shape

    def read_beside(row, gs):
        x, z = row // depth - 4, pl.ds(row % depth, 1)
        near = jnp.where(x < 0, 0, nx - 4)
        for f in range(F):
            second = first = jnp.zeros((1, ny), F32)
            for q in range(4):
                p = near + q
                d = p - x
                away = jnp.abs(d)
                c2 = c1 = jnp.float32(0.0)
                for t in range(1, 5):
                    c2 = jnp.where(away == t, jnp.float32(SECOND[t]), c2)
                    c1 = jnp.where(away == t, jnp.float32(FIRST[t]), c1)
                c1 = jnp.where(d < 0, -c1, c1)
                u = cur[f, p, z, :]
                second = second + c2 * u
                first = first + c1 * u
            gs[0][f : f + 1, :] = second
            gs[1][f : f + 1, :] = first

    at_receivers(rec, True, read_beside, [ta, tb], [ga, gb])
    both = jnp.zeros((16, 128), F32)
    for table in (table_low, table_high):
        for term in range(3):
            both = both + table[16 * term : 16 * term + 16, :].astype(F32)
    shares = []
    for h in range(2):
        const = both[8 * h : 8 * h + 8]
        reach = const[0:1] * ta[h] + const[1:2] * tb[h]
        shares.append(
            jnp.concatenate(
                [reach[1 + j : 2 + j] + const[2 + j : 3 + j] * reach[0:1] for j in range(k)], axis=0
            )
        )

    def read_own(row, gs):
        x, z = row // depth, pl.ds(row % depth, 1)
        for j in range(k):
            gs[0][j : j + 1, :] = part[1 + j, x, z, :] + perturb[j, x, z, :] * acc[x, z, :]

    at_receivers(rec, False, read_own, [ta], [ga])
    for h in range(2):
        traces[h * k : h * k + k, :] = shares[h] + ta[h, 0:k, :]


def near_planes(msg, f, first, rs):
    if first and f > 0:
        base = 5 + 4 * (f - 1)
        return [msg[base + p, rs, :].astype(F32) for p in range(4)]
    base = 5 * f
    near = msg[base, rs, :].astype(F32) + msg[base + 1, rs, :].astype(F32)
    return [near] + [msg[base + 1 + p, rs, :].astype(F32) for p in range(1, 4)]


def send_plane(msg, f, p, rs, new):
    top = new.astype(BF)
    if p == 0:
        msg[5 * f, rs, :] = top
        msg[5 * f + 1, rs, :] = (new - top.astype(F32)).astype(BF)
    else:
        msg[5 * f + 1 + p, rs, :] = top


def finish_part(n, part, acc_own, low_in, high_in, coef, perturb, acc, nxt, low, high, out):
    nx, depth, ny = part.shape[1:]
    rows = 16
    last = n == ITERS - 1
    for f in range(F):

        def piece(i, c, f=f):
            z0 = pl.multiple_of(i * rows, rows)
            rs = pl.ds(z0, rows)
            below = near_planes(low_in, f, n == 0, rs)
            above = near_planes(high_in, f, n == 0, rs)
            for x in range(nx):
                lower = x < 4
                planes, d, sign = (below, x, -1.0) if lower else (above, nx - 1 - x, 1.0)
                second = first = None
                for j in range(4 - d):
                    t = d + 1 + j
                    s, g = SECOND[t] * planes[j], (sign * FIRST[t]) * planes[j]
                    second = s if second is None else second + s
                    first = g if first is None else first + g
                reach = coef[0, x, rs, :] * second + coef[2, x, rs, :] * first
                if f == 0:
                    acc[x, rs, :] = acc_own[x, rs, :] + reach
                    if last:
                        continue
                    new = part[f, x, rs, :] + reach
                else:
                    new = part[f, x, rs, :] + reach + perturb[f - 1, x, rs, :] * acc[x, rs, :]
                if last:
                    out[f - 1, pl.ds(z0 * nx + x, rows, stride=nx), :] = new
                else:
                    nxt[f, x, rs, :] = new
                    send_plane(low if lower else high, f, d, rs, new)
            return c

        lax.fori_loop(0, depth // rows, piece, 0)


def sample_new(n, rec, nxt, traces, gathered, depth, k):
    offset = (n % 2) * k

    def read(row, gs):
        for j in range(k):
            gs[0][offset + j : offset + j + 1, :] = nxt[
                j + 1, row // depth, pl.ds(row % depth, 1), :
            ]

    at_receivers(rec, False, read, [traces], [gathered])


def gather_kernel(labels, *refs):
    rec = refs[:7]
    part, acc_own, low_in, high_in, coef, incoming = refs[7:13]
    nxt, perturb, low, high, traces, acc, gathered = refs[13:]
    k, nx, depth, ny = perturb.shape
    zb = (incoming.shape[1] - 16) // (CAP * k)
    perturb[...] = jnp.zeros(perturb.shape, F32)

    def add(s, c):
        label = labels[s]
        t, a = s // CAP, s % CAP

        @pl.when(label > 0)
        def _():
            b = label - 1
            x = b % nx
            z0 = pl.multiple_of((b // nx) * zb, zb)
            for j in range(k):
                at = pl.multiple_of((a * k + j) * zb, zb)
                perturb[j, x, pl.ds(z0, zb), :] = perturb[j, x, pl.ds(z0, zb), :] + incoming[
                    t, pl.ds(at, zb), :
                ].astype(F32)

        return c

    lax.fori_loop(0, incoming.shape[0] * CAP, add, 0)
    finish_part(0, part, acc_own, low_in, high_in, coef, perturb, acc, nxt, low, high, None)
    sample_new(0, rec, nxt, traces, gathered, depth, k)


def finish_kernel(n, *refs):
    rec = refs[:7]
    part, acc_own, low_in, high_in, coef, perturb = refs[7:13]
    rest = refs[13:]
    k, nx, depth, ny = perturb.shape
    if n == ITERS - 1:
        out, acc = rest
        finish_part(
            n, part, acc_own, low_in, high_in, coef, perturb, acc, None, None, None, out
        )
        return
    if n == 1:
        table, nxt, low, high, traces, acc, gathered = rest
        low[5 * F] = table[...]
        high[5 * F] = table[...]
    else:
        nxt, low, high, traces, acc, gathered = rest
    finish_part(n, part, acc_own, low_in, high_in, coef, perturb, acc, nxt, low, high, None)
    sample_new(n, rec, nxt, traces, gathered, depth, k)


def cost(flops, moved):
    return pl.CostEstimate(flops=flops, bytes_accessed=moved, transcendentals=0)


def exchange(low, high):
    count = lax.axis_size("tile")
    forward = [(i, i + 1) for i in range(count - 1)]
    backward = [(b, a) for a, b in forward]
    return lax.ppermute(high, "tile", forward), lax.ppermute(low, "tile", backward)


def swap(value):
    count = lax.axis_size("tile")
    return lax.ppermute(value, "tile", [(i, i ^ 1) for i in range(count)])


def two_terms(plane):
    top = plane.astype(BF)
    return [top, (plane - lax.reduce_precision(plane, 8, 7)).astype(BF)]


def local(
    background_prev,
    background_now,
    stiffness,
    drift_terms,
    born_prev,
    born_now,
    pieces,
    piece_target,
    piece_block,
    wavelet,
    source_cell,
    receiver_z,
    receiver_x,
    receiver_y,
):
    tiles = lax.axis_size("tile")
    place = lax.axis_index("tile")
    k = born_now.shape[0]
    depth, nx, ny = background_now.shape
    zb = pieces.shape[2]

    packed = pack(pieces, piece_target[:, 0], piece_block, tiles)
    incoming = lax.all_to_all(packed, "tile", 0, 0, tiled=True)
    names = incoming[:, CAP * k * zb : CAP * k * zb + CAP, 0]
    labels = names.astype(jnp.int32).reshape(tiles * CAP)

    def face(planes):
        near = two_terms(background_now[:, planes[0], :])
        rows = near + [background_now[:, p, :].astype(BF) for p in planes[1:]]
        born = jnp.stack([born_now[:, :, p, :] for p in planes], axis=1)
        return jnp.concatenate([jnp.stack(rows), born.reshape(k * 4, depth, ny)])

    low_in, high_in = exchange(face((0, 1, 2, 3)), face((7, 6, 5, 4)))

    where = jnp.stack([place * nx, jnp.int32(nx), jnp.int32(depth)]).astype(jnp.int32)
    rec = list_receivers(receiver_z, receiver_x, receiver_y, where)
    src = jnp.stack([source_cell[0], source_cell[1] - place * nx, source_cell[2]])

    def planes_first(background, born):
        return jnp.concatenate(
            [
                background.transpose(1, 0, 2)[None],
                born.astype(F32).transpose(0, 2, 1, 3),
            ]
        )

    cur = planes_first(background_now, born_now)
    prev = planes_first(background_prev, born_prev)
    coef = jnp.concatenate(
        [
            (stiffness.astype(F32) * (1.0 / 5040.0))[None],
            drift_terms.astype(F32) * (1.0 / 840.0),
        ]
    ).transpose(0, 2, 1, 3)
    taps = jnp.asarray(tap_matrix(ny)).astype(BF)

    state = jax.ShapeDtypeStruct((F, nx, depth, ny), F32)
    field = jax.ShapeDtypeStruct((nx, depth, ny), F32)
    faces = jax.ShapeDtypeStruct((5 * F, depth, ny), BF)
    wider = jax.ShapeDtypeStruct((5 * F + 1, depth, ny), BF)
    traced = jax.ShapeDtypeStruct((2, 8, 128), F32)
    small = VM((8, 128), F32)
    pair = VM((2, 8, 128), F32)
    work = [VM((nx + 8, depth + 16, ny), F32), VM((nx, depth, 2 * ny), F32)]
    cells = F * nx * depth * ny

    def call(kernel, name, out_shape, scratch, scalars, arrays, flops):
        return pl.pallas_call(
            kernel,
            out_shape=out_shape,
            in_specs=[sspec()] * len(scalars) + [vspec()] * len(arrays),
            out_specs=tuple(vspec() for _ in out_shape),
            scratch_shapes=scratch,
            compiler_params=params(),
            cost_estimate=cost(flops * cells, 16 * cells),
            name=name,
        )(*scalars, *arrays)

    records = []
    perturb = table = tables = None
    for n in range(ITERS):
        name = "own%d" % (n + 1)
        start = (wavelet, src)
        arrays = (cur, prev, coef, taps)
        if n == 1:
            part, acc, table = call(
                functools.partial(own_table_kernel, n),
                name,
                (state, field, jax.ShapeDtypeStruct((64, 128), BF)),
                work + [small, pair],
                start + tuple(rec),
                arrays + (perturb,),
                80,
            )
        elif n == ITERS - 1:
            part, acc, mine = call(
                functools.partial(own_trace_kernel, n),
                name,
                (state, field, jax.ShapeDtypeStruct((8, 128), F32)),
                work + [small, small, pair, pair],
                start + tuple(rec),
                arrays + (perturb,) + tables,
                80,
            )
        else:
            part, acc = call(
                functools.partial(own_kernel, n), name, (state, field), work, start, arrays, 80
            )
        arrays = (part, acc, low_in, high_in, coef)
        name = "finish%d" % (n + 1)
        keep = VM((nx, depth, ny), F32)
        if n == 0:
            nxt, perturb, low, high, traces = call(
                gather_kernel,
                name,
                (state, jax.ShapeDtypeStruct((k, nx, depth, ny), F32), faces, faces, traced),
                [keep, small],
                (labels,) + tuple(rec),
                arrays + (incoming,),
                20,
            )
        elif n == ITERS - 1:
            (born,) = call(
                functools.partial(finish_kernel, n),
                name,
                (jax.ShapeDtypeStruct((k, depth * nx, ny), F32),),
                [keep],
                tuple(rec),
                arrays + (perturb,),
                20,
            )
            break
        else:
            face_type = wider if n == 1 else faces
            nxt, low, high, traces = call(
                functools.partial(finish_kernel, n),
                name,
                (state, face_type, face_type, traced),
                [keep, small],
                tuple(rec),
                arrays + (perturb,) + ((table,) if n == 1 else ()),
                20,
            )
        records.append(traces)
        low_in, high_in = exchange(low, high)
        if n == 1:
            tables = (low_in[5 * F], high_in[5 * F])
        prev, cur = cur, nxt

    early = jnp.stack([records[0] + records[1], records[2]])
    early = early + swap(early)
    odd = place % 2
    half = jnp.where(odd == 0, early[0], early[1])
    message = jnp.concatenate([half, mine[None]])
    message, low_in, high_in = lax.optimization_barrier((message, low_in, high_in))
    groups = [list(range(c, tiles, 2)) for c in range(2)]
    copies = lax.all_to_all(
        jnp.broadcast_to(message[None], (tiles // 2,) + message.shape),
        "tile",
        0,
        0,
        axis_index_groups=groups,
        tiled=True,
    )
    total = jnp.sum(copies, axis=0)
    other = swap(total)
    ours, theirs = total[:2], other[:2]
    first_two = jnp.where(odd == 0, ours, theirs).reshape(2, 2, k, 128)
    third = jnp.where(odd == 0, theirs, ours)[:, :k]
    fourth = (total[2] + other[2]).reshape(2, k, 128)
    steps = jnp.concatenate([first_two, third[:, None], fourth[:, None]], axis=1)
    traces = steps.transpose(2, 1, 0, 3).reshape(k, ITERS, 256)
    return born.reshape(k, depth, nx, ny), traces


def solution(mesh):
    placed = (
        P(None, "tile", None),
        P(None, "tile", None),
        P(None, "tile", None),
        P(None, None, "tile", None),
        P("dir", None, "tile", None),
        P("dir", None, "tile", None),
        P("dir", "tile", None, None),
        P("tile", None),
        P("tile"),
        P(),
        P(),
        P(),
        P(),
        P(),
    )
    return jax.shard_map(
        local,
        mesh=mesh,
        in_specs=placed,
        out_specs=(P("dir", None, "tile", None), P("dir", None, None)),
        check_vma=False,
    )
```

time: 748 us -> 283 us (0.38)
  the two profiles are of different devices: /device:TPU:1 before, /device:TPU:89 now
where the time goes in v1:
time: 283 us; the launch traced here: 282 us
  waiting for transfers between devices  97.4 us (34%)
  starting transfers between devices  49.7 us (18%)
  Pallas kernels  48.8 us (17%)
  blocking collectives  40.6 us (14%)
  local copies, waits for them, and re-layouts  38.6 us (14%)
  other arithmetic  4.77 us (2%)
    all_to_all x1, waiting for transfers between devices, local(): incoming = lax.all_to_all(packed, 'tile', 0, 0, tiled=True)  71.8 us
    all_to_all x1, blocking collectives, local(): lax.all_to_all(jnp.broadcast_to(message[None], (tiles // 2,) + message.sh...  40.6 us
    pallas_call x8, Pallas kernels, call(): pl.pallas_call(kernel, out_shape=out_shape, in_specs=[sspec()] * len(scal...  39 us
    unnamed x127, local copies, waits for them, and re-layouts  32.7 us
    ppermute x4, waiting for transfers between devices, exchange(): lax.ppermute(low, 'tile', backward)  25.6 us
    all_to_all x1, starting transfers between devices, local(): incoming = lax.all_to_all(packed, 'tile', 0, 0, tiled=True)  16.8 us
    ppermute x4, starting transfers between devices, exchange(): lax.ppermute(low, 'tile', backward)  15 us
    ppermute x4, starting transfers between devices, exchange(): lax.ppermute(high, 'tile', forward)  14.1 us
  transfers between devices with their start and end apart: 11, of which 4 were waited for; matrix products, arithmetic and copies ran while one was open for 5% of the time, Pallas kernels for 13%

profile of v1, /device:TPU:89, one launch (start us, length us, event | category | flops | bytes accessed | tf_op | source)
XLA Modules:
  0.0 281.9 jit_solution(13589645054765330293)
XLA Ops:
  0.6 1.2 copy-done.7
  1.9 0.7 copy-done.48
  2.5 0.7 copy-done.49
  3.2 3.0 %pack.1 = bf16[32,272,128]{2,1,0:T(8,128)(2,1)} custom-call(s32[32]{0:T(128)S(1)} %bitcast.107, s32[32]{0:T(128)S(1)} %copy-done.49, bf16[4,32,32,128]{3,2,1,0:T(8,128)(2,1)S(1)} %copy-done.7), custom_call_target="tpu_custom_call" | custom-call | tf_op jit(solution)/shard_map/pack/pallas_call | solution.py:85
  6.2 16.8 %all-to-all-start = ((bf16[32,272,128]{2,1,0:T(8,128)(2,1)}), bf16[32,272,128]{2,1,0:T(8,128)(2,1)}, u32[]{:S(2)}, u32[]{:S(2)}) async-start(bf16[32,272,128]{2,1,0:T(8,128)(2,1)} %pack.1), calls=%async_computation | async-start | bytes 4456448 | tf_op jit(solution)/shard_map/all_to_all | solution.py:478
  23.1 0.9 copy-done.50
  24.0 1.0 fusion.7
  28.8 0.7 constant_dynamic-update-slice_fusion
  29.5 7.6 %collective-permute-start = (bf16[21,64,128]{2,1,0:T(8,128)(2,1)}, bf16[21,64,128]{2,1,0:T(8,128)(2,1)S(1)}, u32[]{:S(2)}, u32[]{:S(2)}) collective-permute-start(bf16[21,64,128]{2,1,0:T(8,128)(2,1)} %constant_dynamic-update-slice_fusion), channel_id=1, source_target_pairs={{0,16},{16,32},{32,48},{48,64},{64,80},{80,96},{96,112},{112,128},... | collective-permute-start | bytes 1032200 | tf_op jit(solution)/shard_map/ppermute | solution.py:442
  37.3 0.7 constant_dynamic-update-slice_fusion.6
  38.0 1.9 collective-permute-start.1
  39.9 0.7 copy.104
  40.7 0.6 fusion.9
  42.0 6.8 %receivers.1 = (s32[256]{0:T(256)S(1)}, s32[256]{0:T(256)S(1)}, s32[256]{0:T(256)S(1)}, s32[256]{0:T(256)S(1)}, s32[256]{0:T(256)S(1)}, /*index=5*/s32[256]{0:T(256)S(1)}, s32[2]{0:T(128)S(1)}) custom-call(s32[256]{0:T(256)S(1)} %copy-done.45, s32[256]{0:T(256)S(1)} %copy-done.46, s32[256]{0:T(256)S(1)} %copy-done.47, s32[3]{0:T(128)S(1)} %pad_add_fusion.where), custom_call_target="tpu_custom_call" | custom-call | tf_op jit(solution)/shard_map/receivers/pallas_call | solution.py:125
  50.2 0.8 copy-done.53
  51.3 1.2 pad_add_fusion.1.src
  53.4 5.9 %own1.1 = (f32[5,8,64,128]{3,2,1,0:T(8,128)S(1)}, f32[8,64,128]{2,1,0:T(8,128)S(1)}) custom-call(f32[4]{0:T(128)S(1)} %copy-done.36, s32[3]{0:T(128)S(1)} %pad_add_fusion.1.src, f32[5,8,64,128]{3,2,1,0:T(8,128)S(1)} %pad_maximum_fusion.cur.refs_8_, f32[5,8,64,128]{3,2,1,0:T(8,128)S(1)} %pad_maximum_fusion.1.prev, ...), custom_call_target="tpu_custom_call" | custom-call | flops 26214400 | bytes 5242880 | tf_op jit(solution)/shard_map/own1/pallas_call | solution.py:523
  59.4 1.1 copy-done.5
  60.4 0.7 copy-done.18
  61.1 71.8 %all-to-all-done.refs_12_ = bf16[32,272,128]{2,1,0:T(8,128)(2,1)} async-done(((bf16[32,272,128]{2,1,0:T(8,128)(2,1)}), bf16[32,272,128]{2,1,0:T(8,128)(2,1)}, u32[]{:S(2)}, u32[]{:S(2)}) %all-to-all-start) | async-done | bytes 2228256 | tf_op jit(solution)/shard_map/all_to_all | solution.py:478
  133.0 1.5 convert_reduce_fusion
  135.0 0.7 copy-done.12
  135.8 0.7 copy-done.14
  136.5 1.3 copy-done.6
  137.8 1.0 copy-done.13
  138.8 1.0 copy-done.15
  139.8 0.9 copy-done.19
  140.7 0.7 copy-done.21
  141.4 0.7 copy-done.25
  142.7 0.7 copy-done.44
  143.3 4.6 %finish1.1 = (f32[5,8,64,128]{3,2,1,0:T(8,128)S(1)}, f32[4,8,64,128]{3,2,1,0:T(8,128)S(1)}, bf16[25,64,128]{2,1,0:T(8,128)(2,1)S(1)}, bf16[25,64,128]{2,1,0:T(8,128)(2,1)S(1)}, f32[2,8,128]{2,1,0:T(8,128)S(1)}) custom-call(s32[64]{0:T(128)S(1)} %copy-done.44, s32[256]{0:T(256)S(1)} %get-tuple-element.33.refs_0_, s32[256]{0:T(256)S(1)} %get-tuple-element.34.refs_1_, ...), custom_call_target="tpu_custom_call" | custom-call | flops 6553600 | bytes 5242880 | tf_op jit(solution)/shard_map/finish1/pallas_call | solution.py:523
  148.5 1.9 collective-permute-start.2
  150.5 8.1 %collective-permute-start.3 = (bf16[25,64,128]{2,1,0:T(8,128)(2,1)S(1)}, bf16[25,64,128]{2,1,0:T(8,128)(2,1)S(1)}, u32[]{:S(2)}, u32[]{:S(2)}) collective-permute-start(bf16[25,64,128]{2,1,0:T(8,128)(2,1)S(1)} %get-tuple-element.47), channel_id=1, source_target_pairs={{16,0},{32,16},{48,32},{64,48},{80,64},{96,80},{112,96},{128,112},... | collective-permute-start | bytes 1228808 | tf_op jit(solution)/shard_map/ppermute | solution.py:442
  158.5 6.7 %own2.1 = (f32[5,8,64,128]{3,2,1,0:T(8,128)S(1)}, f32[8,64,128]{2,1,0:T(8,128)S(1)}, bf16[64,128]{1,0:T(8,128)(2,1)S(1)}) custom-call(f32[4]{0:T(128)S(1)} %copy-done.37, s32[3]{0:T(128)S(1)} %copy-done.33, s32[256]{0:T(256)S(1)} %get-tuple-element.33.refs_0_, s32[256]{0:T(256)S(1)} %get-tuple-element.34.refs_1_, s32[256]{0:T(256)S(1)} %get-tuple-element.35.refs_2_, ...), custom_call_target="tpu_custom_call" | custom-call | flops 26214400 | bytes 5242880 | tf_op jit(solution)/shard_map/own2/pallas_call | solution.py:523
  165.3 4.6 %collective-permute-done.3.refs_10_ = bf16[25,64,128]{2,1,0:T(8,128)(2,1)S(1)} collective-permute-done((bf16[25,64,128]{2,1,0:T(8,128)(2,1)S(1)}, bf16[25,64,128]{2,1,0:T(8,128)(2,1)S(1)}, u32[]{:S(2)}, u32[]{:S(2)}) %collective-permute-start.3) | collective-permute-done | bytes 409632 | tf_op jit(solution)/shard_map/ppermute | solution.py:442
  169.9 3.1 %finish2.1 = (f32[5,8,64,128]{3,2,1,0:T(8,128)S(1)}, bf16[26,64,128]{2,1,0:T(8,128)(2,1)}, bf16[26,64,128]{2,1,0:T(8,128)(2,1)}, f32[2,8,128]{2,1,0:T(8,128)S(1)}) custom-call(s32[256]{0:T(256)S(1)} %get-tuple-element.33.refs_0_, s32[256]{0:T(256)S(1)} %get-tuple-element.34.refs_1_, s32[256]{0:T(256)S(1)} %get-tuple-element.35.refs_2_, ...), custom_call_target="tpu_custom_call" | custom-call | flops 6553600 | bytes 5242880 | tf_op jit(solution)/shard_map/finish2/pallas_call | solution.py:523
  173.6 1.9 collective-permute-start.4
  175.5 3.2 %collective-permute-start.5 = (bf16[26,64,128]{2,1,0:T(8,128)(2,1)}, bf16[26,64,128]{2,1,0:T(8,128)(2,1)}, u32[]{:S(2)}, u32[]{:S(2)}) collective-permute-start(bf16[26,64,128]{2,1,0:T(8,128)(2,1)} %get-tuple-element.53), channel_id=1, source_target_pairs={{16,0},{32,16},{48,32},{64,48},{80,64},{96,80},{112,96},{128,112},... | collective-permute-start | bytes 1277960 | tf_op jit(solution)/shard_map/ppermute | solution.py:442
  178.7 1.3 copy-done.1
  180.0 0.6 copy-done.34
  180.7 0.7 copy-done.38
  181.3 5.9 %own3.1 = (f32[5,8,64,128]{3,2,1,0:T(8,128)S(1)}, f32[8,64,128]{2,1,0:T(8,128)S(1)}) custom-call(f32[4]{0:T(128)S(1)} %copy-done.38, s32[3]{0:T(128)S(1)} %copy-done.34, f32[5,8,64,128]{3,2,1,0:T(8,128)S(1)} %get-tuple-element.49.cur.refs_8_, f32[5,8,64,128]{3,2,1,0:T(8,128)S(1)} %copy-done.1, ...), custom_call_target="tpu_custom_call" | custom-call | flops 26214400 | bytes 5242880 | tf_op jit(solution)/shard_map/own3/pallas_call | solution.py:523
  187.3 20.2 %collective-permute-done.5.refs_10_ = bf16[26,64,128]{2,1,0:T(8,128)(2,1)} collective-permute-done((bf16[26,64,128]{2,1,0:T(8,128)(2,1)}, bf16[26,64,128]{2,1,0:T(8,128)(2,1)}, u32[]{:S(2)}, u32[]{:S(2)}) %collective-permute-start.5) | collective-permute-done | bytes 426016 | tf_op jit(solution)/shard_map/ppermute | solution.py:442
  207.5 2.7 finish3.1
  210.3 1.9 collective-permute-start.8
  212.2 2.7 collective-permute-start.6
  214.9 1.9 collective-permute-start.7
  216.8 0.7 slice_bitcast_fusion.3.refs_12_
  217.6 0.7 slice_bitcast_fusion.2.refs_13_
  218.3 7.4 %own4.1 = (f32[5,8,64,128]{3,2,1,0:T(8,128)S(1)}, f32[8,64,128]{2,1,0:T(8,128)S(1)}, f32[8,128]{1,0:T(8,128)S(1)}) custom-call(f32[4]{0:T(128)S(1)} %copy-done.39, s32[3]{0:T(128)S(1)} %copy-done.35, s32[256]{0:T(256)S(1)} %get-tuple-element.33.refs_0_, s32[256]{0:T(256)S(1)} %get-tuple-element.34.refs_1_, s32[256]{0:T(256)S(1)} %get-tuple-element.35.refs_2_, ...), custom_call_target="tpu_custom_call" | custom-call | flops 26214400 | bytes 5242880 | tf_op jit(solution)/shard_map/own4/pallas_call | solution.py:523
  225.7 1.1 copy-done.3
  226.8 0.7 copy-done.16
  227.6 0.7 copy-done.8
  228.3 0.8 collective-permute-done.7.refs_10_
  229.1 0.8 copy-done.10
  229.9 40.6 %all_to_all.10 = f32[16,3,8,128]{3,2,1,0:T(8,128)S(1)} all-to-all(f32[16,3,8,128]{3,2,1,0:T(8,128)S(1)} %broadcast_in_dim.25), channel_id=1, replica_groups={{0,32,64,96,128,160,192,224,256,288,320,352,384,416,448,480},{16,48,80,..., dimensions={0} | all-to-all | bytes 393216 | tf_op jit(solution)/shard_map/all_to_all | solution.py:612
  270.6 1.9 collective-permute-start.9
  272.5 1.3 copy-done.4
  273.8 1.0 copy-done.9
  274.8 1.0 copy-done.11
  275.8 0.9 copy-done.17
  276.8 0.7 copy-done.23
  277.4 0.7 copy-done.27
  278.7 2.5 finish4.1
  (136 shorter events, 10.3 us)
Async XLA Ops:
  0.6 1.2 copy-start.7
  1.9 0.7 copy-start.48
  2.5 0.7 copy-start.49
  6.2 16.8 %copy-start.54 = (f32[64,8,128]{2,1,0:T(8,128)S(1)}, f32[64,8,128]{2,1,0:T(8,128)}, u32[]{:S(2)}) copy-start(f32[64,8,128]{2,1,0:T(8,128)} %param.16) | copy-start | bytes 786436
  6.2 126.8 %all-to-all-start = ((bf16[32,272,128]{2,1,0:T(8,128)(2,1)}), bf16[32,272,128]{2,1,0:T(8,128)(2,1)}, u32[]{:S(2)}, u32[]{:S(2)}) async-start(bf16[32,272,128]{2,1,0:T(8,128)(2,1)} %pack.1), calls=%async_computation | async-start | bytes 4456448 | tf_op jit(solution)/shard_map/all_to_all | solution.py:478
  23.0 1.0 copy-start.50
  24.0 2.3 copy-start.51
  29.5 10.4 %copy-start.57 = (f32[64,8,128]{2,1,0:T(8,128)S(1)}, f32[64,8,128]{2,1,0:T(8,128)}, u32[]{:S(2)}) copy-start(f32[64,8,128]{2,1,0:T(8,128)} %param.15) | copy-start | bytes 786436
  29.5 105.5 %collective-permute-start = (bf16[21,64,128]{2,1,0:T(8,128)(2,1)}, bf16[21,64,128]{2,1,0:T(8,128)(2,1)S(1)}, u32[]{:S(2)}, u32[]{:S(2)}) collective-permute-start(bf16[21,64,128]{2,1,0:T(8,128)(2,1)} %constant_dynamic-update-slice_fusion), channel_id=1, source_target_pairs={{0,16},{16,32},{32,48},{48,64},{64,80},{80,96},{96,112},{112,128},... | collective-permute-start | bytes 1032200 | tf_op jit(solution)/shard_map/ppermute | solution.py:442
  37.1 3.6 %copy-start.59 = (s32[3]{0:T(128)S(1)}, s32[3]{0:T(128)}, u32[]{:S(2)}) copy-start(s32[3]{0:T(128)} %param.25) | copy-start | bytes 40
  37.1 4.9 %copy-start.45 = (s32[256]{0:T(256)S(1)}, s32[256]{0:T(256)}, u32[]{:S(2)}) copy-start(s32[256]{0:T(256)} %rz.1) | copy-start | bytes 3076
  37.1 4.9 %copy-start.46 = (s32[256]{0:T(256)S(1)}, s32[256]{0:T(256)}, u32[]{:S(2)}) copy-start(s32[256]{0:T(256)} %rx.1) | copy-start | bytes 3076
  37.1 4.9 %copy-start.47 = (s32[256]{0:T(256)S(1)}, s32[256]{0:T(256)}, u32[]{:S(2)}) copy-start(s32[256]{0:T(256)} %ry.1) | copy-start | bytes 3076
  37.2 11.7 %copy-start.58 = (bf16[64,8,128]{2,1,0:T(8,128)(2,1)S(1)}, bf16[64,8,128]{2,1,0:T(8,128)(2,1)}, u32[]{:S(2)}) copy-start(bf16[64,8,128]{2,1,0:T(8,128)(2,1)} %param.17) | copy-start | bytes 393220
  37.2 11.7 %copy-start.56 = (bf16[3,64,8,128]{3,2,1,0:T(8,128)(2,1)S(1)}, bf16[3,64,8,128]{3,2,1,0:T(8,128)(2,1)}, u32[]{:S(2)}) copy-start(bf16[3,64,8,128]{3,2,1,0:T(8,128)(2,1)} %param.18) | copy-start | bytes 1179652
  38.0 97.8 %collective-permute-start.1 = (bf16[21,64,128]{2,1,0:T(8,128)(2,1)}, bf16[21,64,128]{2,1,0:T(8,128)(2,1)S(1)}, u32[]{:S(2)}, u32[]{:S(2)}) collective-permute-start(bf16[21,64,128]{2,1,0:T(8,128)(2,1)} %constant_dynamic-update-slice_fusion.6), channel_id=1, source_target_pairs={{16,0},{32,16},{48,32},{64,48},{80,64},{96,80},{112,96},{128,112},... | collective-permute-start | bytes 1032200 | tf_op jit(solution)/shard_map/ppermute | solution.py:442
  49.0 1.0 copy-start.55
  50.1 0.9 copy-start.53
  51.1 1.4 copy-start.52
  52.5 0.9 copy-start.2
  52.5 0.9 copy-start.36
  59.4 1.1 copy-start.5
  60.4 0.7 copy-start.18
  135.0 0.7 copy-start.12
  135.8 0.7 copy-start.14
  136.5 1.3 copy-start.6
  137.8 1.0 copy-start.13
  138.8 1.0 copy-start.15
  139.8 0.9 copy-start.19
  140.7 0.7 copy-start.21
  141.4 0.7 copy-start.25
  142.1 0.6 copy-start.29
  142.7 0.7 copy-start.44
  143.3 15.2 %copy-start.33 = (s32[3]{0:T(128)S(1)}, s32[3]{0:T(128)}, u32[]{:S(2)}) copy-start(s32[3]{0:T(128)} %copy-done.32) | copy-start | bytes 40
  143.3 15.2 %copy-start.37 = (f32[4]{0:T(128)S(1)}, f32[4]{0:T(128)}, u32[]{:S(2)}) copy-start(f32[4]{0:T(128)} %wav.7) | copy-start | bytes 52
  148.5 16.7 %copy-start = (f32[5,8,64,128]{3,2,1,0:T(8,128)}, f32[5,8,64,128]{3,2,1,0:T(8,128)S(1)}, u32[]{:S(2)}) copy-start(f32[5,8,64,128]{3,2,1,0:T(8,128)S(1)} %get-tuple-element.42.refs_7_.prev) | copy-start | bytes 3932164
  148.5 16.8 %collective-permute-start.2 = (bf16[25,64,128]{2,1,0:T(8,128)(2,1)S(1)}, bf16[25,64,128]{2,1,0:T(8,128)(2,1)S(1)}, u32[]{:S(2)}, u32[]{:S(2)}) collective-permute-start(bf16[25,64,128]{2,1,0:T(8,128)(2,1)S(1)} %get-tuple-element.46), channel_id=1, source_target_pairs={{0,16},{16,32},{32,48},{48,64},{64,80},{80,96},{96,112},{112,128},... | collective-permute-start | bytes 1228808 | tf_op jit(solution)/shard_map/ppermute | solution.py:442
  150.5 19.4 %collective-permute-start.3 = (bf16[25,64,128]{2,1,0:T(8,128)(2,1)S(1)}, bf16[25,64,128]{2,1,0:T(8,128)(2,1)S(1)}, u32[]{:S(2)}, u32[]{:S(2)}) collective-permute-start(bf16[25,64,128]{2,1,0:T(8,128)(2,1)S(1)} %get-tuple-element.47), channel_id=1, source_target_pairs={{16,0},{32,16},{48,32},{64,48},{80,64},{96,80},{112,96},{128,112},... | collective-permute-start | bytes 1228808 | tf_op jit(solution)/shard_map/ppermute | solution.py:442
  173.6 13.7 %collective-permute-start.4 = (bf16[26,64,128]{2,1,0:T(8,128)(2,1)}, bf16[26,64,128]{2,1,0:T(8,128)(2,1)}, u32[]{:S(2)}, u32[]{:S(2)}) collective-permute-start(bf16[26,64,128]{2,1,0:T(8,128)(2,1)} %get-tuple-element.52), channel_id=1, source_target_pairs={{0,16},{16,32},{32,48},{48,64},{64,80},{80,96},{96,112},{112,128},... | collective-permute-start | bytes 1277960 | tf_op jit(solution)/shard_map/ppermute | solution.py:442
  175.5 31.9 %collective-permute-start.5 = (bf16[26,64,128]{2,1,0:T(8,128)(2,1)}, bf16[26,64,128]{2,1,0:T(8,128)(2,1)}, u32[]{:S(2)}, u32[]{:S(2)}) collective-permute-start(bf16[26,64,128]{2,1,0:T(8,128)(2,1)} %get-tuple-element.53), channel_id=1, source_target_pairs={{16,0},{32,16},{48,32},{64,48},{80,64},{96,80},{112,96},{128,112},... | collective-permute-start | bytes 1277960 | tf_op jit(solution)/shard_map/ppermute | solution.py:442
  178.7 1.3 copy-start.1
  180.0 0.6 copy-start.34
  180.7 0.7 copy-start.38
  181.3 6.0 %copy-start.41 = (f32[2,8,128]{2,1,0:T(8,128)S(1)}, f32[2,8,128]{2,1,0:T(8,128)}, u32[]{:S(2)}) copy-start(f32[2,8,128]{2,1,0:T(8,128)} %copy-done.40) | copy-start | bytes 24580
  181.3 6.0 %copy-start.43 = (f32[2,8,128]{2,1,0:T(8,128)S(1)}, f32[2,8,128]{2,1,0:T(8,128)}, u32[]{:S(2)}) copy-start(f32[2,8,128]{2,1,0:T(8,128)} %copy-done.42) | copy-start | bytes 24580
  181.3 26.2 %copy-start.22 = (s32[256]{0:T(256)S(1)}, s32[256]{0:T(256)}, u32[]{:S(2)}) copy-start(s32[256]{0:T(256)} %copy-done.20) | copy-start | bytes 3076
  181.3 26.2 %copy-start.26 = (s32[256]{0:T(256)S(1)}, s32[256]{0:T(256)}, u32[]{:S(2)}) copy-start(s32[256]{0:T(256)} %copy-done.24) | copy-start | bytes 3076
  181.3 26.2 %copy-start.30 = (s32[2]{0:T(128)S(1)}, s32[2]{0:T(128)}, u32[]{:S(2)}) copy-start(s32[2]{0:T(128)} %copy-done.28) | copy-start | bytes 28
  207.5 10.8 %copy-start.35 = (s32[3]{0:T(128)S(1)}, s32[3]{0:T(128)}, u32[]{:S(2)}) copy-start(s32[3]{0:T(128)} %copy-done.32) | copy-start | bytes 40
  207.5 10.8 %copy-start.39 = (f32[4]{0:T(128)S(1)}, f32[4]{0:T(128)}, u32[]{:S(2)}) copy-start(f32[4]{0:T(128)} %wav.7) | copy-start | bytes 52
  210.3 17.3 %collective-permute-start.8 = (f32[2,2,8,128]{3,2,1,0:T(8,128)S(1)}, f32[2,2,8,128]{3,2,1,0:T(8,128)S(1)}, u32[]{:S(2)}, u32[]{:S(2)}) collective-permute-start(f32[2,2,8,128]{3,2,1,0:T(8,128)S(1)} %pad_maximum_fusion.4), channel_id=1, source_target_pairs={{0,16},{16,0},{32,48},{48,32},{64,80},{80,64},{96,112},{112,96},{1... | collective-permute-start | bytes 49160 | tf_op jit(solution)/shard_map/ppermute | solution.py:447
  212.2 15.4 %collective-permute-start.6 = (bf16[25,64,128]{2,1,0:T(8,128)(2,1)S(1)}, bf16[25,64,128]{2,1,0:T(8,128)(2,1)S(1)}, u32[]{:S(2)}, u32[]{:S(2)}) collective-permute-start(bf16[25,64,128]{2,1,0:T(8,128)(2,1)S(1)} %get-tuple-element.57), channel_id=1, source_target_pairs={{0,16},{16,32},{32,48},{48,64},{64,80},{80,96},{96,112},{112,128},... | collective-permute-start | bytes 1228808 | tf_op jit(solution)/shard_map/ppermute | solution.py:442
  214.9 14.2 %collective-permute-start.7 = (bf16[25,64,128]{2,1,0:T(8,128)(2,1)S(1)}, bf16[25,64,128]{2,1,0:T(8,128)(2,1)S(1)}, u32[]{:S(2)}, u32[]{:S(2)}) collective-permute-start(bf16[25,64,128]{2,1,0:T(8,128)(2,1)S(1)} %get-tuple-element.58), channel_id=1, source_target_pairs={{16,0},{32,16},{48,32},{64,48},{80,64},{96,80},{112,96},{128,112},... | collective-permute-start | bytes 1228808 | tf_op jit(solution)/shard_map/ppermute | solution.py:442
  225.7 1.1 copy-start.3
  226.8 0.7 copy-start.16
  227.6 0.8 copy-start.8
  229.1 0.8 copy-start.10
  270.6 10.6 %collective-permute-start.9 = (f32[3,8,128]{2,1,0:T(8,128)S(1)}, f32[3,8,128]{2,1,0:T(8,128)S(1)}, u32[]{:S(2)}, u32[]{:S(2)}) collective-permute-start(f32[3,8,128]{2,1,0:T(8,128)S(1)} %reduce_sum.9), channel_id=1, source_target_pairs={{0,16},{16,0},{32,48},{48,32},{64,80},{80,64},{96,112},{112,96},{1... | collective-permute-start | bytes 36872 | tf_op jit(solution)/shard_map/ppermute | solution.py:447
  272.5 1.3 copy-start.4
  273.8 1.0 copy-start.9
  274.8 1.0 copy-start.11
  275.8 0.9 copy-start.17
  276.8 0.7 copy-start.23
  277.4 0.7 copy-start.27
  (7 other events, 4.1 us)

commit v2 on v1

--- a/solution.py
+++ b/solution.py
@@ -30,8 +30,8 @@
     return pl.BlockSpec(memory_space=SM)
 
 
-def params():
-    return pltpu.CompilerParams(vmem_limit_bytes=16 * 1024 * 1024)
+def params(mib=16):
+    return pltpu.CompilerParams(vmem_limit_bytes=mib * 1024 * 1024)
 
 
 def tap_matrix(ny):
@@ -68,12 +68,12 @@
         return c
 
     lax.fori_loop(0, rows, place, 0)
-    row_at = lax.broadcasted_iota(jnp.int32, (16, ny), 0)
+    lane_at = lax.broadcasted_iota(jnp.int32, (16, ny), 1)
 
     def name(t, c):
         held = jnp.zeros((16, ny), jnp.int32)
         for a in range(CAP):
-            held = jnp.where(row_at == a, label[t * CAP + a], held)
+            held = jnp.where(lane_at == a, label[t * CAP + a], held)
         packed[t, CAP * directions * zb :, :] = held.astype(F32).astype(BF)
         return c
 
@@ -93,8 +93,7 @@
     )(target, block, pieces)
 
 
-def list_kernel(rz, rx, ry, where, *outs):
-    row_in, y_in, at_in, row_by, y_by, at_by, count = outs
+def list_kernel(rz, rx, ry, where, rec):
     first, planes, depth = where[0], where[1], where[2]
 
     def look(i, n):
@@ -104,37 +103,36 @@
 
         @pl.when(inside)
         def _():
-            row_in[n[0]] = x * depth + rz[i]
-            y_in[n[0]] = ry[i]
-            at_in[n[0]] = i
+            rec[0, n[0]] = x * depth + rz[i]
+            rec[1, n[0]] = ry[i]
+            rec[2, n[0]] = i
 
         @pl.when(beside)
         def _():
-            row_by[n[1]] = (x + 4) * depth + rz[i]
-            y_by[n[1]] = ry[i]
-            at_by[n[1]] = i
+            rec[3, n[1]] = (x + 4) * depth + rz[i]
+            rec[4, n[1]] = ry[i]
+            rec[5, n[1]] = i
 
         return n[0] + inside.astype(jnp.int32), n[1] + beside.astype(jnp.int32)
 
-    count[0], count[1] = lax.fori_loop(0, rz.shape[0], look, (jnp.int32(0), jnp.int32(0)))
+    inner, outer = lax.fori_loop(0, rz.shape[0], look, (jnp.int32(0), jnp.int32(0)))
+    rec[6, 0] = inner
+    rec[6, 1] = outer
 
 
 def list_receivers(rz, rx, ry, where):
     n = rz.shape[0]
-    ints = jax.ShapeDtypeStruct((n,), jnp.int32)
     return pl.pallas_call(
         list_kernel,
-        out_shape=(ints,) * 6 + (jax.ShapeDtypeStruct((2,), jnp.int32),),
+        out_shape=jax.ShapeDtypeStruct((8, n), jnp.int32),
         in_specs=[sspec()] * 4,
-        out_specs=(sspec(),) * 7,
+        out_specs=sspec(),
         compiler_params=params(),
         name="receivers",
     )(rz, rx, ry, where)
 
 
-def at_receivers(rec, beside, read, into, gathered):
-    rows, ys, ats = rec[3:6] if beside else rec[0:3]
-    count = rec[6]
+def at_receivers(rec, read, into, gathered):
     for target in into:
         target[...] = jnp.zeros(target.shape, F32)
     for g in gathered:
@@ -142,7 +140,7 @@
     lane = lax.broadcasted_iota(jnp.int32, gathered[0].shape, 1)
 
     def one(j, c):
-        row, y, at = rows[j], ys[j], ats[j]
+        row, y, at = rec[0, j], rec[1, j], rec[2, j]
         read(row, gathered)
         to = at % 128
         for g, target in zip(gathered, into):
@@ -150,7 +148,7 @@
             target[at // 128] = target[at // 128] + jnp.where(lane == to, moved, 0.0)
         return c
 
-    lax.fori_loop(0, count[1] if beside else count[0], one, 0)
+    lax.fori_loop(0, rec[6, 0], one, 0)
 
 
 def apply_own(cur, f, buf, ybuf, taps, coef, emit):
@@ -239,8 +237,7 @@
 def own_table_kernel(
     n, wav, src, *refs
 ):
-    rec = refs[:7]
-    cur, prev, coef, taps, perturb, part, acc, table, buf, ybuf, gathered, found = refs[7:]
+    rec, cur, prev, coef, taps, perturb, part, acc, table, buf, ybuf, gathered, found = refs
     own_part(n, wav, src, cur, prev, coef, taps, part, acc, buf, ybuf)
     k, nx, depth, ny = perturb.shape
 
@@ -251,7 +248,7 @@
         for j in range(k):
             gs[0][2 + j : 3 + j, :] = perturb[j, x, z, :]
 
-    at_receivers(rec, False, read, [found], [gathered])
+    at_receivers(rec, read, [found], [gathered])
     left = found[...].reshape(16, 128)
     for term in range(3):
         rounded = left.astype(BF)
@@ -260,56 +257,140 @@
     table[48:64, :] = jnp.zeros((16, 128), BF)
 
 
-def own_trace_kernel(n, wav, src, *refs):
-    rec = refs[:7]
-    (cur, prev, coef, taps, perturb, table_low, table_high) = refs[7:14]
-    part, acc, traces, buf, ybuf, ga, gb, ta, tb = refs[14:]
-    own_part(n, wav, src, cur, prev, coef, taps, part, acc, buf, ybuf)
+def share_kernel(*refs):
+    rec, cur, prev, coef, perturb, table_low, table_high, traces = refs[:8]
+    gathered, found = refs[8:14], refs[14:20]
     k, nx, depth, ny = perturb.shape
-
-    def read_beside(row, gs):
+    lane = lax.broadcasted_iota(jnp.int32, (8, 128), 1)
+    for ref in gathered + found:
+        ref[...] = jnp.zeros(ref.shape, F32)
+
+    g2, g1 = gathered[:2]
+    t2, t1 = found[:2]
+
+    def beside(i, c):
+        row, y, at = rec[3, i], rec[4, i], rec[5, i]
         x, z = row // depth - 4, pl.ds(row % depth, 1)
         near = jnp.where(x < 0, 0, nx - 4)
+        weights = []
+        for q in range(4):
+            d = near + q - x
+            away = jnp.abs(d)
+            c2 = c1 = jnp.float32(0.0)
+            for t in range(1, 5):
+                c2 = jnp.where(away == t, jnp.float32(SECOND[t]), c2)
+                c1 = jnp.where(away == t, jnp.float32(FIRST[t]), c1)
+            weights.append((c2, jnp.where(d < 0, -c1, c1)))
         for f in range(F):
             second = first = jnp.zeros((1, ny), F32)
             for q in range(4):
-                p = near + q
-                d = p - x
-                away = jnp.abs(d)
-                c2 = c1 = jnp.float32(0.0)
-                for t in range(1, 5):
-                    c2 = jnp.where(away == t, jnp.float32(SECOND[t]), c2)
-                    c1 = jnp.where(away == t, jnp.float32(FIRST[t]), c1)
-                c1 = jnp.where(d < 0, -c1, c1)
-                u = cur[f, p, z, :]
-                second = second + c2 * u
-                first = first + c1 * u
-            gs[0][f : f + 1, :] = second
-            gs[1][f : f + 1, :] = first
-
-    at_receivers(rec, True, read_beside, [ta, tb], [ga, gb])
+                u = cur[f, near + q, z, :]
+                second = second + weights[q][0] * u
+                first = first + weights[q][1] * u
+            g2[f : f + 1, :] = second
+            g1[f : f + 1, :] = first
+        to = at % 128
+        shift = (to - y + 128) % 128
+        here = lane == to
+        h = at // 128
+        t2[h] = t2[h] + jnp.where(here, pltpu.roll(g2[...], shift, 1), 0.0)
+        t1[h] = t1[h] + jnp.where(here, pltpu.roll(g1[...], shift, 1), 0.0)
+        return c
+
+    lax.fori_loop(0, rec[6, 1], beside, 0)
     both = jnp.zeros((16, 128), F32)
     for table in (table_low, table_high):
         for term in range(3):
             both = both + table[16 * term : 16 * term + 16, :].astype(F32)
-    shares = []
     for h in range(2):
         const = both[8 * h : 8 * h + 8]
-        reach = const[0:1] * ta[h] + const[1:2] * tb[h]
-        shares.append(
-            jnp.concatenate(
-                [reach[1 + j : 2 + j] + const[2 + j : 3 + j] * reach[0:1] for j in range(k)], axis=0
-            )
-        )
-
-    def read_own(row, gs):
-        x, z = row // depth, pl.ds(row % depth, 1)
+        reach = const[0:1] * t2[h] + const[1:2] * t1[h]
         for j in range(k):
-            gs[0][j : j + 1, :] = part[1 + j, x, z, :] + perturb[j, x, z, :] * acc[x, z, :]
-
-    at_receivers(rec, False, read_own, [ta], [ga])
+            traces[h * k + j : h * k + j + 1, :] = (
+                reach[1 + j : 2 + j] + const[2 + j : 3 + j] * reach[0:1]
+            )
+
+    for ref in found:
+        ref[...] = jnp.zeros(ref.shape, F32)
+    gs, gz, gx, gu, gp, gc = gathered
+    fs, fz, fx, fy, fu, fc = found
+
+    def inside(at, size, weight):
+        return jnp.where((at >= 0) & (at < size), jnp.float32(weight), jnp.float32(0.0))
+
+    def own(i, c):
+        row, y, at = rec[0, i], rec[1, i], rec[2, i]
+        x, z = row // depth, row % depth
+        here_z = pl.ds(z, 1)
+        reach = []
+        for d in (1, 2, 3, 4, -1, -2, -3, -4):
+            t = abs(d)
+            sign = 1.0 if d > 0 else -1.0
+            px, pz = jnp.clip(x + d, 0, nx - 1), jnp.clip(z + d, 0, depth - 1)
+            reach.append(
+                (
+                    px,
+                    inside(x + d, nx, SECOND[t]),
+                    inside(x + d, nx, sign * FIRST[t]),
+                    pl.ds(pz, 1),
+                    inside(z + d, depth, SECOND[t]),
+                    inside(z + d, depth, sign * FIRST[t]),
+                )
+            )
+        for f in range(F):
+            u = cur[f, x, here_z, :]
+            second = (3.0 * CENTRE) * u
+            along_x = along_z = jnp.zeros((1, ny), F32)
+            for px, x2, x1, pz, z2, z1 in reach:
+                v = cur[f, px, here_z, :]
+                w = cur[f, x, pz, :]
+                second = second + x2 * v + z2 * w
+                along_x = along_x + x1 * v
+                along_z = along_z + z1 * w
+            gs[f : f + 1, :] = second
+            gz[f : f + 1, :] = along_z
+            gx[f : f + 1, :] = along_x
+            gu[f : f + 1, :] = u
+            gp[f : f + 1, :] = 2.0 * u - prev[f, x, here_z, :]
+        for a in range(4):
+            gc[a : a + 1, :] = coef[a, x, here_z, :]
+        for j in range(k):
+            gc[4 + j : 5 + j, :] = perturb[j, x, here_z, :]
+        to = at % 128
+        shift = to - y + 256
+        here = lane == to
+        h = at // 128
+
+        def moved(ref, by=0):
+            return pltpu.roll(ref[...], (shift - by) % 128, 1)
+
+        second, along_y = moved(gs), jnp.zeros((8, 128), F32)
+        for d in (1, 2, 3, 4, -1, -2, -3, -4):
+            t = abs(d)
+            v = moved(gu, d)
+            second = second + inside(y + d, ny, SECOND[t]) * v
+            along_y = along_y + inside(y + d, ny, FIRST[t] if d > 0 else -FIRST[t]) * v
+        for ref, value in (
+            (fs, second),
+            (fz, moved(gz)),
+            (fx, moved(gx)),
+            (fy, along_y),
+            (fu, moved(gp)),
+            (fc, moved(gc)),
+        ):
+            ref[h] = ref[h] + jnp.where(here, value, 0.0)
+        return c
+
+    lax.fori_loop(0, rec[6, 0], own, 0)
     for h in range(2):
-        traces[h * k : h * k + k, :] = shares[h] + ta[h, 0:k, :]
+        con = fc[h]
+        value = con[0:1] * fs[h] + con[1:2] * fz[h] + con[2:3] * fx[h] + con[3:4] * fy[h]
+        base = fu[h] + value
+        for j in range(k):
+            at = slice(h * k + j, h * k + j + 1)
+            traces[at, :] = (
+                traces[at, :] + base[1 + j : 2 + j] + con[4 + j : 5 + j] * value[0:1]
+            )
 
 
 def near_planes(msg, f, first, rs):
@@ -377,20 +458,34 @@
                 j + 1, row // depth, pl.ds(row % depth, 1), :
             ]
 
-    at_receivers(rec, False, read, [traces], [gathered])
-
-
-def gather_kernel(labels, *refs):
-    rec = refs[:7]
-    part, acc_own, low_in, high_in, coef, incoming = refs[7:13]
-    nxt, perturb, low, high, traces, acc, gathered = refs[13:]
+    at_receivers(rec, read, [traces], [gathered])
+
+
+def gather_kernel(*refs):
+    rec = refs[0]
+    far = refs[1:7]
+    nxt, perturb, low, high, traces = refs[7:12]
+    near = refs[12:18]
+    acc, gathered, names, labels, arrived, landed = refs[18:]
+    loads = [pltpu.make_async_copy(a, b, landed.at[i]) for i, (a, b) in enumerate(zip(far, near))]
+    for load in reversed(loads):
+        load.start()
+    part, acc_own, low_in, high_in, coef, incoming = near
     k, nx, depth, ny = perturb.shape
+    loads[5].wait()
     zb = (incoming.shape[1] - 16) // (CAP * k)
+    for t in range(incoming.shape[0]):
+        names[t : t + 1, :] = (
+            incoming[t, CAP * k * zb : CAP * k * zb + 16, :].astype(F32)[0:1].astype(jnp.int32)
+        )
+    copy = pltpu.make_async_copy(names, labels, arrived)
+    copy.start()
     perturb[...] = jnp.zeros(perturb.shape, F32)
+    copy.wait()
 
     def add(s, c):
-        label = labels[s]
         t, a = s // CAP, s % CAP
+        label = labels[t, a]
 
         @pl.when(label > 0)
         def _():
@@ -406,14 +501,19 @@
         return c
 
     lax.fori_loop(0, incoming.shape[0] * CAP, add, 0)
+    for load in loads[:5]:
+        load.wait()
     finish_part(0, part, acc_own, low_in, high_in, coef, perturb, acc, nxt, low, high, None)
     sample_new(0, rec, nxt, traces, gathered, depth, k)
 
 
 def finish_kernel(n, *refs):
-    rec = refs[:7]
-    part, acc_own, low_in, high_in, coef, perturb = refs[7:13]
-    rest = refs[13:]
+    if n == ITERS - 1:
+        rec = None
+    else:
+        rec, refs = refs[0], refs[1:]
+    part, acc_own, low_in, high_in, coef, perturb = refs[:6]
+    rest = refs[6:]
     k, nx, depth, ny = perturb.shape
     if n == ITERS - 1:
         out, acc = rest
@@ -476,8 +576,6 @@
 
     packed = pack(pieces, piece_target[:, 0], piece_block, tiles)
     incoming = lax.all_to_all(packed, "tile", 0, 0, tiled=True)
-    names = incoming[:, CAP * k * zb : CAP * k * zb + CAP, 0]
-    labels = names.astype(jnp.int32).reshape(tiles * CAP)
 
     def face(planes):
         near = two_terms(background_now[:, planes[0], :])
@@ -519,14 +617,14 @@
     work = [VM((nx + 8, depth + 16, ny), F32), VM((nx, depth, 2 * ny), F32)]
     cells = F * nx * depth * ny
 
-    def call(kernel, name, out_shape, scratch, scalars, arrays, flops):
+    def call(kernel, name, out_shape, scratch, scalars, arrays, flops, spec=vspec(), mib=16):
         return pl.pallas_call(
             kernel,
             out_shape=out_shape,
-            in_specs=[sspec()] * len(scalars) + [vspec()] * len(arrays),
+            in_specs=[sspec()] * len(scalars) + [spec] * len(arrays),
             out_specs=tuple(vspec() for _ in out_shape),
             scratch_shapes=scratch,
-            compiler_params=params(),
+            compiler_params=params(mib),
             cost_estimate=cost(flops * cells, 16 * cells),
             name=name,
         )(*scalars, *arrays)
@@ -543,19 +641,22 @@
                 name,
                 (state, field, jax.ShapeDtypeStruct((64, 128), BF)),
                 work + [small, pair],
-                start + tuple(rec),
+                start + (rec,),
                 arrays + (perturb,),
                 80,
             )
         elif n == ITERS - 1:
-            part, acc, mine = call(
-                functools.partial(own_trace_kernel, n),
-                name,
-                (state, field, jax.ShapeDtypeStruct((8, 128), F32)),
-                work + [small, small, pair, pair],
-                start + tuple(rec),
-                arrays + (perturb,) + tables,
-                80,
+            (mine,) = call(
+                share_kernel,
+                "share",
+                (jax.ShapeDtypeStruct((8, 128), F32),),
+                [small] * 6 + [pair] * 6,
+                (rec,),
+                (cur, prev, coef, perturb) + tables,
+                20,
+            )
+            part, acc = call(
+                functools.partial(own_kernel, n), name, (state, field), work, start, arrays, 80000
             )
         else:
             part, acc = call(
@@ -569,10 +670,20 @@
                 gather_kernel,
                 name,
                 (state, jax.ShapeDtypeStruct((k, nx, depth, ny), F32), faces, faces, traced),
-                [keep, small],
-                (labels,) + tuple(rec),
+                [VM(a.shape, a.dtype) for a in arrays + (incoming,)]
+                + [
+                    keep,
+                    small,
+                    VM((tiles, 128), jnp.int32),
+                    SM((tiles, 128), jnp.int32),
+                    pltpu.SemaphoreType.DMA,
+                    pltpu.SemaphoreType.DMA((6,)),
+                ],
+                (rec,),
                 arrays + (incoming,),
                 20,
+                pl.BlockSpec(memory_space=pltpu.HBM),
+                58,
             )
         elif n == ITERS - 1:
             (born,) = call(
@@ -580,7 +691,7 @@
                 name,
                 (jax.ShapeDtypeStruct((k, depth * nx, ny), F32),),
                 [keep],
-                tuple(rec),
+                (),
                 arrays + (perturb,),
                 20,
             )
@@ -592,7 +703,7 @@
                 name,
                 (state, face_type, face_type, traced),
                 [keep, small],
-                tuple(rec),
+                (rec,),
                 arrays + (perturb,) + ((table,) if n == 1 else ()),
                 20,
             )
@@ -607,7 +718,6 @@
     odd = place % 2
     half = jnp.where(odd == 0, early[0], early[1])
     message = jnp.concatenate([half, mine[None]])
-    message, low_in, high_in = lax.optimization_barrier((message, low_in, high_in))
     groups = [list(range(c, tiles, 2)) for c in range(2)]
     copies = lax.all_to_all(
         jnp.broadcast_to(message[None], (tiles // 2,) + message.shape),
@@ -617,6 +727,7 @@
         axis_index_groups=groups,
         tiled=True,
     )
+    copies, born = lax.optimization_barrier((copies, born))
     total = jnp.sum(copies, axis=0)
     other = swap(total)
     ours, theirs = total[:2], other[:2]

time: 283 us -> 256 us (0.905)
  the two profiles are of different devices: /device:TPU:89 before, /device:TPU:1 now
where the time goes in v2:
time: 256 us; the launch traced here: 255 us
  waiting for transfers between devices  110 us (43%)
  Pallas kernels  57.3 us (22%)
  starting transfers between devices  56.6 us (22%)
  local copies, waits for them, and re-layouts  24 us (9%)
  other arithmetic  4.41 us (2%)
    ppermute x4, waiting for transfers between devices, exchange(): lax.ppermute(low, 'tile', backward)  91.1 us
    pallas_call x9, Pallas kernels, call(): pl.pallas_call(kernel, out_shape=out_shape, in_specs=[sspec()] * len(scal...  47.8 us
    ppermute x4, starting transfers between devices, exchange(): lax.ppermute(high, 'tile', forward)  20.5 us
    all_to_all x1, starting transfers between devices, local(): incoming = lax.all_to_all(packed, 'tile', 0, 0, tiled=True)  19.4 us
    ppermute x4, waiting for transfers between devices, exchange(): lax.ppermute(high, 'tile', forward)  18.5 us
    unnamed x77, local copies, waits for them, and re-layouts  17.9 us
    ppermute x4, starting transfers between devices, exchange(): lax.ppermute(low, 'tile', backward)  7.67 us
    pallas_call x1, Pallas kernels, list_receivers(): pl.pallas_call(list_kernel, out_shape=jax.ShapeDtypeStruct((8, n), jnp.in...  6.43 us
  transfers between devices with their start and end apart: 12, of which 7 were waited for; matrix products, arithmetic and copies ran while one was open for 5% of the time, Pallas kernels for 15%

profile of v2, /device:TPU:1, one launch (start us, length us, event | category | flops | bytes accessed | tf_op | source)
XLA Modules:
  0.0 254.5 jit_solution(1189163423985025334)
XLA Ops:
  0.6 1.2 copy-done.10
  1.9 0.7 copy-done.23
  2.5 0.7 copy-done.24
  3.2 3.0 %pack.1 = bf16[32,272,128]{2,1,0:T(8,128)(2,1)} custom-call(s32[32]{0:T(128)S(1)} %bitcast.107, s32[32]{0:T(128)S(1)} %copy-done.24, bf16[4,32,32,128]{3,2,1,0:T(8,128)(2,1)S(1)} %copy-done.10), custom_call_target="tpu_custom_call" | custom-call | tf_op jit(solution)/shard_map/pack/pallas_call | solution.py:85
  6.2 19.4 %all-to-all-start = ((bf16[32,272,128]{2,1,0:T(8,128)(2,1)}), bf16[32,272,128]{2,1,0:T(8,128)(2,1)}, u32[]{:S(2)}, u32[]{:S(2)}) async-start(bf16[32,272,128]{2,1,0:T(8,128)(2,1)} %pack.1), calls=%async_computation | async-start | bytes 4456448 | tf_op jit(solution)/shard_map/all_to_all | solution.py:578
  25.7 0.9 copy-done.25
  26.6 1.2 fusion.7
  27.9 0.6 constant_dynamic-update-slice_fusion.11
  28.5 0.6 constant_dynamic-update-slice_fusion.10
  29.1 0.6 constant_dynamic-update-slice_fusion.4
  29.7 0.6 constant_dynamic-update-slice_fusion.9
  30.4 0.6 constant_dynamic-update-slice_fusion.8
  31.0 0.6 constant_dynamic-update-slice_fusion.7
  31.6 0.7 constant_dynamic-update-slice_fusion
  32.3 7.6 %collective-permute-start = (bf16[21,64,128]{2,1,0:T(8,128)(2,1)}, bf16[21,64,128]{2,1,0:T(8,128)(2,1)}, u32[]{:S(2)}, u32[]{:S(2)}) collective-permute-start(bf16[21,64,128]{2,1,0:T(8,128)(2,1)} %constant_dynamic-update-slice_fusion), channel_id=1, source_target_pairs={{0,16},{16,32},{32,48},{48,64},{64,80},{80,96},{96,112},{112,128},... | collective-permute-start | bytes 1032200 | tf_op jit(solution)/shard_map/ppermute | solution.py:542
  40.0 0.7 constant_dynamic-update-slice_fusion.6
  40.8 1.9 collective-permute-start.1
  42.7 0.6 fusion.9
  44.4 1.3 copy-done.29
  45.9 1.4 pad_add_fusion.1.src
  47.3 6.4 %receivers.1.refs_0_ = s32[8,256]{1,0:T(8,128)S(1)} custom-call(s32[256]{0:T(256)S(1)} %copy-done.20, s32[256]{0:T(256)S(1)} %copy-done.21, s32[256]{0:T(256)S(1)} %copy-done.22, s32[3]{0:T(128)S(1)} %pad_add_fusion.where), custom_call_target="tpu_custom_call" | custom-call | tf_op jit(solution)/shard_map/receivers/pallas_call | solution.py:125
  53.7 0.6 copy-done.11
  54.3 0.1 pad_maximum_fusion.1.prev
  54.5 0.8 copy-done.27
  55.3 0.1 pad_maximum_fusion.cur.refs_2_
  55.4 0.8 copy-done.9
  56.2 6.0 %own1.1 = (f32[5,8,64,128]{3,2,1,0:T(8,128)S(1)}, f32[8,64,128]{2,1,0:T(8,128)S(1)}) custom-call(f32[4]{0:T(128)S(1)} %copy-done.17, s32[3]{0:T(128)S(1)} %pad_add_fusion.1.src, f32[5,8,64,128]{3,2,1,0:T(8,128)S(1)} %pad_maximum_fusion.cur.refs_2_, f32[5,8,64,128]{3,2,1,0:T(8,128)S(1)} %pad_maximum_fusion.1.prev, ...), custom_call_target="tpu_custom_call" | custom-call | flops 26214400 | bytes 5242880 | tf_op jit(solution)/shard_map/own1/pallas_call | solution.py:621
  62.2 1.1 copy-done.8
  63.3 0.7 copy-done.13
  64.0 18.3 %collective-permute-done.refs_3_ = bf16[21,64,128]{2,1,0:T(8,128)(2,1)} collective-permute-done((bf16[21,64,128]{2,1,0:T(8,128)(2,1)}, bf16[21,64,128]{2,1,0:T(8,128)(2,1)}, u32[]{:S(2)}, u32[]{:S(2)}) %collective-permute-start) | collective-permute-done | bytes 344096 | tf_op jit(solution)/shard_map/ppermute | solution.py:542
  82.3 59.9 %collective-permute-done.1.refs_4_ = bf16[21,64,128]{2,1,0:T(8,128)(2,1)} collective-permute-done((bf16[21,64,128]{2,1,0:T(8,128)(2,1)}, bf16[21,64,128]{2,1,0:T(8,128)(2,1)}, u32[]{:S(2)}, u32[]{:S(2)}) %collective-permute-start.1) | collective-permute-done | bytes 344096 | tf_op jit(solution)/shard_map/ppermute | solution.py:542
  142.2 8.7 %finish1.1 = (f32[5,8,64,128]{3,2,1,0:T(8,128)}, f32[4,8,64,128]{3,2,1,0:T(8,128)}, bf16[25,64,128]{2,1,0:T(8,128)(2,1)}, bf16[25,64,128]{2,1,0:T(8,128)(2,1)}, f32[2,8,128]{2,1,0:T(8,128)}) custom-call(s32[8,256]{1,0:T(8,128)} %copy-done.11, f32[5,8,64,128]{3,2,1,0:T(8,128)} %copy-done.8, f32[8,64,128]{2,1,0:T(8,128)} %copy-done.13, ...), custom_call_target="tpu_custom_call" | custom-call | flops 6553600 | bytes 5242880 | tf_op jit(solution)/shard_map/finish1/pallas_call | solution.py:621
  150.9 3.7 %collective-permute-start.2 = (bf16[25,64,128]{2,1,0:T(8,128)(2,1)}, bf16[25,64,128]{2,1,0:T(8,128)(2,1)S(1)}, u32[]{:S(2)}, u32[]{:S(2)}) collective-permute-start(bf16[25,64,128]{2,1,0:T(8,128)(2,1)} %get-tuple-element.33), channel_id=1, source_target_pairs={{0,16},{16,32},{32,48},{48,64},{64,80},{80,96},{96,112},{112,128},... | collective-permute-start | bytes 1228808 | tf_op jit(solution)/shard_map/ppermute | solution.py:542
  154.6 1.9 collective-permute-start.3
  156.6 1.2 copy-done.2
  157.8 1.3 copy-done.4
  159.1 7.0 %own2.1 = (f32[5,8,64,128]{3,2,1,0:T(8,128)S(1)}, f32[8,64,128]{2,1,0:T(8,128)S(1)}, bf16[64,128]{1,0:T(8,128)(2,1)S(1)}) custom-call(f32[4]{0:T(128)S(1)} %copy-done.17, s32[3]{0:T(128)S(1)} %pad_add_fusion.1.src, s32[8,256]{1,0:T(8,128)S(1)} %copy-done.12, f32[5,8,64,128]{3,2,1,0:T(8,128)S(1)} %copy-done.4, ...), custom_call_target="tpu_custom_call" | custom-call | flops 26214400 | bytes 5242880 | tf_op jit(solution)/shard_map/own2/pallas_call | solution.py:621
  166.1 0.2 collective-permute-done.2.refs_3_
  166.4 3.0 %collective-permute-done.3.refs_4_ = bf16[25,64,128]{2,1,0:T(8,128)(2,1)S(1)} collective-permute-done((bf16[25,64,128]{2,1,0:T(8,128)(2,1)}, bf16[25,64,128]{2,1,0:T(8,128)(2,1)S(1)}, u32[]{:S(2)}, u32[]{:S(2)}) %collective-permute-start.3) | collective-permute-done | bytes 409632 | tf_op jit(solution)/shard_map/ppermute | solution.py:542
  169.4 3.4 %finish2.1 = (f32[5,8,64,128]{3,2,1,0:T(8,128)S(1)}, bf16[26,64,128]{2,1,0:T(8,128)(2,1)}, bf16[26,64,128]{2,1,0:T(8,128)(2,1)}, f32[2,8,128]{2,1,0:T(8,128)S(1)}) custom-call(s32[8,256]{1,0:T(8,128)S(1)} %copy-done.12, f32[5,8,64,128]{3,2,1,0:T(8,128)S(1)} %get-tuple-element.31.refs_1_, f32[8,64,128]{2,1,0:T(8,128)S(1)} %get-tuple-element.32.refs_2_, ...), custom_call_target="tpu_custom_call" | custom-call | flops 6553600 | bytes 5242880 | tf_op jit(solution)/shard_map/finish2/pallas_call | solution.py:621
  172.8 4.5 %collective-permute-start.4 = (bf16[26,64,128]{2,1,0:T(8,128)(2,1)}, bf16[26,64,128]{2,1,0:T(8,128)(2,1)}, u32[]{:S(2)}, u32[]{:S(2)}) collective-permute-start(bf16[26,64,128]{2,1,0:T(8,128)(2,1)} %get-tuple-element.40), channel_id=1, source_target_pairs={{0,16},{16,32},{32,48},{48,64},{64,80},{80,96},{96,112},{112,128},... | collective-permute-start | bytes 1277960 | tf_op jit(solution)/shard_map/ppermute | solution.py:542
  177.3 1.9 collective-permute-start.5
  179.3 1.3 copy-done.5
  180.6 0.7 copy-done.15
  181.3 0.7 copy-done.18
  181.9 6.0 %own3.1 = (f32[5,8,64,128]{3,2,1,0:T(8,128)S(1)}, f32[8,64,128]{2,1,0:T(8,128)S(1)}) custom-call(f32[4]{0:T(128)S(1)} %copy-done.18, s32[3]{0:T(128)S(1)} %copy-done.15, f32[5,8,64,128]{3,2,1,0:T(8,128)S(1)} %get-tuple-element.37.cur.refs_2_.prev, f32[5,8,64,128]{3,2,1,0:T(8,128)S(1)} %copy-done.5, f32[4,8,64,128]{3,2,1,0:T(8,128)S(1)} %copy-done.1, ...), custom_call_target="tpu_custom_call" | custom-call | flops 26214400 | bytes 5242880 | tf_op jit(solution)/shard_map/own3/pallas_call | solution.py:621
  188.0 18.3 %collective-permute-done.5.refs_4_ = bf16[26,64,128]{2,1,0:T(8,128)(2,1)} collective-permute-done((bf16[26,64,128]{2,1,0:T(8,128)(2,1)}, bf16[26,64,128]{2,1,0:T(8,128)(2,1)}, u32[]{:S(2)}, u32[]{:S(2)}) %collective-permute-start.5) | collective-permute-done | bytes 426016 | tf_op jit(solution)/shard_map/ppermute | solution.py:542
  206.3 3.9 %finish3.1 = (f32[5,8,64,128]{3,2,1,0:T(8,128)S(1)}, bf16[25,64,128]{2,1,0:T(8,128)(2,1)}, bf16[25,64,128]{2,1,0:T(8,128)(2,1)}, f32[2,8,128]{2,1,0:T(8,128)S(1)}) custom-call(s32[8,256]{1,0:T(8,128)S(1)} %copy-done.12, f32[5,8,64,128]{3,2,1,0:T(8,128)S(1)} %get-tuple-element.38.refs_1_, f32[8,64,128]{2,1,0:T(8,128)S(1)} %get-tuple-element.39.refs_2_, ...), custom_call_target="tpu_custom_call" | custom-call | flops 6553600 | bytes 5242880 | tf_op jit(solution)/shard_map/finish3/pallas_call | solution.py:621
  210.2 1.9 collective-permute-start.6
  212.1 4.7 %collective-permute-start.7 = (bf16[25,64,128]{2,1,0:T(8,128)(2,1)}, bf16[25,64,128]{2,1,0:T(8,128)(2,1)}, u32[]{:S(2)}, u32[]{:S(2)}) collective-permute-start(bf16[25,64,128]{2,1,0:T(8,128)(2,1)} %get-tuple-element.46), channel_id=1, source_target_pairs={{0,16},{16,32},{32,48},{48,64},{64,80},{80,96},{96,112},{112,128},... | collective-permute-start | bytes 1228808 | tf_op jit(solution)/shard_map/ppermute | solution.py:542
  216.9 1.9 collective-permute-start.8
  218.8 0.7 slice_bitcast_fusion.3.refs_5_
  219.5 0.7 slice_bitcast_fusion.2.refs_6_
  220.2 3.9 %share.1 = f32[8,128]{1,0:T(8,128)S(1)} custom-call(s32[8,256]{1,0:T(8,128)S(1)} %copy-done.12, f32[5,8,64,128]{3,2,1,0:T(8,128)S(1)} %get-tuple-element.43.refs_1_.cur, f32[5,8,64,128]{3,2,1,0:T(8,128)S(1)} %get-tuple-element.37.cur.refs_2_.prev, f32[4,8,64,128]{3,2,1,0:T(8,128)S(1)} %copy-done.1, f32[4,8,64,128]{3,2,1,0:T(8,128)S(1)} %copy-done.3, ...), custom_call_target="tpu_custom_call" | custom-call | flops 6553600 | bytes 5242880 | tf_op jit(solution)/shard_map/share/pallas_call | solution.py:621
  224.2 0.7 broadcast_in_dim.25
  224.9 4.2 %all-to-all-start.1 = ((f32[16,3,8,128]{3,2,1,0:T(8,128)}), f32[16,3,8,128]{3,2,1,0:T(8,128)}, u32[]{:S(2)}, u32[]{:S(2)}) async-start(f32[16,3,8,128]{3,2,1,0:T(8,128)} %broadcast_in_dim.25), calls=%async_computation.1 | async-start | bytes 393216 | tf_op jit(solution)/shard_map/all_to_all | solution.py:722
  229.1 1.3 copy-done.7
  230.4 5.9 %own4.1 = (f32[5,8,64,128]{3,2,1,0:T(8,128)S(1)}, f32[8,64,128]{2,1,0:T(8,128)S(1)}) custom-call(f32[4]{0:T(128)S(1)} %copy-done.19, s32[3]{0:T(128)S(1)} %copy-done.16, f32[5,8,64,128]{3,2,1,0:T(8,128)S(1)} %copy-done.7, f32[5,8,64,128]{3,2,1,0:T(8,128)S(1)} %get-tuple-element.37.cur.refs_2_.prev, f32[4,8,64,128]{3,2,1,0:T(8,128)S(1)} %copy-done.1, ...), custom_call_target="tpu_custom_call" | custom-call | flops 26214400000 | bytes 5242880 | tf_op jit(solution)/shard_map/own4/pallas_call | solution.py:621
  236.4 9.8 %collective-permute-done.8.refs_3_ = bf16[25,64,128]{2,1,0:T(8,128)(2,1)} collective-permute-done((bf16[25,64,128]{2,1,0:T(8,128)(2,1)}, bf16[25,64,128]{2,1,0:T(8,128)(2,1)}, u32[]{:S(2)}, u32[]{:S(2)}) %collective-permute-start.8) | collective-permute-done | bytes 409632 | tf_op jit(solution)/shard_map/ppermute | solution.py:542
  246.3 2.9 %finish4.1 = f32[4,512,128]{2,1,0:T(8,128)} custom-call(f32[5,8,64,128]{3,2,1,0:T(8,128)S(1)} %get-tuple-element.44.refs_0_, f32[8,64,128]{2,1,0:T(8,128)S(1)} %get-tuple-element.45.refs_1_, bf16[25,64,128]{2,1,0:T(8,128)(2,1)} %collective-permute-done.7.refs_2_, bf16[25,64,128]{2,1,0:T(8,128)(2,1)} %collective-permute-done.8.refs_3_, ...), custom_call_target="tpu_custom_call" | custom-call | flops 6553600 | bytes 5242880 | tf_op jit(solution)/shard_map/finish4/pallas_call | solution.py:621
  249.2 0.9 reduce_sum.9
  250.1 2.9 %collective-permute-start.9 = (f32[3,8,128]{2,1,0:T(8,128)S(1)}, f32[3,8,128]{2,1,0:T(8,128)S(1)}, u32[]{:S(2)}, u32[]{:S(2)}) collective-permute-start(f32[3,8,128]{2,1,0:T(8,128)S(1)} %reduce_sum.9), channel_id=1, source_target_pairs={{0,16},{16,0},{32,48},{48,32},{64,80},{80,64},{96,112},{112,96},{1... | collective-permute-start | bytes 36872 | tf_op jit(solution)/shard_map/ppermute | solution.py:547
  253.1 0.8 collective-permute-done.9
  253.9 0.6 reshape.174
  (86 shorter events, 1.0 us)
Async XLA Ops:
  0.6 1.2 copy-start.10
  1.9 0.7 copy-start.23
  2.5 0.7 copy-start.24
  6.2 19.4 %copy-start.28 = (f32[64,8,128]{2,1,0:T(8,128)S(1)}, f32[64,8,128]{2,1,0:T(8,128)}, u32[]{:S(2)}) copy-start(f32[64,8,128]{2,1,0:T(8,128)} %param.16) | copy-start | bytes 786436
  6.2 136.0 %all-to-all-start = ((bf16[32,272,128]{2,1,0:T(8,128)(2,1)}), bf16[32,272,128]{2,1,0:T(8,128)(2,1)}, u32[]{:S(2)}, u32[]{:S(2)}) async-start(bf16[32,272,128]{2,1,0:T(8,128)(2,1)} %pack.1), calls=%async_computation | async-start | bytes 4456448 | tf_op jit(solution)/shard_map/all_to_all | solution.py:578
  25.6 1.0 copy-start.25
  26.6 2.5 copy-start.26
  32.3 10.4 %copy-start.34 = (s32[3]{0:T(128)S(1)}, s32[3]{0:T(128)}, u32[]{:S(2)}) copy-start(s32[3]{0:T(128)} %param.25) | copy-start | bytes 40
  32.3 11.8 %copy-start.32 = (bf16[64,8,128]{2,1,0:T(8,128)(2,1)S(1)}, bf16[64,8,128]{2,1,0:T(8,128)(2,1)}, u32[]{:S(2)}) copy-start(bf16[64,8,128]{2,1,0:T(8,128)(2,1)} %param.17) | copy-start | bytes 393220
  32.3 50.0 %collective-permute-start = (bf16[21,64,128]{2,1,0:T(8,128)(2,1)}, bf16[21,64,128]{2,1,0:T(8,128)(2,1)}, u32[]{:S(2)}, u32[]{:S(2)}) collective-permute-start(bf16[21,64,128]{2,1,0:T(8,128)(2,1)} %constant_dynamic-update-slice_fusion), channel_id=1, source_target_pairs={{0,16},{16,32},{32,48},{48,64},{64,80},{80,96},{96,112},{112,128},... | collective-permute-start | bytes 1032200 | tf_op jit(solution)/shard_map/ppermute | solution.py:542
  39.9 4.2 %copy-start.30 = (bf16[3,64,8,128]{3,2,1,0:T(8,128)(2,1)S(1)}, bf16[3,64,8,128]{3,2,1,0:T(8,128)(2,1)}, u32[]{:S(2)}) copy-start(bf16[3,64,8,128]{3,2,1,0:T(8,128)(2,1)} %param.18) | copy-start | bytes 1179652
  40.8 101.4 %collective-permute-start.1 = (bf16[21,64,128]{2,1,0:T(8,128)(2,1)}, bf16[21,64,128]{2,1,0:T(8,128)(2,1)}, u32[]{:S(2)}, u32[]{:S(2)}) collective-permute-start(bf16[21,64,128]{2,1,0:T(8,128)(2,1)} %constant_dynamic-update-slice_fusion.6), channel_id=1, source_target_pairs={{16,0},{32,16},{48,32},{64,48},{80,64},{96,80},{112,96},{128,112},... | collective-permute-start | bytes 1032200 | tf_op jit(solution)/shard_map/ppermute | solution.py:542
  44.3 11.1 %copy-start = (f32[4,8,64,128]{3,2,1,0:T(8,128)}, f32[4,8,64,128]{3,2,1,0:T(8,128)S(1)}, u32[]{:S(2)}) copy-start(f32[4,8,64,128]{3,2,1,0:T(8,128)S(1)} %maximum_bitcast_fusion.coef.refs_5_.refs_3_.refs_4_) | copy-start | bytes 3145732
  44.3 1.4 copy-start.29
  44.3 2.9 %copy-start.31 = (f32[64,8,128]{2,1,0:T(8,128)S(1)}, f32[64,8,128]{2,1,0:T(8,128)}, u32[]{:S(2)}) copy-start(f32[64,8,128]{2,1,0:T(8,128)} %param.15) | copy-start | bytes 786436
  45.7 1.5 copy-start.20
  45.7 1.6 copy-start.21
  45.7 1.6 copy-start.22
  47.2 109.3 %copy-start.14 = (s32[3]{0:T(128)}, s32[3]{0:T(128)S(1)}, u32[]{:S(2)}) copy-start(s32[3]{0:T(128)S(1)} %pad_add_fusion.1.src) | copy-start | bytes 40
  53.7 0.6 copy-start.11
  54.3 0.9 copy-start.27
  55.3 0.9 copy-start.9
  55.3 0.9 copy-start.17
  62.2 1.1 copy-start.8
  63.3 0.8 copy-start.13
  142.2 14.3 %copy-start.1 = (f32[4,8,64,128]{3,2,1,0:T(8,128)S(1)}, f32[4,8,64,128]{3,2,1,0:T(8,128)}, u32[]{:S(2)}) copy-start(f32[4,8,64,128]{3,2,1,0:T(8,128)} %copy-done) | copy-start | bytes 3145732
  142.2 14.4 %copy-start.12 = (s32[8,256]{1,0:T(8,128)S(1)}, s32[8,256]{1,0:T(8,128)}, u32[]{:S(2)}) copy-start(s32[8,256]{1,0:T(8,128)} %copy-done.11) | copy-start | bytes 24580
  150.9 15.4 %collective-permute-start.2 = (bf16[25,64,128]{2,1,0:T(8,128)(2,1)}, bf16[25,64,128]{2,1,0:T(8,128)(2,1)S(1)}, u32[]{:S(2)}, u32[]{:S(2)}) collective-permute-start(bf16[25,64,128]{2,1,0:T(8,128)(2,1)} %get-tuple-element.33), channel_id=1, source_target_pairs={{0,16},{16,32},{32,48},{48,64},{64,80},{80,96},{96,112},{112,128},... | collective-permute-start | bytes 1228808 | tf_op jit(solution)/shard_map/ppermute | solution.py:542
  154.6 14.8 %collective-permute-start.3 = (bf16[25,64,128]{2,1,0:T(8,128)(2,1)}, bf16[25,64,128]{2,1,0:T(8,128)(2,1)S(1)}, u32[]{:S(2)}, u32[]{:S(2)}) collective-permute-start(bf16[25,64,128]{2,1,0:T(8,128)(2,1)} %get-tuple-element.34), channel_id=1, source_target_pairs={{16,0},{32,16},{48,32},{64,48},{80,64},{96,80},{112,96},{128,112},... | collective-permute-start | bytes 1228808 | tf_op jit(solution)/shard_map/ppermute | solution.py:542
  156.6 1.2 copy-start.2
  157.8 1.3 copy-start.4
  159.1 10.3 %copy-start.3 = (f32[4,8,64,128]{3,2,1,0:T(8,128)S(1)}, f32[4,8,64,128]{3,2,1,0:T(8,128)}, u32[]{:S(2)}) copy-start(f32[4,8,64,128]{3,2,1,0:T(8,128)} %get-tuple-element.30.refs_5_.refs_6_.refs_4_) | copy-start | bytes 3145732
  172.8 15.2 %collective-permute-start.4 = (bf16[26,64,128]{2,1,0:T(8,128)(2,1)}, bf16[26,64,128]{2,1,0:T(8,128)(2,1)}, u32[]{:S(2)}, u32[]{:S(2)}) collective-permute-start(bf16[26,64,128]{2,1,0:T(8,128)(2,1)} %get-tuple-element.40), channel_id=1, source_target_pairs={{0,16},{16,32},{32,48},{48,64},{64,80},{80,96},{96,112},{112,128},... | collective-permute-start | bytes 1277960 | tf_op jit(solution)/shard_map/ppermute | solution.py:542
  177.3 29.0 %collective-permute-start.5 = (bf16[26,64,128]{2,1,0:T(8,128)(2,1)}, bf16[26,64,128]{2,1,0:T(8,128)(2,1)}, u32[]{:S(2)}, u32[]{:S(2)}) collective-permute-start(bf16[26,64,128]{2,1,0:T(8,128)(2,1)} %get-tuple-element.41), channel_id=1, source_target_pairs={{16,0},{32,16},{48,32},{64,48},{80,64},{96,80},{112,96},{128,112},... | collective-permute-start | bytes 1277960 | tf_op jit(solution)/shard_map/ppermute | solution.py:542
  179.3 1.3 copy-start.5
  180.6 0.7 copy-start.15
  181.3 0.7 copy-start.18
  181.9 6.0 %copy-start.33 = (f32[2,8,128]{2,1,0:T(8,128)S(1)}, f32[2,8,128]{2,1,0:T(8,128)}, u32[]{:S(2)}) copy-start(f32[2,8,128]{2,1,0:T(8,128)} %get-tuple-element.28) | copy-start | bytes 24580
  210.2 14.0 %copy-start.6 = (f32[5,8,64,128]{3,2,1,0:T(8,128)}, f32[5,8,64,128]{3,2,1,0:T(8,128)S(1)}, u32[]{:S(2)}) copy-start(f32[5,8,64,128]{3,2,1,0:T(8,128)S(1)} %get-tuple-element.43.refs_1_.cur) | copy-start | bytes 3932164
  210.2 14.0 %collective-permute-start.6 = (f32[2,2,8,128]{3,2,1,0:T(8,128)S(1)}, f32[2,2,8,128]{3,2,1,0:T(8,128)S(1)}, u32[]{:S(2)}, u32[]{:S(2)}) collective-permute-start(f32[2,2,8,128]{3,2,1,0:T(8,128)S(1)} %pad_maximum_fusion.4), channel_id=1, source_target_pairs={{0,16},{16,0},{32,48},{48,32},{64,80},{80,64},{96,112},{112,96},{1... | collective-permute-start | bytes 49160 | tf_op jit(solution)/shard_map/ppermute | solution.py:547
  212.1 24.3 %collective-permute-start.7 = (bf16[25,64,128]{2,1,0:T(8,128)(2,1)}, bf16[25,64,128]{2,1,0:T(8,128)(2,1)}, u32[]{:S(2)}, u32[]{:S(2)}) collective-permute-start(bf16[25,64,128]{2,1,0:T(8,128)(2,1)} %get-tuple-element.46), channel_id=1, source_target_pairs={{0,16},{16,32},{32,48},{48,64},{64,80},{80,96},{96,112},{112,128},... | collective-permute-start | bytes 1228808 | tf_op jit(solution)/shard_map/ppermute | solution.py:542
  216.9 29.4 %collective-permute-start.8 = (bf16[25,64,128]{2,1,0:T(8,128)(2,1)}, bf16[25,64,128]{2,1,0:T(8,128)(2,1)}, u32[]{:S(2)}, u32[]{:S(2)}) collective-permute-start(bf16[25,64,128]{2,1,0:T(8,128)(2,1)} %get-tuple-element.47), channel_id=1, source_target_pairs={{16,0},{32,16},{48,32},{64,48},{80,64},{96,80},{112,96},{128,112},... | collective-permute-start | bytes 1228808 | tf_op jit(solution)/shard_map/ppermute | solution.py:542
  220.2 8.9 %copy-start.16 = (s32[3]{0:T(128)S(1)}, s32[3]{0:T(128)}, u32[]{:S(2)}) copy-start(s32[3]{0:T(128)} %copy-done.14) | copy-start | bytes 40
  220.2 8.9 %copy-start.19 = (f32[4]{0:T(128)S(1)}, f32[4]{0:T(128)}, u32[]{:S(2)}) copy-start(f32[4]{0:T(128)} %wav.7) | copy-start | bytes 52
  224.9 24.2 %all-to-all-start.1 = ((f32[16,3,8,128]{3,2,1,0:T(8,128)}), f32[16,3,8,128]{3,2,1,0:T(8,128)}, u32[]{:S(2)}, u32[]{:S(2)}) async-start(f32[16,3,8,128]{3,2,1,0:T(8,128)} %broadcast_in_dim.25), calls=%async_computation.1 | async-start | bytes 393216 | tf_op jit(solution)/shard_map/all_to_all | solution.py:722
  229.1 1.3 copy-start.7
  250.1 3.8 %collective-permute-start.9 = (f32[3,8,128]{2,1,0:T(8,128)S(1)}, f32[3,8,128]{2,1,0:T(8,128)S(1)}, u32[]{:S(2)}, u32[]{:S(2)}) collective-permute-start(f32[3,8,128]{2,1,0:T(8,128)S(1)} %reduce_sum.9), channel_id=1, source_target_pairs={{0,16},{16,0},{32,48},{48,32},{64,80},{80,64},{96,112},{112,96},{1... | collective-permute-start | bytes 36872 | tf_op jit(solution)/shard_map/ppermute | solution.py:547

commit v3 on v2

--- a/solution.py
+++ b/solution.py
@@ -258,8 +258,8 @@
 
 
 def share_kernel(*refs):
-    rec, cur, prev, coef, perturb, table_low, table_high, traces = refs[:8]
-    gathered, found = refs[8:14], refs[14:20]
+    rec, cur, prev, coef, perturb, table, traces = refs[:7]
+    gathered, found = refs[7:13], refs[13:19]
     k, nx, depth, ny = perturb.shape
     lane = lax.broadcasted_iota(jnp.int32, (8, 128), 1)
     for ref in gathered + found:
@@ -298,12 +298,8 @@
         return c
 
     lax.fori_loop(0, rec[6, 1], beside, 0)
-    both = jnp.zeros((16, 128), F32)
-    for table in (table_low, table_high):
-        for term in range(3):
-            both = both + table[16 * term : 16 * term + 16, :].astype(F32)
     for h in range(2):
-        const = both[8 * h : 8 * h + 8]
+        const = table[8 * h : 8 * h + 8, :]
         reach = const[0:1] * t2[h] + const[1:2] * t1[h]
         for j in range(k):
             traces[h * k + j : h * k + j + 1, :] = (
@@ -449,6 +445,16 @@
         lax.fori_loop(0, depth // rows, piece, 0)
 
 
+def by_parity(odd, run):
+    @pl.when(odd == 0)
+    def _():
+        run(True)
+
+    @pl.when(odd == 1)
+    def _():
+        run(False)
+
+
 def sample_new(n, rec, nxt, traces, gathered, depth, k):
     offset = (n % 2) * k
 
@@ -462,15 +468,15 @@
 
 
 def gather_kernel(*refs):
-    rec = refs[0]
-    far = refs[1:7]
-    nxt, perturb, low, high, traces = refs[7:12]
-    near = refs[12:18]
-    acc, gathered, names, labels, arrived, landed = refs[18:]
+    src, rec = refs[:2]
+    far = refs[2:8]
+    nxt, perturb, away, beside, traces = refs[8:13]
+    near = refs[13:19]
+    acc, gathered, names, labels, arrived, landed = refs[19:]
     loads = [pltpu.make_async_copy(a, b, landed.at[i]) for i, (a, b) in enumerate(zip(far, near))]
     for load in reversed(loads):
         load.start()
-    part, acc_own, low_in, high_in, coef, incoming = near
+    part, acc_own, away_in, beside_in, coef, incoming = near
     k, nx, depth, ny = perturb.shape
     loads[5].wait()
     zb = (incoming.shape[1] - 16) // (CAP * k)
@@ -503,43 +509,58 @@
     lax.fori_loop(0, incoming.shape[0] * CAP, add, 0)
     for load in loads[:5]:
         load.wait()
-    finish_part(0, part, acc_own, low_in, high_in, coef, perturb, acc, nxt, low, high, None)
+
+    def run(even):
+        low_in, high_in = (away_in, beside_in) if even else (beside_in, away_in)
+        low, high = (away, beside) if even else (beside, away)
+        finish_part(0, part, acc_own, low_in, high_in, coef, perturb, acc, nxt, low, high, None)
+
+    by_parity(src[3], run)
     sample_new(0, rec, nxt, traces, gathered, depth, k)
 
 
-def finish_kernel(n, *refs):
-    if n == ITERS - 1:
-        rec = None
-    else:
+def finish_kernel(n, src, *refs):
+    last = n == ITERS - 1
+    rec = None
+    if not last:
         rec, refs = refs[0], refs[1:]
-    part, acc_own, low_in, high_in, coef, perturb = refs[:6]
+    part, acc_own, away_in, beside_in, coef, perturb = refs[:6]
     rest = refs[6:]
     k, nx, depth, ny = perturb.shape
-    if n == ITERS - 1:
+    out = nxt = away = beside = None
+    if last:
         out, acc = rest
-        finish_part(
-            n, part, acc_own, low_in, high_in, coef, perturb, acc, None, None, None, out
-        )
-        return
-    if n == 1:
-        table, nxt, low, high, traces, acc, gathered = rest
-        low[5 * F] = table[...]
-        high[5 * F] = table[...]
+    elif n == 1:
+        table, nxt, away, beside, traces, acc, gathered = rest
+        away[5 * F] = table[...]
+        beside[5 * F] = table[...]
     else:
-        nxt, low, high, traces, acc, gathered = rest
-    finish_part(n, part, acc_own, low_in, high_in, coef, perturb, acc, nxt, low, high, None)
-    sample_new(n, rec, nxt, traces, gathered, depth, k)
+        nxt, away, beside, traces, found, acc, gathered = rest
+        both = jnp.zeros((16, 128), F32)
+        for msg in (away_in, beside_in):
+            for term in range(3):
+                both = both + msg[5 * F, 16 * term : 16 * term + 16, :].astype(F32)
+        found[...] = both
+
+    def run(even):
+        low_in, high_in = (away_in, beside_in) if even else (beside_in, away_in)
+        low, high = (away, beside) if even else (beside, away)
+        finish_part(n, part, acc_own, low_in, high_in, coef, perturb, acc, nxt, low, high, out)
+
+    by_parity(src[3], run)
+    if not last:
+        sample_new(n, rec, nxt, traces, gathered, depth, k)
 
 
 def cost(flops, moved):
     return pl.CostEstimate(flops=flops, bytes_accessed=moved, transcendentals=0)
 
 
-def exchange(low, high):
+def exchange(away, beside):
     count = lax.axis_size("tile")
-    forward = [(i, i + 1) for i in range(count - 1)]
-    backward = [(b, a) for a, b in forward]
-    return lax.ppermute(high, "tile", forward), lax.ppermute(low, "tile", backward)
+    pairs = [(i, i + 1) for i in range(1, count - 1, 2)]
+    there = lax.ppermute(away, "tile", pairs + [(b, a) for a, b in pairs])
+    return there, swap(beside)
 
 
 def swap(value):
@@ -574,6 +595,7 @@
     depth, nx, ny = background_now.shape
     zb = pieces.shape[2]
 
+    odd = place % 2
     packed = pack(pieces, piece_target[:, 0], piece_block, tiles)
     incoming = lax.all_to_all(packed, "tile", 0, 0, tiled=True)
 
@@ -583,11 +605,12 @@
         born = jnp.stack([born_now[:, :, p, :] for p in planes], axis=1)
         return jnp.concatenate([jnp.stack(rows), born.reshape(k * 4, depth, ny)])
 
-    low_in, high_in = exchange(face((0, 1, 2, 3)), face((7, 6, 5, 4)))
+    low, high = face((0, 1, 2, 3)), face((7, 6, 5, 4))
+    low_in, high_in = exchange(jnp.where(odd == 0, low, high), jnp.where(odd == 0, high, low))
 
     where = jnp.stack([place * nx, jnp.int32(nx), jnp.int32(depth)]).astype(jnp.int32)
     rec = list_receivers(receiver_z, receiver_x, receiver_y, where)
-    src = jnp.stack([source_cell[0], source_cell[1] - place * nx, source_cell[2]])
+    src = jnp.stack([source_cell[0], source_cell[1] - place * nx, source_cell[2], odd])
 
     def planes_first(background, born):
         return jnp.concatenate(
@@ -630,7 +653,7 @@
         )(*scalars, *arrays)
 
     records = []
-    perturb = table = tables = None
+    perturb = table = found = None
     for n in range(ITERS):
         name = "own%d" % (n + 1)
         start = (wavelet, src)
@@ -652,7 +675,7 @@
                 (jax.ShapeDtypeStruct((8, 128), F32),),
                 [small] * 6 + [pair] * 6,
                 (rec,),
-                (cur, prev, coef, perturb) + tables,
+                (cur, prev, coef, perturb, found),
                 20,
             )
             part, acc = call(
@@ -660,7 +683,13 @@
             )
         else:
             part, acc = call(
-                functools.partial(own_kernel, n), name, (state, field), work, start, arrays, 80
+                functools.partial(own_kernel, n),
+                name,
+                (state, field),
+                work,
+                start,
+                arrays,
+                80,
             )
         arrays = (part, acc, low_in, high_in, coef)
         name = "finish%d" % (n + 1)
@@ -679,7 +708,7 @@
                     pltpu.SemaphoreType.DMA,
                     pltpu.SemaphoreType.DMA((6,)),
                 ],
-                (rec,),
+                (src, rec),
                 arrays + (incoming,),
                 20,
                 pl.BlockSpec(memory_space=pltpu.HBM),
@@ -691,31 +720,31 @@
                 name,
                 (jax.ShapeDtypeStruct((k, depth * nx, ny), F32),),
                 [keep],
-                (),
+                (src,),
                 arrays + (perturb,),
                 20,
             )
             break
         else:
             face_type = wider if n == 1 else faces
-            nxt, low, high, traces = call(
+            more = () if n == 1 else (jax.ShapeDtypeStruct((16, 128), F32),)
+            nxt, low, high, traces, *more = call(
                 functools.partial(finish_kernel, n),
                 name,
-                (state, face_type, face_type, traced),
+                (state, face_type, face_type, traced) + more,
                 [keep, small],
-                (rec,),
+                (src, rec),
                 arrays + (perturb,) + ((table,) if n == 1 else ()),
                 20,
             )
+            if n == 2:
+                (found,) = more
         records.append(traces)
         low_in, high_in = exchange(low, high)
-        if n == 1:
-            tables = (low_in[5 * F], high_in[5 * F])
         prev, cur = cur, nxt
 
     early = jnp.stack([records[0] + records[1], records[2]])
     early = early + swap(early)
-    odd = place % 2
     half = jnp.where(odd == 0, early[0], early[1])
     message = jnp.concatenate([half, mine[None]])
     groups = [list(range(c, tiles, 2)) for c in range(2)]

time: 256 us -> 249 us (0.973); the launches traced: 255 us -> 244 us
  starting transfers between devices: 56.6 us -> 65.3 us
  local copies, waits for them, and re-layouts: 24 us -> 16.1 us
  Pallas kernels: 57.3 us -> 51.9 us
  waiting for transfers between devices: 110 us -> 105 us
    ppermute x8 -> x4, waiting for transfers between devices: 110 us -> 97.8 us  [exchange(): there = lax.ppermute(away, 'tile', pairs + [(b, a) for a, b in pairs])]
    ppermute x2 -> x6, starting transfers between devices: 4.85 us -> 13 us  [swap(): return lax.ppermute(value, 'tile', [(i, i ^ 1) for i in range(count)])]
    all_to_all x1, waiting for transfers between devices: 0.01 us -> 6.28 us  [local(): lax.all_to_all(jnp.broadcast_to(message[None], (tiles // 2,) + message.sh...]
    pallas_call x9, Pallas kernels: 47.8 us -> 42.5 us  [call(): pl.pallas_call(kernel, out_shape=out_shape, in_specs=[sspec()] * len(scal...]
    unnamed x77 -> x79, local copies, waits for them, and re-layouts: 17.9 us -> 12.9 us
    all_to_all x1, starting transfers between devices: 4.18 us -> 8.53 us  [local(): lax.all_to_all(jnp.broadcast_to(message[None], (tiles // 2,) + message.sh...]
    ppermute x8 -> x4, starting transfers between devices: 28.2 us -> 24.4 us  [exchange(): there = lax.ppermute(away, 'tile', pairs + [(b, a) for a, b in pairs])]
  transfers between devices with their start and end apart: 12 -> 12, of which waited for: 7 -> 5; matrix products, arithmetic and copies ran while one was open for 5% -> 2% of each run, Pallas kernels for 15% -> 15%
where the time goes in v3:
time: 249 us; the launch traced here: 244 us
  waiting for transfers between devices  105 us (42%)
  starting transfers between devices  65.3 us (26%)
  Pallas kernels  51.9 us (21%)
  local copies, waits for them, and re-layouts  16.1 us (6%)
  other arithmetic  3.88 us (2%)
    ppermute x4, waiting for transfers between devices, exchange(): there = lax.ppermute(away, 'tile', pairs + [(b, a) for a, b in pairs])  97.8 us
    pallas_call x9, Pallas kernels, call(): pl.pallas_call(kernel, out_shape=out_shape, in_specs=[sspec()] * len(scal...  42.5 us
    ppermute x4, starting transfers between devices, exchange(): there = lax.ppermute(away, 'tile', pairs + [(b, a) for a, b in pairs])  24.4 us
    all_to_all x1, starting transfers between devices, local(): incoming = lax.all_to_all(packed, 'tile', 0, 0, tiled=True)  19.4 us
    ppermute x6, starting transfers between devices, swap(): return lax.ppermute(value, 'tile', [(i, i ^ 1) for i in range(count)])  13 us
    unnamed x79, local copies, waits for them, and re-layouts  12.9 us
    all_to_all x1, starting transfers between devices, local(): lax.all_to_all(jnp.broadcast_to(message[None], (tiles // 2,) + message.sh...  8.53 us
    pallas_call x1, Pallas kernels, list_receivers(): pl.pallas_call(list_kernel, out_shape=jax.ShapeDtypeStruct((8, n), jnp.in...  6.43 us
  transfers between devices with their start and end apart: 12, of which 5 were waited for; matrix products, arithmetic and copies ran while one was open for 2% of the time, Pallas kernels for 15%

profile of v3, /device:TPU:1, one launch (start us, length us, event | category | flops | bytes accessed | tf_op | source)
XLA Modules:
  0.0 244.1 jit_solution(3267482943261762967)
XLA Ops:
  0.6 1.2 copy-done.10
  1.9 0.7 copy-done.20
  2.5 0.7 copy-done.21
  3.2 3.0 %pack.1 = bf16[32,272,128]{2,1,0:T(8,128)(2,1)} custom-call(s32[32]{0:T(128)S(1)} %bitcast.112, s32[32]{0:T(128)S(1)} %copy-done.21, bf16[4,32,32,128]{3,2,1,0:T(8,128)(2,1)S(1)} %copy-done.10), custom_call_target="tpu_custom_call" | custom-call | tf_op jit(solution)/shard_map/pack/pallas_call | solution.py:85
  6.1 19.4 %all-to-all-start = ((bf16[32,272,128]{2,1,0:T(8,128)(2,1)}), bf16[32,272,128]{2,1,0:T(8,128)(2,1)}, u32[]{:S(2)}, u32[]{:S(2)}) async-start(bf16[32,272,128]{2,1,0:T(8,128)(2,1)} %pack.1), calls=%async_computation | async-start | bytes 4456448 | tf_op jit(solution)/shard_map/all_to_all | solution.py:600
  25.5 0.0 copy-start.22
  25.6 0.1 copy.80
  25.6 0.1 copy.91
  25.7 0.9 copy-done.22
  26.6 1.2 fusion.7
  28.1 0.0 copy-start.31
  28.2 0.0 copy-start.29
  28.2 0.1 constant_dynamic-update-slice_fusion
  28.3 0.8 broadcast_select_fusion
  29.1 2.2 collective-permute-start.1
  31.3 7.3 %collective-permute-start = (bf16[21,64,128]{2,1,0:T(8,128)(2,1)S(1)}, bf16[21,64,128]{2,1,0:T(8,128)(2,1)}, u32[]{:S(2)}, u32[]{:S(2)}) collective-permute-start(bf16[21,64,128]{2,1,0:T(8,128)(2,1)S(1)} %get-tuple-element.53), channel_id=1, source_target_pairs={{16,32},{48,64},{80,96},{112,128},{144,160},{176,192},{208,224},{2... | collective-permute-start | bytes 1032200 | tf_op jit(solution)/shard_map/ppermute | solution.py:562
  38.6 0.6 fusion.9
  39.9 0.1 pad_add_fusion.1.where
  40.0 0.1 convert_multiply_fusion
  40.1 0.1 maximum_bitcast_fusion.coef.refs_6_.refs_3_.refs_5_.refs_4_
  40.2 0.0 copy-start
  40.2 0.0 copy-start.26
  40.2 0.1 convert_bitcast_fusion.1
  40.4 1.3 copy-done.26
  41.6 0.1 convert_bitcast_fusion
  41.8 1.3 pad_add_fusion.src.refs_0_
  43.0 0.1 copy.82
  43.1 6.4 %receivers.1.refs_1_.refs_0_ = s32[8,256]{1,0:T(8,128)S(1)} custom-call(s32[256]{0:T(256)S(1)} %copy-done.17, s32[256]{0:T(256)S(1)} %copy-done.18, s32[256]{0:T(256)S(1)} %copy-done.19, s32[3]{0:T(128)S(1)} %pad_add_fusion.1.where), custom_call_target="tpu_custom_call" | custom-call | tf_op jit(solution)/shard_map/receivers/pallas_call | solution.py:125
  49.6 0.6 copy-done.11
  50.2 0.1 pad_maximum_fusion.1.prev
  50.3 0.8 copy-done.24
  51.1 0.1 pad_maximum_fusion.cur.refs_2_
  51.2 0.8 copy-done.9
  52.0 6.0 %own1.1 = (f32[5,8,64,128]{3,2,1,0:T(8,128)S(1)}, f32[8,64,128]{2,1,0:T(8,128)S(1)}) custom-call(f32[4]{0:T(128)S(1)} %copy-done.16, s32[4]{0:T(128)S(1)} %pad_add_fusion.src.refs_0_, f32[5,8,64,128]{3,2,1,0:T(8,128)S(1)} %pad_maximum_fusion.cur.refs_2_, f32[5,8,64,128]{3,2,1,0:T(8,128)S(1)} %pad_maximum_fusion.1.prev, ...), custom_call_target="tpu_custom_call" | custom-call | flops 26214400 | bytes 5242880 | tf_op jit(solution)/shard_map/own1/pallas_call | solution.py:644
  58.0 1.1 copy-done.8
  59.1 0.7 copy-done.13
  59.8 82.3 %collective-permute-done.refs_4_ = bf16[21,64,128]{2,1,0:T(8,128)(2,1)} collective-permute-done((bf16[21,64,128]{2,1,0:T(8,128)(2,1)S(1)}, bf16[21,64,128]{2,1,0:T(8,128)(2,1)}, u32[]{:S(2)}, u32[]{:S(2)}) %collective-permute-start) | collective-permute-done | bytes 344096 | tf_op jit(solution)/shard_map/ppermute | solution.py:562
  142.2 8.1 %finish1.1 = (f32[5,8,64,128]{3,2,1,0:T(8,128)}, f32[4,8,64,128]{3,2,1,0:T(8,128)}, bf16[25,64,128]{2,1,0:T(8,128)(2,1)}, bf16[25,64,128]{2,1,0:T(8,128)(2,1)}, f32[2,8,128]{2,1,0:T(8,128)}) custom-call(s32[4]{0:T(128)} %copy-done.14, s32[8,256]{1,0:T(8,128)} %copy-done.11, f32[5,8,64,128]{3,2,1,0:T(8,128)} %copy-done.8, f32[8,64,128]{2,1,0:T(8,128)} %copy-done.13, ...), custom_call_target="tpu_custom_call" | custom-call | flops 6553600 | bytes 5242880 | tf_op jit(solution)/shard_map/finish1/pallas_call | solution.py:644
  150.3 4.5 %collective-permute-start.2 = (bf16[25,64,128]{2,1,0:T(8,128)(2,1)}, bf16[25,64,128]{2,1,0:T(8,128)(2,1)S(1)}, u32[]{:S(2)}, u32[]{:S(2)}) collective-permute-start(bf16[25,64,128]{2,1,0:T(8,128)(2,1)} %get-tuple-element.34), channel_id=1, source_target_pairs={{16,32},{48,64},{80,96},{112,128},{144,160},{176,192},{208,224},{2... | collective-permute-start | bytes 1228808 | tf_op jit(solution)/shard_map/ppermute | solution.py:562
  154.8 1.9 collective-permute-start.3
  156.8 1.2 copy-done.2
  158.0 1.3 copy-done.4
  159.3 6.3 %own2.1 = (f32[5,8,64,128]{3,2,1,0:T(8,128)S(1)}, f32[8,64,128]{2,1,0:T(8,128)S(1)}, bf16[64,128]{1,0:T(8,128)(2,1)S(1)}) custom-call(f32[4]{0:T(128)S(1)} %copy-done.16, s32[4]{0:T(128)S(1)} %copy-done.15, s32[8,256]{1,0:T(8,128)S(1)} %copy-done.12, f32[5,8,64,128]{3,2,1,0:T(8,128)S(1)} %copy-done.4, f32[5,8,64,128]{3,2,1,0:T(8,128)S(1)} %pad_maximum_fusion.cur.refs_2_, ...), custom_call_target="tpu_custom_call" | custom-call | flops 26214400 | bytes 5242880 | tf_op jit(solution)/shard_map/own2/pallas_call | solution.py:644
  165.7 5.5 %collective-permute-done.2.refs_3_ = bf16[25,64,128]{2,1,0:T(8,128)(2,1)S(1)} collective-permute-done((bf16[25,64,128]{2,1,0:T(8,128)(2,1)}, bf16[25,64,128]{2,1,0:T(8,128)(2,1)S(1)}, u32[]{:S(2)}, u32[]{:S(2)}) %collective-permute-start.2) | collective-permute-done | bytes 409632 | tf_op jit(solution)/shard_map/ppermute | solution.py:562
  171.2 2.0 finish2.1
  173.1 3.6 %collective-permute-start.4 = (bf16[26,64,128]{2,1,0:T(8,128)(2,1)S(1)}, bf16[26,64,128]{2,1,0:T(8,128)(2,1)S(1)}, u32[]{:S(2)}, u32[]{:S(2)}) collective-permute-start(bf16[26,64,128]{2,1,0:T(8,128)(2,1)S(1)} %get-tuple-element.41), channel_id=1, source_target_pairs={{16,32},{48,64},{80,96},{112,128},{144,160},{176,192},{208,224},{2... | collective-permute-start | bytes 1277960 | tf_op jit(solution)/shard_map/ppermute | solution.py:562
  176.7 1.9 collective-permute-start.5
  178.7 5.9 %own3.1 = (f32[5,8,64,128]{3,2,1,0:T(8,128)S(1)}, f32[8,64,128]{2,1,0:T(8,128)S(1)}) custom-call(f32[4]{0:T(128)S(1)} %copy-done.16, s32[4]{0:T(128)S(1)} %copy-done.15, f32[5,8,64,128]{3,2,1,0:T(8,128)S(1)} %get-tuple-element.38.cur.refs_2_.prev, f32[5,8,64,128]{3,2,1,0:T(8,128)S(1)} %copy-done.5, f32[4,8,64,128]{3,2,1,0:T(8,128)S(1)} %copy-done.1, ...), custom_call_target="tpu_custom_call" | custom-call | flops 26214400 | bytes 5242880 | tf_op jit(solution)/shard_map/own3/pallas_call | solution.py:644
  184.6 10.0 %collective-permute-done.4.refs_3_ = bf16[26,64,128]{2,1,0:T(8,128)(2,1)S(1)} collective-permute-done((bf16[26,64,128]{2,1,0:T(8,128)(2,1)S(1)}, bf16[26,64,128]{2,1,0:T(8,128)(2,1)S(1)}, u32[]{:S(2)}, u32[]{:S(2)}) %collective-permute-start.4) | collective-permute-done | bytes 426016 | tf_op jit(solution)/shard_map/ppermute | solution.py:562
  194.6 2.9 %finish3.1 = (f32[5,8,64,128]{3,2,1,0:T(8,128)S(1)}, bf16[25,64,128]{2,1,0:T(8,128)(2,1)}, bf16[25,64,128]{2,1,0:T(8,128)(2,1)}, f32[2,8,128]{2,1,0:T(8,128)S(1)}, f32[16,128]{1,0:T(8,128)S(1)}) custom-call(s32[4]{0:T(128)S(1)} %copy-done.15, s32[8,256]{1,0:T(8,128)S(1)} %copy-done.12, f32[5,8,64,128]{3,2,1,0:T(8,128)S(1)} %get-tuple-element.39.refs_1_, ...), custom_call_target="tpu_custom_call" | custom-call | flops 6553600 | bytes 5242880 | tf_op jit(solution)/shard_map/finish3/pallas_call | solution.py:644
  197.4 1.9 collective-permute-start.6
  199.4 9.0 %collective-permute-start.7 = (bf16[25,64,128]{2,1,0:T(8,128)(2,1)}, bf16[25,64,128]{2,1,0:T(8,128)(2,1)}, u32[]{:S(2)}, u32[]{:S(2)}) collective-permute-start(bf16[25,64,128]{2,1,0:T(8,128)(2,1)} %get-tuple-element.48), channel_id=1, source_target_pairs={{16,32},{48,64},{80,96},{112,128},{144,160},{176,192},{208,224},{2... | collective-permute-start | bytes 1228808 | tf_op jit(solution)/shard_map/ppermute | solution.py:562
  208.4 1.9 collective-permute-start.8
  210.3 2.5 %share.1 = f32[8,128]{1,0:T(8,128)S(1)} custom-call(s32[8,256]{1,0:T(8,128)S(1)} %copy-done.12, f32[5,8,64,128]{3,2,1,0:T(8,128)S(1)} %get-tuple-element.44.refs_1_.cur, f32[5,8,64,128]{3,2,1,0:T(8,128)S(1)} %get-tuple-element.38.cur.refs_2_.prev, f32[4,8,64,128]{3,2,1,0:T(8,128)S(1)} %copy-done.1, f32[4,8,64,128]{3,2,1,0:T(8,128)S(1)} %copy-done.3, ...), custom_call_target="tpu_custom_call" | custom-call | flops 6553600 | bytes 5242880 | tf_op jit(solution)/shard_map/share/pallas_call | solution.py:644
  212.9 0.7 broadcast_in_dim.25
  213.6 8.5 %all-to-all-start.1 = ((f32[16,3,8,128]{3,2,1,0:T(8,128)}), f32[16,3,8,128]{3,2,1,0:T(8,128)}, u32[]{:S(2)}, u32[]{:S(2)}) async-start(f32[16,3,8,128]{3,2,1,0:T(8,128)} %broadcast_in_dim.25), calls=%async_computation.1 | async-start | bytes 393216 | tf_op jit(solution)/shard_map/all_to_all | solution.py:751
  222.1 1.3 copy-done.7
  223.4 5.8 %own4.1 = (f32[5,8,64,128]{3,2,1,0:T(8,128)S(1)}, f32[8,64,128]{2,1,0:T(8,128)S(1)}) custom-call(f32[4]{0:T(128)S(1)} %copy-done.16, s32[4]{0:T(128)S(1)} %copy-done.15, f32[5,8,64,128]{3,2,1,0:T(8,128)S(1)} %copy-done.7, f32[5,8,64,128]{3,2,1,0:T(8,128)S(1)} %get-tuple-element.38.cur.refs_2_.prev, f32[4,8,64,128]{3,2,1,0:T(8,128)S(1)} %copy-done.1, ...), custom_call_target="tpu_custom_call" | custom-call | flops 26214400000 | bytes 5242880 | tf_op jit(solution)/shard_map/own4/pallas_call | solution.py:644
  229.3 3.0 %finish4.1 = f32[4,512,128]{2,1,0:T(8,128)} custom-call(s32[4]{0:T(128)S(1)} %copy-done.15, f32[5,8,64,128]{3,2,1,0:T(8,128)S(1)} %get-tuple-element.46.refs_0_, f32[8,64,128]{2,1,0:T(8,128)S(1)} %get-tuple-element.47.refs_1_, bf16[25,64,128]{2,1,0:T(8,128)(2,1)} %collective-permute-done.7.refs_2_, bf16[25,64,128]{2,1,0:T(8,128)(2,1)} %collective-permute-done.8.refs_3_, ...), custom_call_target="tpu_custom_call" | custom-call | flops 6553600 | bytes 5242880 | tf_op jit(solution)/shard_map/finish4/pallas_call | solution.py:644
  232.3 6.3 %all-to-all-done.1 = f32[16,3,8,128]{3,2,1,0:T(8,128)} async-done(((f32[16,3,8,128]{3,2,1,0:T(8,128)}), f32[16,3,8,128]{3,2,1,0:T(8,128)}, u32[]{:S(2)}, u32[]{:S(2)}) %all-to-all-start.1) | async-done | bytes 196640 | tf_op jit(solution)/shard_map/all_to_all | solution.py:751
  238.5 0.9 reduce_sum.9
  239.5 3.1 %collective-permute-start.9 = (f32[3,8,128]{2,1,0:T(8,128)S(1)}, f32[3,8,128]{2,1,0:T(8,128)S(1)}, u32[]{:S(2)}, u32[]{:S(2)}) collective-permute-start(f32[3,8,128]{2,1,0:T(8,128)S(1)} %reduce_sum.9), channel_id=1, source_target_pairs={{0,16},{16,0},{32,48},{48,32},{64,80},{80,64},{96,112},{112,96},{1... | collective-permute-start | bytes 36872 | tf_op jit(solution)/shard_map/ppermute | solution.py:568
  242.6 0.8 collective-permute-done.9
  243.4 0.6 reshape.174
  (82 shorter events, 0.5 us)
Async XLA Ops:
  0.6 1.2 copy-start.10
  1.9 0.7 copy-start.20
  2.5 0.7 copy-start.21
  6.1 19.4 %copy-start.25 = (f32[64,8,128]{2,1,0:T(8,128)S(1)}, f32[64,8,128]{2,1,0:T(8,128)}, u32[]{:S(2)}) copy-start(f32[64,8,128]{2,1,0:T(8,128)} %param.16) | copy-start | bytes 786436
  6.1 136.0 %all-to-all-start = ((bf16[32,272,128]{2,1,0:T(8,128)(2,1)}), bf16[32,272,128]{2,1,0:T(8,128)(2,1)}, u32[]{:S(2)}, u32[]{:S(2)}) async-start(bf16[32,272,128]{2,1,0:T(8,128)(2,1)} %pack.1), calls=%async_computation | async-start | bytes 4456448 | tf_op jit(solution)/shard_map/all_to_all | solution.py:600
  25.5 1.0 copy-start.22
  25.7 2.4 copy-start.23
  28.1 10.5 %copy-start.31 = (s32[3]{0:T(128)S(1)}, s32[3]{0:T(128)}, u32[]{:S(2)}) copy-start(s32[3]{0:T(128)} %param.25) | copy-start | bytes 40
  28.2 11.8 %copy-start.29 = (bf16[64,8,128]{2,1,0:T(8,128)(2,1)S(1)}, bf16[64,8,128]{2,1,0:T(8,128)(2,1)}, u32[]{:S(2)}) copy-start(bf16[64,8,128]{2,1,0:T(8,128)(2,1)} %param.17) | copy-start | bytes 393220
  28.2 11.8 %copy-start.27 = (bf16[3,64,8,128]{3,2,1,0:T(8,128)(2,1)S(1)}, bf16[3,64,8,128]{3,2,1,0:T(8,128)(2,1)}, u32[]{:S(2)}) copy-start(bf16[3,64,8,128]{3,2,1,0:T(8,128)(2,1)} %param.18) | copy-start | bytes 1179652
  29.1 30.7 %collective-permute-start.1 = (bf16[21,64,128]{2,1,0:T(8,128)(2,1)}, bf16[21,64,128]{2,1,0:T(8,128)(2,1)}, u32[]{:S(2)}, u32[]{:S(2)}) collective-permute-start(bf16[21,64,128]{2,1,0:T(8,128)(2,1)} %get-tuple-element.52), channel_id=1, source_target_pairs={{0,16},{16,0},{32,48},{48,32},{64,80},{80,64},{96,112},{112,96},{1... | collective-permute-start | bytes 1032200 | tf_op jit(solution)/shard_map/ppermute | solution.py:568
  31.3 110.9 %collective-permute-start = (bf16[21,64,128]{2,1,0:T(8,128)(2,1)S(1)}, bf16[21,64,128]{2,1,0:T(8,128)(2,1)}, u32[]{:S(2)}, u32[]{:S(2)}) collective-permute-start(bf16[21,64,128]{2,1,0:T(8,128)(2,1)S(1)} %get-tuple-element.53), channel_id=1, source_target_pairs={{16,32},{48,64},{80,96},{112,128},{144,160},{176,192},{208,224},{2... | collective-permute-start | bytes 1032200 | tf_op jit(solution)/shard_map/ppermute | solution.py:562
  40.2 11.0 %copy-start = (f32[4,8,64,128]{3,2,1,0:T(8,128)}, f32[4,8,64,128]{3,2,1,0:T(8,128)S(1)}, u32[]{:S(2)}) copy-start(f32[4,8,64,128]{3,2,1,0:T(8,128)S(1)} %maximum_bitcast_fusion.coef.refs_6_.refs_3_.refs_5_.refs_4_) | copy-start | bytes 3145732
  40.2 1.4 copy-start.26
  40.2 2.8 %copy-start.28 = (f32[64,8,128]{2,1,0:T(8,128)S(1)}, f32[64,8,128]{2,1,0:T(8,128)}, u32[]{:S(2)}) copy-start(f32[64,8,128]{2,1,0:T(8,128)} %param.15) | copy-start | bytes 786436
  41.6 1.5 copy-start.17
  41.6 1.5 copy-start.18
  41.6 1.5 copy-start.19
  43.0 8.2 %copy-start.14 = (s32[4]{0:T(128)}, s32[4]{0:T(128)S(1)}, u32[]{:S(2)}) copy-start(s32[4]{0:T(128)S(1)} %pad_add_fusion.src.refs_0_) | copy-start | bytes 52
  49.6 0.6 copy-start.11
  50.2 0.9 copy-start.24
  51.1 0.9 copy-start.9
  51.1 0.9 copy-start.16
  58.0 1.1 copy-start.8
  59.1 0.7 copy-start.13
  142.2 14.6 %copy-start.1 = (f32[4,8,64,128]{3,2,1,0:T(8,128)S(1)}, f32[4,8,64,128]{3,2,1,0:T(8,128)}, u32[]{:S(2)}) copy-start(f32[4,8,64,128]{3,2,1,0:T(8,128)} %copy-done) | copy-start | bytes 3145732
  142.2 14.6 %copy-start.12 = (s32[8,256]{1,0:T(8,128)S(1)}, s32[8,256]{1,0:T(8,128)}, u32[]{:S(2)}) copy-start(s32[8,256]{1,0:T(8,128)} %copy-done.11) | copy-start | bytes 24580
  142.2 14.6 %copy-start.15 = (s32[4]{0:T(128)S(1)}, s32[4]{0:T(128)}, u32[]{:S(2)}) copy-start(s32[4]{0:T(128)} %copy-done.14) | copy-start | bytes 52
  150.3 20.8 %collective-permute-start.2 = (bf16[25,64,128]{2,1,0:T(8,128)(2,1)}, bf16[25,64,128]{2,1,0:T(8,128)(2,1)S(1)}, u32[]{:S(2)}, u32[]{:S(2)}) collective-permute-start(bf16[25,64,128]{2,1,0:T(8,128)(2,1)} %get-tuple-element.34), channel_id=1, source_target_pairs={{16,32},{48,64},{80,96},{112,128},{144,160},{176,192},{208,224},{2... | collective-permute-start | bytes 1228808 | tf_op jit(solution)/shard_map/ppermute | solution.py:562
  154.8 16.3 %collective-permute-start.3 = (bf16[25,64,128]{2,1,0:T(8,128)(2,1)}, bf16[25,64,128]{2,1,0:T(8,128)(2,1)S(1)}, u32[]{:S(2)}, u32[]{:S(2)}) collective-permute-start(bf16[25,64,128]{2,1,0:T(8,128)(2,1)} %get-tuple-element.35), channel_id=1, source_target_pairs={{0,16},{16,0},{32,48},{48,32},{64,80},{80,64},{96,112},{112,96},{1... | collective-permute-start | bytes 1228808 | tf_op jit(solution)/shard_map/ppermute | solution.py:568
  156.8 1.2 copy-start.2
  158.0 1.3 copy-start.4
  159.3 11.8 %copy-start.3 = (f32[4,8,64,128]{3,2,1,0:T(8,128)S(1)}, f32[4,8,64,128]{3,2,1,0:T(8,128)}, u32[]{:S(2)}) copy-start(f32[4,8,64,128]{3,2,1,0:T(8,128)} %get-tuple-element.31.refs_5_.refs_6_.refs_4_) | copy-start | bytes 3145732
  171.2 7.5 %copy-start.5 = (f32[5,8,64,128]{3,2,1,0:T(8,128)S(1)}, f32[5,8,64,128]{3,2,1,0:T(8,128)}, u32[]{:S(2)}) copy-start(f32[5,8,64,128]{3,2,1,0:T(8,128)} %get-tuple-element.30.refs_1_.prev) | copy-start | bytes 3932164
  173.1 21.4 %collective-permute-start.4 = (bf16[26,64,128]{2,1,0:T(8,128)(2,1)S(1)}, bf16[26,64,128]{2,1,0:T(8,128)(2,1)S(1)}, u32[]{:S(2)}, u32[]{:S(2)}) collective-permute-start(bf16[26,64,128]{2,1,0:T(8,128)(2,1)S(1)} %get-tuple-element.41), channel_id=1, source_target_pairs={{16,32},{48,64},{80,96},{112,128},{144,160},{176,192},{208,224},{2... | collective-permute-start | bytes 1277960 | tf_op jit(solution)/shard_map/ppermute | solution.py:562
  176.7 17.8 %collective-permute-start.5 = (bf16[26,64,128]{2,1,0:T(8,128)(2,1)S(1)}, bf16[26,64,128]{2,1,0:T(8,128)(2,1)S(1)}, u32[]{:S(2)}, u32[]{:S(2)}) collective-permute-start(bf16[26,64,128]{2,1,0:T(8,128)(2,1)S(1)} %get-tuple-element.42), channel_id=1, source_target_pairs={{0,16},{16,0},{32,48},{48,32},{64,80},{80,64},{96,112},{112,96},{1... | collective-permute-start | bytes 1277960 | tf_op jit(solution)/shard_map/ppermute | solution.py:568
  178.7 5.9 %copy-start.30 = (f32[2,8,128]{2,1,0:T(8,128)S(1)}, f32[2,8,128]{2,1,0:T(8,128)}, u32[]{:S(2)}) copy-start(f32[2,8,128]{2,1,0:T(8,128)} %get-tuple-element.29) | copy-start | bytes 24580
  197.4 15.4 %copy-start.6 = (f32[5,8,64,128]{3,2,1,0:T(8,128)}, f32[5,8,64,128]{3,2,1,0:T(8,128)S(1)}, u32[]{:S(2)}) copy-start(f32[5,8,64,128]{3,2,1,0:T(8,128)S(1)} %get-tuple-element.44.refs_1_.cur) | copy-start | bytes 3932164
  197.4 15.4 %collective-permute-start.6 = (f32[2,2,8,128]{3,2,1,0:T(8,128)S(1)}, f32[2,2,8,128]{3,2,1,0:T(8,128)S(1)}, u32[]{:S(2)}, u32[]{:S(2)}) collective-permute-start(f32[2,2,8,128]{3,2,1,0:T(8,128)S(1)} %pad_maximum_fusion.4), channel_id=1, source_target_pairs={{0,16},{16,0},{32,48},{48,32},{64,80},{80,64},{96,112},{112,96},{1... | collective-permute-start | bytes 49160 | tf_op jit(solution)/shard_map/ppermute | solution.py:568
  199.4 29.9 %collective-permute-start.7 = (bf16[25,64,128]{2,1,0:T(8,128)(2,1)}, bf16[25,64,128]{2,1,0:T(8,128)(2,1)}, u32[]{:S(2)}, u32[]{:S(2)}) collective-permute-start(bf16[25,64,128]{2,1,0:T(8,128)(2,1)} %get-tuple-element.48), channel_id=1, source_target_pairs={{16,32},{48,64},{80,96},{112,128},{144,160},{176,192},{208,224},{2... | collective-permute-start | bytes 1228808 | tf_op jit(solution)/shard_map/ppermute | solution.py:562
  208.4 20.9 %collective-permute-start.8 = (bf16[25,64,128]{2,1,0:T(8,128)(2,1)}, bf16[25,64,128]{2,1,0:T(8,128)(2,1)}, u32[]{:S(2)}, u32[]{:S(2)}) collective-permute-start(bf16[25,64,128]{2,1,0:T(8,128)(2,1)} %get-tuple-element.49), channel_id=1, source_target_pairs={{0,16},{16,0},{32,48},{48,32},{64,80},{80,64},{96,112},{112,96},{1... | collective-permute-start | bytes 1228808 | tf_op jit(solution)/shard_map/ppermute | solution.py:568
  213.6 25.0 %all-to-all-start.1 = ((f32[16,3,8,128]{3,2,1,0:T(8,128)}), f32[16,3,8,128]{3,2,1,0:T(8,128)}, u32[]{:S(2)}, u32[]{:S(2)}) async-start(f32[16,3,8,128]{3,2,1,0:T(8,128)} %broadcast_in_dim.25), calls=%async_computation.1 | async-start | bytes 393216 | tf_op jit(solution)/shard_map/all_to_all | solution.py:751
  222.1 1.3 copy-start.7
  239.5 3.9 %collective-permute-start.9 = (f32[3,8,128]{2,1,0:T(8,128)S(1)}, f32[3,8,128]{2,1,0:T(8,128)S(1)}, u32[]{:S(2)}, u32[]{:S(2)}) collective-permute-start(f32[3,8,128]{2,1,0:T(8,128)S(1)} %reduce_sum.9), channel_id=1, source_target_pairs={{0,16},{16,0},{32,48},{48,32},{64,80},{80,64},{96,112},{112,96},{1... | collective-permute-start | bytes 36872 | tf_op jit(solution)/shard_map/ppermute | solution.py:568

commit v4 on v3

--- a/solution.py
+++ b/solution.py
@@ -681,6 +681,24 @@
             part, acc = call(
                 functools.partial(own_kernel, n), name, (state, field), work, start, arrays, 80000
             )
+            message = jnp.concatenate([records[0] + records[1], records[2][:, :k].reshape(1, 8, 128), mine[None]])
+            groups = [list(range(c, tiles, 2)) for c in range(2)]
+            copies = lax.all_to_all(
+                jnp.broadcast_to(message[None], (tiles // 2,) + message.shape),
+                "tile",
+                0,
+                0,
+                axis_index_groups=groups,
+                tiled=True,
+            )
+            copies, part, acc = lax.optimization_barrier((copies, part, acc))
+            total = jnp.sum(copies, axis=0)
+            total = total + swap(total)
+            first_two = total[:2].reshape(2, 2, k, 128)
+            rest = total[2:].reshape(2, 2, k, 128).transpose(1, 0, 2, 3)
+            steps = jnp.concatenate([first_two, rest], axis=1)
+            traces = steps.transpose(2, 1, 0, 3).reshape(k, ITERS, 256)
+            part, traces = lax.optimization_barrier((part, traces))
         else:
             part, acc = call(
                 functools.partial(own_kernel, n),
@@ -743,28 +761,6 @@
         low_in, high_in = exchange(low, high)
         prev, cur = cur, nxt
 
-    early = jnp.stack([records[0] + records[1], records[2]])
-    early = early + swap(early)
-    half = jnp.where(odd == 0, early[0], early[1])
-    message = jnp.concatenate([half, mine[None]])
-    groups = [list(range(c, tiles, 2)) for c in range(2)]
-    copies = lax.all_to_all(
-        jnp.broadcast_to(message[None], (tiles // 2,) + message.shape),
-        "tile",
-        0,
-        0,
-        axis_index_groups=groups,
-        tiled=True,
-    )
-    copies, born = lax.optimization_barrier((copies, born))
-    total = jnp.sum(copies, axis=0)
-    other = swap(total)
-    ours, theirs = total[:2], other[:2]
-    first_two = jnp.where(odd == 0, ours, theirs).reshape(2, 2, k, 128)
-    third = jnp.where(odd == 0, theirs, ours)[:, :k]
-    fourth = (total[2] + other[2]).reshape(2, k, 128)
-    steps = jnp.concatenate([first_two, third[:, None], fourth[:, None]], axis=1)
-    traces = steps.transpose(2, 1, 0, 3).reshape(k, ITERS, 256)
     return born.reshape(k, depth, nx, ny), traces
 
 

time: 249 us -> 252 us (1.012)
  starting transfers between devices: 65.3 us -> 59.1 us
  waiting for transfers between devices: 105 us -> 111 us
  local copies, waits for them, and re-layouts: 16.1 us -> 19.4 us
    all_to_all x1, waiting for transfers between devices: 6.28 us -> 12 us  [local(): lax.all_to_all(jnp.broadcast_to(message[None], (tiles // 2,) + message.sh...]
    ppermute x4, starting transfers between devices: 24.4 us -> 19.5 us  [exchange(): there = lax.ppermute(away, 'tile', pairs + [(b, a) for a, b in pairs])]
    unnamed x79 -> x87, local copies, waits for them, and re-layouts: 12.9 us -> 16.1 us
    ppermute x6 -> x5, starting transfers between devices: 13 us -> 9.88 us  [swap(): return lax.ppermute(value, 'tile', [(i, i ^ 1) for i in range(count)])]
  transfers between devices with their start and end apart: 12 -> 11, of which waited for: 5 -> 5; matrix products, arithmetic and copies ran while one was open for 2% -> 3% of each run, Pallas kernels for 15% -> 13%
where the time goes in v4:
time: 252 us; the launch traced here: 249 us
  waiting for transfers between devices  111 us (44%)
  starting transfers between devices  59.1 us (23%)
  Pallas kernels  53.5 us (21%)
  local copies, waits for them, and re-layouts  19.4 us (8%)
  other arithmetic  4.06 us (2%)
    ppermute x4, waiting for transfers between devices, exchange(): there = lax.ppermute(away, 'tile', pairs + [(b, a) for a, b in pairs])  97.6 us
    pallas_call x9, Pallas kernels, call(): pl.pallas_call(kernel, out_shape=out_shape, in_specs=[sspec()] * len(scal...  44.1 us
    ppermute x4, starting transfers between devices, exchange(): there = lax.ppermute(away, 'tile', pairs + [(b, a) for a, b in pairs])  19.5 us
    all_to_all x1, starting transfers between devices, local(): incoming = lax.all_to_all(packed, 'tile', 0, 0, tiled=True)  19.4 us
    unnamed x87, local copies, waits for them, and re-layouts  16.1 us
    all_to_all x1, waiting for transfers between devices, local(): lax.all_to_all(jnp.broadcast_to(message[None], (tiles // 2,) + message.sh...  12 us
    all_to_all x1, starting transfers between devices, local(): lax.all_to_all(jnp.broadcast_to(message[None], (tiles // 2,) + message.sh...  10.3 us
    ppermute x5, starting transfers between devices, swap(): return lax.ppermute(value, 'tile', [(i, i ^ 1) for i in range(count)])  9.88 us
  transfers between devices with their start and end apart: 11, of which 5 were waited for; matrix products, arithmetic and copies ran while one was open for 3% of the time, Pallas kernels for 13%

profile of v4, /device:TPU:1, one launch (start us, length us, event | category | flops | bytes accessed | tf_op | source)
XLA Modules:
  0.0 248.7 jit_solution(12506649080969936707)
XLA Ops:
  0.6 1.2 copy-done.12
  1.9 0.7 copy-done.24
  2.5 0.7 copy-done.25
  3.2 3.0 %pack.1 = bf16[32,272,128]{2,1,0:T(8,128)(2,1)} custom-call(s32[32]{0:T(128)S(1)} %bitcast.106, s32[32]{0:T(128)S(1)} %copy-done.25, bf16[4,32,32,128]{3,2,1,0:T(8,128)(2,1)S(1)} %copy-done.12), custom_call_target="tpu_custom_call" | custom-call | tf_op jit(solution)/shard_map/pack/pallas_call | solution.py:85
  6.2 19.4 %all-to-all-start = ((bf16[32,272,128]{2,1,0:T(8,128)(2,1)}), bf16[32,272,128]{2,1,0:T(8,128)(2,1)}, u32[]{:S(2)}, u32[]{:S(2)}) async-start(bf16[32,272,128]{2,1,0:T(8,128)(2,1)} %pack.1), calls=%async_computation | async-start | bytes 4456448 | tf_op jit(solution)/shard_map/all_to_all | solution.py:600
  25.6 0.1 copy.100
  25.7 0.1 copy.113
  25.7 0.9 copy-done.28
  26.6 1.2 fusion.4
  28.2 0.0 copy-start.31
  28.2 0.1 constant_dynamic-update-slice_fusion
  28.3 0.9 broadcast_select_fusion
  29.2 2.2 collective-permute-start.1
  31.4 7.3 %collective-permute-start = (bf16[21,64,128]{2,1,0:T(8,128)(2,1)}, bf16[21,64,128]{2,1,0:T(8,128)(2,1)}, u32[]{:S(2)}, u32[]{:S(2)}) collective-permute-start(bf16[21,64,128]{2,1,0:T(8,128)(2,1)} %get-tuple-element.59), channel_id=1, source_target_pairs={{16,32},{48,64},{80,96},{112,128},{144,160},{176,192},{208,224},{2... | collective-permute-start | bytes 1032200 | tf_op jit(solution)/shard_map/ppermute | solution.py:562
  38.8 0.6 fusion.7
  40.1 0.1 pad_add_fusion.1.where
  40.2 0.1 convert_multiply_fusion
  40.3 0.1 maximum_bitcast_fusion.coef.refs_6_.refs_3_.refs_5_.refs_4_
  40.4 0.0 copy-start
  40.4 0.1 convert_bitcast_fusion.1
  40.5 1.3 copy-done.30
  41.8 0.1 convert_bitcast_fusion
  41.9 1.3 pad_add_fusion.src.refs_0_
  43.2 0.1 copy.102
  43.3 6.4 %receivers.1.refs_1_.refs_0_ = s32[8,256]{1,0:T(8,128)S(1)} custom-call(s32[256]{0:T(256)S(1)} %copy-done.21, s32[256]{0:T(256)S(1)} %copy-done.22, s32[256]{0:T(256)S(1)} %copy-done.23, s32[3]{0:T(128)S(1)} %pad_add_fusion.1.where), custom_call_target="tpu_custom_call" | custom-call | tf_op jit(solution)/shard_map/receivers/pallas_call | solution.py:125
  49.8 0.6 copy-done.13
  50.4 0.1 pad_maximum_fusion.1.prev
  50.5 0.0 copy-start.11
  50.5 0.1 pad_maximum_fusion.cur.refs_2_
  50.6 0.8 copy-done.11
  51.4 6.0 %own1.1 = (f32[5,8,64,128]{3,2,1,0:T(8,128)S(1)}, f32[8,64,128]{2,1,0:T(8,128)S(1)}) custom-call(f32[4]{0:T(128)S(1)} %copy-done.20, s32[4]{0:T(128)S(1)} %pad_add_fusion.src.refs_0_, f32[5,8,64,128]{3,2,1,0:T(8,128)S(1)} %pad_maximum_fusion.cur.refs_2_, f32[5,8,64,128]{3,2,1,0:T(8,128)S(1)} %pad_maximum_fusion.1.prev, ...), custom_call_target="tpu_custom_call" | custom-call | flops 26214400 | bytes 5242880 | tf_op jit(solution)/shard_map/own1/pallas_call | solution.py:644
  57.4 1.1 copy-done.10
  58.5 0.7 copy-done.17
  59.2 83.0 %collective-permute-done.refs_4_ = bf16[21,64,128]{2,1,0:T(8,128)(2,1)} collective-permute-done((bf16[21,64,128]{2,1,0:T(8,128)(2,1)}, bf16[21,64,128]{2,1,0:T(8,128)(2,1)}, u32[]{:S(2)}, u32[]{:S(2)}) %collective-permute-start) | collective-permute-done | bytes 344096 | tf_op jit(solution)/shard_map/ppermute | solution.py:562
  142.2 8.5 %finish1.1 = (f32[5,8,64,128]{3,2,1,0:T(8,128)}, f32[4,8,64,128]{3,2,1,0:T(8,128)}, bf16[25,64,128]{2,1,0:T(8,128)(2,1)}, bf16[25,64,128]{2,1,0:T(8,128)(2,1)}, f32[2,8,128]{2,1,0:T(8,128)}) custom-call(s32[4]{0:T(128)} %copy-done.18, s32[8,256]{1,0:T(8,128)} %copy-done.13, f32[5,8,64,128]{3,2,1,0:T(8,128)} %copy-done.10, f32[8,64,128]{2,1,0:T(8,128)} %copy-done.17, ...), custom_call_target="tpu_custom_call" | custom-call | flops 6553600 | bytes 5242880 | tf_op jit(solution)/shard_map/finish1/pallas_call | solution.py:644
  150.7 4.3 %collective-permute-start.2 = (bf16[25,64,128]{2,1,0:T(8,128)(2,1)}, bf16[25,64,128]{2,1,0:T(8,128)(2,1)S(1)}, u32[]{:S(2)}, u32[]{:S(2)}) collective-permute-start(bf16[25,64,128]{2,1,0:T(8,128)(2,1)} %get-tuple-element.37), channel_id=1, source_target_pairs={{16,32},{48,64},{80,96},{112,128},{144,160},{176,192},{208,224},{2... | collective-permute-start | bytes 1228808 | tf_op jit(solution)/shard_map/ppermute | solution.py:562
  155.0 1.9 collective-permute-start.3
  157.0 1.2 copy-done.2
  158.2 1.3 copy-done.4
  159.5 6.8 %own2.1 = (f32[5,8,64,128]{3,2,1,0:T(8,128)S(1)}, f32[8,64,128]{2,1,0:T(8,128)S(1)}, bf16[64,128]{1,0:T(8,128)(2,1)S(1)}) custom-call(f32[4]{0:T(128)S(1)} %copy-done.20, s32[4]{0:T(128)S(1)} %copy-done.19, s32[8,256]{1,0:T(8,128)S(1)} %copy-done.14, f32[5,8,64,128]{3,2,1,0:T(8,128)S(1)} %copy-done.4, f32[5,8,64,128]{3,2,1,0:T(8,128)S(1)} %pad_maximum_fusion.cur.refs_2_, ...), custom_call_target="tpu_custom_call" | custom-call | flops 26214400 | bytes 5242880 | tf_op jit(solution)/shard_map/own2/pallas_call | solution.py:644
  166.4 5.2 %collective-permute-done.2.refs_3_ = bf16[25,64,128]{2,1,0:T(8,128)(2,1)S(1)} collective-permute-done((bf16[25,64,128]{2,1,0:T(8,128)(2,1)}, bf16[25,64,128]{2,1,0:T(8,128)(2,1)S(1)}, u32[]{:S(2)}, u32[]{:S(2)}) %collective-permute-start.2) | collective-permute-done | bytes 409632 | tf_op jit(solution)/shard_map/ppermute | solution.py:562
  171.6 2.3 finish2.1
  173.9 3.3 %collective-permute-start.4 = (bf16[26,64,128]{2,1,0:T(8,128)(2,1)S(1)}, bf16[26,64,128]{2,1,0:T(8,128)(2,1)S(1)}, u32[]{:S(2)}, u32[]{:S(2)}) collective-permute-start(bf16[26,64,128]{2,1,0:T(8,128)(2,1)S(1)} %get-tuple-element.44), channel_id=1, source_target_pairs={{16,32},{48,64},{80,96},{112,128},{144,160},{176,192},{208,224},{2... | collective-permute-start | bytes 1277960 | tf_op jit(solution)/shard_map/ppermute | solution.py:562
  177.2 1.9 collective-permute-start.5
  179.2 6.0 %own3.1 = (f32[5,8,64,128]{3,2,1,0:T(8,128)S(1)}, f32[8,64,128]{2,1,0:T(8,128)S(1)}) custom-call(f32[4]{0:T(128)S(1)} %copy-done.20, s32[4]{0:T(128)S(1)} %copy-done.19, f32[5,8,64,128]{3,2,1,0:T(8,128)S(1)} %get-tuple-element.41.cur.refs_2_.prev, f32[5,8,64,128]{3,2,1,0:T(8,128)S(1)} %copy-done.5, f32[4,8,64,128]{3,2,1,0:T(8,128)S(1)} %copy-done.1, ...), custom_call_target="tpu_custom_call" | custom-call | flops 26214400 | bytes 5242880 | tf_op jit(solution)/shard_map/own3/pallas_call | solution.py:644
  185.1 9.5 %collective-permute-done.4.refs_3_ = bf16[26,64,128]{2,1,0:T(8,128)(2,1)S(1)} collective-permute-done((bf16[26,64,128]{2,1,0:T(8,128)(2,1)S(1)}, bf16[26,64,128]{2,1,0:T(8,128)(2,1)S(1)}, u32[]{:S(2)}, u32[]{:S(2)}) %collective-permute-start.4) | collective-permute-done | bytes 426016 | tf_op jit(solution)/shard_map/ppermute | solution.py:562
  194.6 2.3 finish3.1
  197.0 3.2 %share.1 = f32[8,128]{1,0:T(8,128)S(1)} custom-call(s32[8,256]{1,0:T(8,128)S(1)} %copy-done.14, f32[5,8,64,128]{3,2,1,0:T(8,128)S(1)} %get-tuple-element.47.refs_1_.cur, f32[5,8,64,128]{3,2,1,0:T(8,128)S(1)} %get-tuple-element.41.cur.refs_2_.prev, f32[4,8,64,128]{3,2,1,0:T(8,128)S(1)} %copy-done.1, f32[4,8,64,128]{3,2,1,0:T(8,128)S(1)} %copy-done.3, ...), custom_call_target="tpu_custom_call" | custom-call | flops 6553600 | bytes 5242880 | tf_op jit(solution)/shard_map/share/pallas_call | solution.py:644
  200.2 0.7 broadcast_in_dim.22
  200.9 10.3 %all-to-all-start.1 = ((f32[16,4,8,128]{3,2,1,0:T(8,128)}), f32[16,4,8,128]{3,2,1,0:T(8,128)}, u32[]{:S(2)}, u32[]{:S(2)}) async-start(f32[16,4,8,128]{3,2,1,0:T(8,128)} %broadcast_in_dim.22), calls=%async_computation.1 | async-start | bytes 524288 | tf_op jit(solution)/shard_map/all_to_all | solution.py:686
  211.2 4.6 %collective-permute-start.7 = (bf16[25,64,128]{2,1,0:T(8,128)(2,1)}, bf16[25,64,128]{2,1,0:T(8,128)(2,1)}, u32[]{:S(2)}, u32[]{:S(2)}) collective-permute-start(bf16[25,64,128]{2,1,0:T(8,128)(2,1)} %copy-done.27), channel_id=1, source_target_pairs={{16,32},{48,64},{80,96},{112,128},{144,160},{176,192},{208,224},{2... | collective-permute-start | bytes 1228808 | tf_op jit(solution)/shard_map/ppermute | solution.py:562
  215.8 1.9 collective-permute-start.8
  217.8 1.3 copy-done.9
  219.1 6.0 %own4.1 = (f32[5,8,64,128]{3,2,1,0:T(8,128)S(1)}, f32[8,64,128]{2,1,0:T(8,128)S(1)}) custom-call(f32[4]{0:T(128)S(1)} %copy-done.20, s32[4]{0:T(128)S(1)} %copy-done.19, f32[5,8,64,128]{3,2,1,0:T(8,128)S(1)} %copy-done.9, f32[5,8,64,128]{3,2,1,0:T(8,128)S(1)} %get-tuple-element.41.cur.refs_2_.prev, f32[4,8,64,128]{3,2,1,0:T(8,128)S(1)} %copy-done.1, ...), custom_call_target="tpu_custom_call" | custom-call | flops 26214400000 | bytes 5242880 | tf_op jit(solution)/shard_map/own4/pallas_call | solution.py:644
  225.0 1.1 copy-done.6
  226.1 0.7 copy-done.15
  226.8 12.0 %all-to-all-done.1 = f32[16,4,8,128]{3,2,1,0:T(8,128)} async-done(((f32[16,4,8,128]{3,2,1,0:T(8,128)}), f32[16,4,8,128]{3,2,1,0:T(8,128)}, u32[]{:S(2)}, u32[]{:S(2)}) %all-to-all-start.1) | async-done | bytes 262176 | tf_op jit(solution)/shard_map/all_to_all | solution.py:686
  238.8 1.0 reduce_sum.9
  239.7 1.9 collective-permute-start.6
  241.7 1.1 collective-permute-done.6
  242.8 0.6 copy.111
  243.5 1.3 copy-done.7
  244.8 0.9 copy-done.16
  245.7 3.0 %finish4.1 = f32[4,512,128]{2,1,0:T(8,128)} custom-call(s32[4]{0:T(128)S(1)} %copy-done.19, f32[5,8,64,128]{3,2,1,0:T(8,128)S(1)} %copy-done.7, f32[8,64,128]{2,1,0:T(8,128)S(1)} %copy-done.16, bf16[25,64,128]{2,1,0:T(8,128)(2,1)} %collective-permute-done.7.refs_2_, bf16[25,64,128]{2,1,0:T(8,128)(2,1)} %collective-permute-done.8.refs_3_, ...), custom_call_target="tpu_custom_call" | custom-call | flops 6553600 | bytes 5242880 | tf_op jit(solution)/shard_map/finish4/pallas_call | solution.py:644
  (85 shorter events, 0.5 us)
Async XLA Ops:
  0.6 1.2 copy-start.12
  1.9 0.7 copy-start.24
  2.5 0.7 copy-start.25
  6.2 19.4 %copy-start.29 = (f32[64,8,128]{2,1,0:T(8,128)S(1)}, f32[64,8,128]{2,1,0:T(8,128)}, u32[]{:S(2)}) copy-start(f32[64,8,128]{2,1,0:T(8,128)} %param.16) | copy-start | bytes 786436
  6.2 136.0 %all-to-all-start = ((bf16[32,272,128]{2,1,0:T(8,128)(2,1)}), bf16[32,272,128]{2,1,0:T(8,128)(2,1)}, u32[]{:S(2)}, u32[]{:S(2)}) async-start(bf16[32,272,128]{2,1,0:T(8,128)(2,1)} %pack.1), calls=%async_computation | async-start | bytes 4456448 | tf_op jit(solution)/shard_map/all_to_all | solution.py:600
  25.6 1.0 copy-start.28
  28.1 10.6 %copy-start.35 = (s32[3]{0:T(128)S(1)}, s32[3]{0:T(128)}, u32[]{:S(2)}) copy-start(s32[3]{0:T(128)} %param.25) | copy-start | bytes 40
  28.2 12.0 %copy-start.33 = (bf16[64,8,128]{2,1,0:T(8,128)(2,1)S(1)}, bf16[64,8,128]{2,1,0:T(8,128)(2,1)}, u32[]{:S(2)}) copy-start(bf16[64,8,128]{2,1,0:T(8,128)(2,1)} %param.17) | copy-start | bytes 393220
  28.2 12.0 %copy-start.31 = (bf16[3,64,8,128]{3,2,1,0:T(8,128)(2,1)S(1)}, bf16[3,64,8,128]{3,2,1,0:T(8,128)(2,1)}, u32[]{:S(2)}) copy-start(bf16[3,64,8,128]{3,2,1,0:T(8,128)(2,1)} %param.18) | copy-start | bytes 1179652
  29.2 30.0 %collective-permute-start.1 = (bf16[21,64,128]{2,1,0:T(8,128)(2,1)}, bf16[21,64,128]{2,1,0:T(8,128)(2,1)}, u32[]{:S(2)}, u32[]{:S(2)}) collective-permute-start(bf16[21,64,128]{2,1,0:T(8,128)(2,1)} %get-tuple-element.58), channel_id=1, source_target_pairs={{0,16},{16,0},{32,48},{48,32},{64,80},{80,64},{96,112},{112,96},{1... | collective-permute-start | bytes 1032200 | tf_op jit(solution)/shard_map/ppermute | solution.py:568
  31.4 110.8 %collective-permute-start = (bf16[21,64,128]{2,1,0:T(8,128)(2,1)}, bf16[21,64,128]{2,1,0:T(8,128)(2,1)}, u32[]{:S(2)}, u32[]{:S(2)}) collective-permute-start(bf16[21,64,128]{2,1,0:T(8,128)(2,1)} %get-tuple-element.59), channel_id=1, source_target_pairs={{16,32},{48,64},{80,96},{112,128},{144,160},{176,192},{208,224},{2... | collective-permute-start | bytes 1032200 | tf_op jit(solution)/shard_map/ppermute | solution.py:562
  40.4 10.3 %copy-start = (f32[4,8,64,128]{3,2,1,0:T(8,128)}, f32[4,8,64,128]{3,2,1,0:T(8,128)S(1)}, u32[]{:S(2)}) copy-start(f32[4,8,64,128]{3,2,1,0:T(8,128)S(1)} %maximum_bitcast_fusion.coef.refs_6_.refs_3_.refs_5_.refs_4_) | copy-start | bytes 3145732
  40.4 1.4 copy-start.30
  40.4 2.9 %copy-start.32 = (f32[64,8,128]{2,1,0:T(8,128)S(1)}, f32[64,8,128]{2,1,0:T(8,128)}, u32[]{:S(2)}) copy-start(f32[64,8,128]{2,1,0:T(8,128)} %param.15) | copy-start | bytes 786436
  41.8 1.5 copy-start.21
  41.8 1.5 copy-start.22
  41.8 1.5 copy-start.23
  43.2 7.4 %copy-start.18 = (s32[4]{0:T(128)}, s32[4]{0:T(128)S(1)}, u32[]{:S(2)}) copy-start(s32[4]{0:T(128)S(1)} %pad_add_fusion.src.refs_0_) | copy-start | bytes 52
  49.8 0.6 copy-start.13
  50.5 0.9 copy-start.11
  50.5 0.9 copy-start.20
  57.4 1.1 copy-start.10
  58.5 0.7 copy-start.17
  142.2 14.8 %copy-start.1 = (f32[4,8,64,128]{3,2,1,0:T(8,128)S(1)}, f32[4,8,64,128]{3,2,1,0:T(8,128)}, u32[]{:S(2)}) copy-start(f32[4,8,64,128]{3,2,1,0:T(8,128)} %copy-done) | copy-start | bytes 3145732
  142.2 14.8 %copy-start.14 = (s32[8,256]{1,0:T(8,128)S(1)}, s32[8,256]{1,0:T(8,128)}, u32[]{:S(2)}) copy-start(s32[8,256]{1,0:T(8,128)} %copy-done.13) | copy-start | bytes 24580
  142.2 14.8 %copy-start.19 = (s32[4]{0:T(128)S(1)}, s32[4]{0:T(128)}, u32[]{:S(2)}) copy-start(s32[4]{0:T(128)} %copy-done.18) | copy-start | bytes 52
  150.7 20.8 %collective-permute-start.2 = (bf16[25,64,128]{2,1,0:T(8,128)(2,1)}, bf16[25,64,128]{2,1,0:T(8,128)(2,1)S(1)}, u32[]{:S(2)}, u32[]{:S(2)}) collective-permute-start(bf16[25,64,128]{2,1,0:T(8,128)(2,1)} %get-tuple-element.37), channel_id=1, source_target_pairs={{16,32},{48,64},{80,96},{112,128},{144,160},{176,192},{208,224},{2... | collective-permute-start | bytes 1228808 | tf_op jit(solution)/shard_map/ppermute | solution.py:562
  155.0 16.5 %collective-permute-start.3 = (bf16[25,64,128]{2,1,0:T(8,128)(2,1)}, bf16[25,64,128]{2,1,0:T(8,128)(2,1)S(1)}, u32[]{:S(2)}, u32[]{:S(2)}) collective-permute-start(bf16[25,64,128]{2,1,0:T(8,128)(2,1)} %get-tuple-element.38), channel_id=1, source_target_pairs={{0,16},{16,0},{32,48},{48,32},{64,80},{80,64},{96,112},{112,96},{1... | collective-permute-start | bytes 1228808 | tf_op jit(solution)/shard_map/ppermute | solution.py:568
  157.0 1.2 copy-start.2
  158.2 1.3 copy-start.4
  159.5 12.0 %copy-start.3 = (f32[4,8,64,128]{3,2,1,0:T(8,128)S(1)}, f32[4,8,64,128]{3,2,1,0:T(8,128)}, u32[]{:S(2)}) copy-start(f32[4,8,64,128]{3,2,1,0:T(8,128)} %get-tuple-element.34.refs_5_.refs_6_.refs_4_) | copy-start | bytes 3145732
  171.6 7.6 %copy-start.34 = (f32[2,8,128]{2,1,0:T(8,128)S(1)}, f32[2,8,128]{2,1,0:T(8,128)}, u32[]{:S(2)}) copy-start(f32[2,8,128]{2,1,0:T(8,128)} %get-tuple-element.32) | copy-start | bytes 24580
  171.6 7.6 %copy-start.5 = (f32[5,8,64,128]{3,2,1,0:T(8,128)S(1)}, f32[5,8,64,128]{3,2,1,0:T(8,128)}, u32[]{:S(2)}) copy-start(f32[5,8,64,128]{3,2,1,0:T(8,128)} %get-tuple-element.33.refs_1_.prev) | copy-start | bytes 3932164
  173.9 20.7 %collective-permute-start.4 = (bf16[26,64,128]{2,1,0:T(8,128)(2,1)S(1)}, bf16[26,64,128]{2,1,0:T(8,128)(2,1)S(1)}, u32[]{:S(2)}, u32[]{:S(2)}) collective-permute-start(bf16[26,64,128]{2,1,0:T(8,128)(2,1)S(1)} %get-tuple-element.44), channel_id=1, source_target_pairs={{16,32},{48,64},{80,96},{112,128},{144,160},{176,192},{208,224},{2... | collective-permute-start | bytes 1277960 | tf_op jit(solution)/shard_map/ppermute | solution.py:562
  177.2 17.4 %collective-permute-start.5 = (bf16[26,64,128]{2,1,0:T(8,128)(2,1)S(1)}, bf16[26,64,128]{2,1,0:T(8,128)(2,1)S(1)}, u32[]{:S(2)}, u32[]{:S(2)}) collective-permute-start(bf16[26,64,128]{2,1,0:T(8,128)(2,1)S(1)} %get-tuple-element.45), channel_id=1, source_target_pairs={{0,16},{16,0},{32,48},{48,32},{64,80},{80,64},{96,112},{112,96},{1... | collective-permute-start | bytes 1277960 | tf_op jit(solution)/shard_map/ppermute | solution.py:568
  196.9 3.2 %copy-start.8 = (f32[5,8,64,128]{3,2,1,0:T(8,128)}, f32[5,8,64,128]{3,2,1,0:T(8,128)S(1)}, u32[]{:S(2)}) copy-start(f32[5,8,64,128]{3,2,1,0:T(8,128)S(1)} %get-tuple-element.47.refs_1_.cur) | copy-start | bytes 3932164
  196.9 3.2 %copy-start.26 = (bf16[25,64,128]{2,1,0:T(8,128)(2,1)}, bf16[25,64,128]{2,1,0:T(8,128)(2,1)S(1)}, u32[]{:S(2)}) copy-start(bf16[25,64,128]{2,1,0:T(8,128)(2,1)S(1)} %get-tuple-element.56) | copy-start | bytes 1228804
  196.9 3.2 %copy-start.27 = (bf16[25,64,128]{2,1,0:T(8,128)(2,1)}, bf16[25,64,128]{2,1,0:T(8,128)(2,1)S(1)}, u32[]{:S(2)}) copy-start(bf16[25,64,128]{2,1,0:T(8,128)(2,1)S(1)} %get-tuple-element.55) | copy-start | bytes 1228804
  200.9 37.9 %all-to-all-start.1 = ((f32[16,4,8,128]{3,2,1,0:T(8,128)}), f32[16,4,8,128]{3,2,1,0:T(8,128)}, u32[]{:S(2)}, u32[]{:S(2)}) async-start(f32[16,4,8,128]{3,2,1,0:T(8,128)} %broadcast_in_dim.22), calls=%async_computation.1 | async-start | bytes 524288 | tf_op jit(solution)/shard_map/all_to_all | solution.py:686
  211.2 32.2 %collective-permute-start.7 = (bf16[25,64,128]{2,1,0:T(8,128)(2,1)}, bf16[25,64,128]{2,1,0:T(8,128)(2,1)}, u32[]{:S(2)}, u32[]{:S(2)}) collective-permute-start(bf16[25,64,128]{2,1,0:T(8,128)(2,1)} %copy-done.27), channel_id=1, source_target_pairs={{16,32},{48,64},{80,96},{112,128},{144,160},{176,192},{208,224},{2... | collective-permute-start | bytes 1228808 | tf_op jit(solution)/shard_map/ppermute | solution.py:562
  215.8 27.6 %collective-permute-start.8 = (bf16[25,64,128]{2,1,0:T(8,128)(2,1)}, bf16[25,64,128]{2,1,0:T(8,128)(2,1)}, u32[]{:S(2)}, u32[]{:S(2)}) collective-permute-start(bf16[25,64,128]{2,1,0:T(8,128)(2,1)} %copy-done.26), channel_id=1, source_target_pairs={{0,16},{16,0},{32,48},{48,32},{64,80},{80,64},{96,112},{112,96},{1... | collective-permute-start | bytes 1228808 | tf_op jit(solution)/shard_map/ppermute | solution.py:568
  217.8 1.3 copy-start.9
  225.0 1.1 copy-start.6
  226.1 0.7 copy-start.15
  239.7 3.1 %collective-permute-start.6 = (f32[4,8,128]{2,1,0:T(8,128)S(1)}, f32[4,8,128]{2,1,0:T(8,128)S(1)}, u32[]{:S(2)}, u32[]{:S(2)}) collective-permute-start(f32[4,8,128]{2,1,0:T(8,128)S(1)} %reduce_sum.9), channel_id=1, source_target_pairs={{0,16},{16,0},{32,48},{48,32},{64,80},{80,64},{96,112},{112,96},{1... | collective-permute-start | bytes 49160 | tf_op jit(solution)/shard_map/ppermute | solution.py:568
  243.5 1.3 copy-start.7
  244.8 0.9 copy-start.16

commit v5 on v3

--- a/solution.py
+++ b/solution.py
@@ -535,7 +535,7 @@
         away[5 * F] = table[...]
         beside[5 * F] = table[...]
     else:
-        nxt, away, beside, traces, found, acc, gathered = rest
+        early, nxt, away, beside, traces, found, acc, gathered = rest
         both = jnp.zeros((16, 128), F32)
         for msg in (away_in, beside_in):
             for term in range(3):
@@ -548,8 +548,25 @@
         finish_part(n, part, acc_own, low_in, high_in, coef, perturb, acc, nxt, low, high, out)
 
     by_parity(src[3], run)
-    if not last:
-        sample_new(n, rec, nxt, traces, gathered, depth, k)
+    if last:
+        return
+    sample_new(n, rec, nxt, traces, gathered, depth, k)
+    if n == 2:
+        left = jnp.concatenate([early[...].reshape(16, 128), traces[...].reshape(16, 128)])
+        for term in range(4):
+            rounded = left.astype(BF) if term < 3 else jnp.zeros((32, 128), BF)
+            beside[5 * F + term // 2, 32 * (term % 2) : 32 * (term % 2) + 32, :] = rounded
+            left = left - rounded.astype(F32)
+
+
+def message_kernel(src, beside, two, third, mine, out):
+    own = jnp.concatenate([two[...].reshape(16, 128), third[...].reshape(16, 128)])
+    theirs = beside[5 * F, 0:32, :].astype(F32) + beside[5 * F, 32:64, :].astype(F32)
+    both = own + (theirs + beside[5 * F + 1, 0:32, :].astype(F32))
+    half = jnp.where(src[3] == 0, both[0:16], both[16:32])
+    message = jnp.concatenate([half, mine[...]]).reshape(3, 8, 128)
+    for i in range(out.shape[0]):
+        out[i] = message
 
 
 def cost(flops, moved):
@@ -634,6 +651,7 @@
     field = jax.ShapeDtypeStruct((nx, depth, ny), F32)
     faces = jax.ShapeDtypeStruct((5 * F, depth, ny), BF)
     wider = jax.ShapeDtypeStruct((5 * F + 1, depth, ny), BF)
+    widest = jax.ShapeDtypeStruct((5 * F + 2, depth, ny), BF)
     traced = jax.ShapeDtypeStruct((2, 8, 128), F32)
     small = VM((8, 128), F32)
     pair = VM((2, 8, 128), F32)
@@ -727,14 +745,18 @@
             break
         else:
             face_type = wider if n == 1 else faces
+            inner_type = wider if n == 1 else widest
+            if n == 2:
+                two = records[0] + records[1]
+            extra = table if n == 1 else two
             more = () if n == 1 else (jax.ShapeDtypeStruct((16, 128), F32),)
             nxt, low, high, traces, *more = call(
                 functools.partial(finish_kernel, n),
                 name,
-                (state, face_type, face_type, traced) + more,
+                (state, face_type, inner_type, traced) + more,
                 [keep, small],
                 (src, rec),
-                arrays + (perturb,) + ((table,) if n == 1 else ()),
+                arrays + (perturb, extra),
                 20,
             )
             if n == 2:
@@ -743,13 +765,18 @@
         low_in, high_in = exchange(low, high)
         prev, cur = cur, nxt
 
-    early = jnp.stack([records[0] + records[1], records[2]])
-    early = early + swap(early)
-    half = jnp.where(odd == 0, early[0], early[1])
-    message = jnp.concatenate([half, mine[None]])
+    (sent,) = call(
+        message_kernel,
+        "message",
+        (jax.ShapeDtypeStruct((tiles // 2, 3, 8, 128), F32),),
+        [],
+        (src,),
+        (high_in, two, records[2], mine),
+        1,
+    )
     groups = [list(range(c, tiles, 2)) for c in range(2)]
     copies = lax.all_to_all(
-        jnp.broadcast_to(message[None], (tiles // 2,) + message.shape),
+        sent,
         "tile",
         0,
         0,

time: 249 us -> 245 us (0.984)
  starting transfers between devices: 65.3 us -> 60.6 us
    all_to_all x1, starting transfers between devices: 8.53 us -> 4.75 us  [local(): lax.all_to_all(sent, 'tile', 0, 0, axis_index_groups=groups, tiled=True)]
    ppermute x6 -> x5, starting transfers between devices: 13 us -> 11.6 us  [swap(): return lax.ppermute(value, 'tile', [(i, i ^ 1) for i in range(count)])]
    pallas_call x9 -> x10, Pallas kernels: 42.5 us -> 43.5 us  [call(): pl.pallas_call(kernel, out_shape=out_shape, in_specs=[sspec()] * len(scal...]
    unnamed x79 -> x85, local copies, waits for them, and re-layouts: 12.9 us -> 13.7 us
  transfers between devices with their start and end apart: 12 -> 11, of which waited for: 5 -> 5; matrix products, arithmetic and copies ran while one was open for 2% -> 2% of each run, Pallas kernels for 15% -> 15%
where the time goes in v5:
time: 245 us; the launch traced here: 241 us
  waiting for transfers between devices  105 us (43%)
  starting transfers between devices  60.6 us (25%)
  Pallas kernels  52.9 us (22%)
  local copies, waits for them, and re-layouts  16.3 us (7%)
  other arithmetic  4.11 us (2%)
    ppermute x4, waiting for transfers between devices, exchange(): there = lax.ppermute(away, 'tile', pairs + [(b, a) for a, b in pairs])  97.3 us
    pallas_call x10, Pallas kernels, call(): pl.pallas_call(kernel, out_shape=out_shape, in_specs=[sspec()] * len(scal...  43.5 us
    ppermute x4, starting transfers between devices, exchange(): there = lax.ppermute(away, 'tile', pairs + [(b, a) for a, b in pairs])  24.8 us
    all_to_all x1, starting transfers between devices, local(): incoming = lax.all_to_all(packed, 'tile', 0, 0, tiled=True)  19.4 us
    unnamed x85, local copies, waits for them, and re-layouts  13.7 us
    ppermute x5, starting transfers between devices, swap(): return lax.ppermute(value, 'tile', [(i, i ^ 1) for i in range(count)])  11.6 us
    all_to_all x1, waiting for transfers between devices, local(): lax.all_to_all(sent, 'tile', 0, 0, axis_index_groups=groups, tiled=True)  6.92 us
    pallas_call x1, Pallas kernels, list_receivers(): pl.pallas_call(list_kernel, out_shape=jax.ShapeDtypeStruct((8, n), jnp.in...  6.43 us
  transfers between devices with their start and end apart: 11, of which 5 were waited for; matrix products, arithmetic and copies ran while one was open for 2% of the time, Pallas kernels for 15%

profile of v5, /device:TPU:1, one launch (start us, length us, event | category | flops | bytes accessed | tf_op | source)
XLA Modules:
  0.0 241.0 jit_solution(14419812970020140198)
XLA Ops:
  0.6 1.2 copy-done.12
  1.9 0.7 copy-done.23
  2.5 0.7 copy-done.24
  3.2 3.0 %pack.1 = bf16[32,272,128]{2,1,0:T(8,128)(2,1)} custom-call(s32[32]{0:T(128)S(1)} %bitcast.103, s32[32]{0:T(128)S(1)} %copy-done.24, bf16[4,32,32,128]{3,2,1,0:T(8,128)(2,1)S(1)} %copy-done.12), custom_call_target="tpu_custom_call" | custom-call | tf_op jit(solution)/shard_map/pack/pallas_call | solution.py:85
  6.1 19.4 %all-to-all-start = ((bf16[32,272,128]{2,1,0:T(8,128)(2,1)}), bf16[32,272,128]{2,1,0:T(8,128)(2,1)}, u32[]{:S(2)}, u32[]{:S(2)}) async-start(bf16[32,272,128]{2,1,0:T(8,128)(2,1)} %pack.1), calls=%async_computation | async-start | bytes 4456448 | tf_op jit(solution)/shard_map/all_to_all | solution.py:617
  25.6 0.1 copy.80
  25.6 0.1 copy.91
  25.7 0.9 copy-done.25
  26.6 1.2 fusion.5
  28.1 0.0 copy-start.34
  28.2 0.0 copy-start.32
  28.2 0.0 copy-start.30
  28.2 0.1 constant_dynamic-update-slice_fusion
  28.3 0.9 broadcast_select_fusion
  29.2 2.2 collective-permute-start.1
  31.4 7.3 %collective-permute-start = (bf16[21,64,128]{2,1,0:T(8,128)(2,1)}, bf16[21,64,128]{2,1,0:T(8,128)(2,1)}, u32[]{:S(2)}, u32[]{:S(2)}) collective-permute-start(bf16[21,64,128]{2,1,0:T(8,128)(2,1)} %get-tuple-element.53), channel_id=1, source_target_pairs={{16,32},{48,64},{80,96},{112,128},{144,160},{176,192},{208,224},{2... | collective-permute-start | bytes 1032200 | tf_op jit(solution)/shard_map/ppermute | solution.py:579
  38.7 0.6 fusion.7
  40.0 0.1 pad_add_fusion.1.where
  40.1 0.1 convert_multiply_fusion
  40.2 0.1 maximum_bitcast_fusion.coef.refs_6_.refs_3_.refs_5_.refs_4_
  40.4 0.0 copy-start.31
  40.4 0.1 convert_bitcast_fusion.1
  40.5 1.3 copy-done.29
  41.8 0.1 convert_bitcast_fusion
  41.9 1.4 pad_add_fusion.src.refs_0_
  43.3 0.1 copy.82
  43.4 6.4 %receivers.1.refs_1_.refs_0_ = s32[8,256]{1,0:T(8,128)S(1)} custom-call(s32[256]{0:T(256)S(1)} %copy-done.20, s32[256]{0:T(256)S(1)} %copy-done.21, s32[256]{0:T(256)S(1)} %copy-done.22, s32[3]{0:T(128)S(1)} %pad_add_fusion.1.where), custom_call_target="tpu_custom_call" | custom-call | tf_op jit(solution)/shard_map/receivers/pallas_call | solution.py:125
  49.8 0.1 pad_maximum_fusion.1.prev
  49.9 0.5 copy-done.14
  50.4 0.4 copy-done.27
  50.8 0.1 pad_maximum_fusion.cur.refs_2_
  50.9 0.7 copy-done.11
  51.7 6.0 %own1.1 = (f32[5,8,64,128]{3,2,1,0:T(8,128)S(1)}, f32[8,64,128]{2,1,0:T(8,128)S(1)}) custom-call(f32[4]{0:T(128)S(1)} %copy-done.19, s32[4]{0:T(128)S(1)} %pad_add_fusion.src.refs_0_, f32[5,8,64,128]{3,2,1,0:T(8,128)S(1)} %pad_maximum_fusion.cur.refs_2_, f32[5,8,64,128]{3,2,1,0:T(8,128)S(1)} %pad_maximum_fusion.1.prev, ...), custom_call_target="tpu_custom_call" | custom-call | flops 26214400 | bytes 5242880 | tf_op jit(solution)/shard_map/own1/pallas_call | solution.py:662
  57.6 1.1 copy-done.10
  58.7 0.7 copy-done.16
  59.5 82.7 %collective-permute-done.refs_4_ = bf16[21,64,128]{2,1,0:T(8,128)(2,1)} collective-permute-done((bf16[21,64,128]{2,1,0:T(8,128)(2,1)}, bf16[21,64,128]{2,1,0:T(8,128)(2,1)}, u32[]{:S(2)}, u32[]{:S(2)}) %collective-permute-start) | collective-permute-done | bytes 344096 | tf_op jit(solution)/shard_map/ppermute | solution.py:579
  142.2 8.2 %finish1.1 = (f32[5,8,64,128]{3,2,1,0:T(8,128)}, f32[4,8,64,128]{3,2,1,0:T(8,128)}, bf16[25,64,128]{2,1,0:T(8,128)(2,1)}, bf16[25,64,128]{2,1,0:T(8,128)(2,1)}, f32[2,8,128]{2,1,0:T(8,128)}) custom-call(s32[4]{0:T(128)} %copy-done.17, s32[8,256]{1,0:T(8,128)} %copy-done.14, f32[5,8,64,128]{3,2,1,0:T(8,128)} %copy-done.10, f32[8,64,128]{2,1,0:T(8,128)} %copy-done.16, ...), custom_call_target="tpu_custom_call" | custom-call | flops 6553600 | bytes 5242880 | tf_op jit(solution)/shard_map/finish1/pallas_call | solution.py:662
  150.4 5.0 %collective-permute-start.2 = (bf16[25,64,128]{2,1,0:T(8,128)(2,1)}, bf16[25,64,128]{2,1,0:T(8,128)(2,1)S(1)}, u32[]{:S(2)}, u32[]{:S(2)}) collective-permute-start(bf16[25,64,128]{2,1,0:T(8,128)(2,1)} %get-tuple-element.33), channel_id=1, source_target_pairs={{16,32},{48,64},{80,96},{112,128},{144,160},{176,192},{208,224},{2... | collective-permute-start | bytes 1228808 | tf_op jit(solution)/shard_map/ppermute | solution.py:579
  155.4 1.9 collective-permute-start.3
  157.4 1.2 copy-done.2
  158.6 1.3 copy-done.4
  159.9 6.5 %own2.1 = (f32[5,8,64,128]{3,2,1,0:T(8,128)S(1)}, f32[8,64,128]{2,1,0:T(8,128)S(1)}, bf16[64,128]{1,0:T(8,128)(2,1)S(1)}) custom-call(f32[4]{0:T(128)S(1)} %copy-done.19, s32[4]{0:T(128)S(1)} %copy-done.18, s32[8,256]{1,0:T(8,128)S(1)} %copy-done.15, f32[5,8,64,128]{3,2,1,0:T(8,128)S(1)} %copy-done.4, f32[5,8,64,128]{3,2,1,0:T(8,128)S(1)} %pad_maximum_fusion.cur.refs_2_, ...), custom_call_target="tpu_custom_call" | custom-call | flops 26214400 | bytes 5242880 | tf_op jit(solution)/shard_map/own2/pallas_call | solution.py:662
  166.4 4.8 %collective-permute-done.2.refs_3_ = bf16[25,64,128]{2,1,0:T(8,128)(2,1)S(1)} collective-permute-done((bf16[25,64,128]{2,1,0:T(8,128)(2,1)}, bf16[25,64,128]{2,1,0:T(8,128)(2,1)S(1)}, u32[]{:S(2)}, u32[]{:S(2)}) %collective-permute-start.2) | collective-permute-done | bytes 409632 | tf_op jit(solution)/shard_map/ppermute | solution.py:579
  171.2 2.0 finish2.1
  173.2 3.8 %collective-permute-start.4 = (bf16[26,64,128]{2,1,0:T(8,128)(2,1)S(1)}, bf16[26,64,128]{2,1,0:T(8,128)(2,1)S(1)}, u32[]{:S(2)}, u32[]{:S(2)}) collective-permute-start(bf16[26,64,128]{2,1,0:T(8,128)(2,1)S(1)} %get-tuple-element.39), channel_id=1, source_target_pairs={{16,32},{48,64},{80,96},{112,128},{144,160},{176,192},{208,224},{2... | collective-permute-start | bytes 1277960 | tf_op jit(solution)/shard_map/ppermute | solution.py:579
  177.1 1.9 collective-permute-start.5
  179.0 6.0 %own3.1 = (f32[5,8,64,128]{3,2,1,0:T(8,128)S(1)}, f32[8,64,128]{2,1,0:T(8,128)S(1)}) custom-call(f32[4]{0:T(128)S(1)} %copy-done.19, s32[4]{0:T(128)S(1)} %copy-done.18, f32[5,8,64,128]{3,2,1,0:T(8,128)S(1)} %get-tuple-element.36.cur.refs_2_.prev, f32[5,8,64,128]{3,2,1,0:T(8,128)S(1)} %copy-done.5, f32[4,8,64,128]{3,2,1,0:T(8,128)S(1)} %copy-done.1, ...), custom_call_target="tpu_custom_call" | custom-call | flops 26214400 | bytes 5242880 | tf_op jit(solution)/shard_map/own3/pallas_call | solution.py:662
  185.0 9.8 %collective-permute-done.4.refs_3_ = bf16[26,64,128]{2,1,0:T(8,128)(2,1)S(1)} collective-permute-done((bf16[26,64,128]{2,1,0:T(8,128)(2,1)S(1)}, bf16[26,64,128]{2,1,0:T(8,128)(2,1)S(1)}, u32[]{:S(2)}, u32[]{:S(2)}) %collective-permute-start.4) | collective-permute-done | bytes 426016 | tf_op jit(solution)/shard_map/ppermute | solution.py:579
  194.8 2.8 %finish3.1 = (f32[5,8,64,128]{3,2,1,0:T(8,128)S(1)}, bf16[25,64,128]{2,1,0:T(8,128)(2,1)}, bf16[27,64,128]{2,1,0:T(8,128)(2,1)S(1)}, f32[2,8,128]{2,1,0:T(8,128)S(1)}, f32[16,128]{1,0:T(8,128)S(1)}) custom-call(s32[4]{0:T(128)S(1)} %copy-done.18, s32[8,256]{1,0:T(8,128)S(1)} %copy-done.15, f32[5,8,64,128]{3,2,1,0:T(8,128)S(1)} %get-tuple-element.37.refs_1_, ...), custom_call_target="tpu_custom_call" | custom-call | flops 6553600 | bytes 5242880 | tf_op jit(solution)/shard_map/finish3/pallas_call | solution.py:662
  197.6 1.9 collective-permute-start.6
  199.5 8.7 %collective-permute-start.7 = (bf16[25,64,128]{2,1,0:T(8,128)(2,1)}, bf16[25,64,128]{2,1,0:T(8,128)(2,1)}, u32[]{:S(2)}, u32[]{:S(2)}) collective-permute-start(bf16[25,64,128]{2,1,0:T(8,128)(2,1)} %get-tuple-element.49), channel_id=1, source_target_pairs={{16,32},{48,64},{80,96},{112,128},{144,160},{176,192},{208,224},{2... | collective-permute-start | bytes 1228808 | tf_op jit(solution)/shard_map/ppermute | solution.py:579
  208.2 2.8 %share.1.mine = f32[8,128]{1,0:T(8,128)S(1)} custom-call(s32[8,256]{1,0:T(8,128)S(1)} %copy-done.15, f32[5,8,64,128]{3,2,1,0:T(8,128)S(1)} %get-tuple-element.45.refs_1_.cur, f32[5,8,64,128]{3,2,1,0:T(8,128)S(1)} %get-tuple-element.36.cur.refs_2_.prev, f32[4,8,64,128]{3,2,1,0:T(8,128)S(1)} %copy-done.1, f32[4,8,64,128]{3,2,1,0:T(8,128)S(1)} %copy-done.3, ...), custom_call_target="tpu_custom_call" | custom-call | flops 6553600 | bytes 5242880 | tf_op jit(solution)/shard_map/share/pallas_call | solution.py:662
  211.1 0.6 message.1
  211.6 0.8 copy-done.6
  212.4 0.7 copy-done.13
  213.1 4.7 %all-to-all-start.1 = ((f32[16,3,8,128]{3,2,1,0:T(8,128)}), f32[16,3,8,128]{3,2,1,0:T(8,128)}, u32[]{:S(2)}, u32[]{:S(2)}) async-start(f32[16,3,8,128]{3,2,1,0:T(8,128)} %copy-done.13), calls=%async_computation.1 | async-start | bytes 393216 | tf_op jit(solution)/shard_map/all_to_all | solution.py:778
  217.8 1.3 copy-done.9
  219.2 6.0 %own4.1 = (f32[5,8,64,128]{3,2,1,0:T(8,128)S(1)}, f32[8,64,128]{2,1,0:T(8,128)S(1)}) custom-call(f32[4]{0:T(128)S(1)} %copy-done.19, s32[4]{0:T(128)S(1)} %copy-done.18, f32[5,8,64,128]{3,2,1,0:T(8,128)S(1)} %copy-done.9, f32[5,8,64,128]{3,2,1,0:T(8,128)S(1)} %get-tuple-element.36.cur.refs_2_.prev, f32[4,8,64,128]{3,2,1,0:T(8,128)S(1)} %copy-done.1, ...), custom_call_target="tpu_custom_call" | custom-call | flops 26214400000 | bytes 5242880 | tf_op jit(solution)/shard_map/own4/pallas_call | solution.py:662
  225.1 2.8 %finish4.1 = f32[4,512,128]{2,1,0:T(8,128)} custom-call(s32[4]{0:T(128)S(1)} %copy-done.18, f32[5,8,64,128]{3,2,1,0:T(8,128)S(1)} %get-tuple-element.47.refs_0_, f32[8,64,128]{2,1,0:T(8,128)S(1)} %get-tuple-element.48.refs_1_, bf16[25,64,128]{2,1,0:T(8,128)(2,1)} %collective-permute-done.7.refs_2_, bf16[27,64,128]{2,1,0:T(8,128)(2,1)S(1)} %copy-done.7, ...), custom_call_target="tpu_custom_call" | custom-call | flops 6553600 | bytes 5242880 | tf_op jit(solution)/shard_map/finish4/pallas_call | solution.py:662
  227.9 6.9 %all-to-all-done.1 = f32[16,3,8,128]{3,2,1,0:T(8,128)} async-done(((f32[16,3,8,128]{3,2,1,0:T(8,128)}), f32[16,3,8,128]{3,2,1,0:T(8,128)}, u32[]{:S(2)}, u32[]{:S(2)}) %all-to-all-start.1) | async-done | bytes 196640 | tf_op jit(solution)/shard_map/all_to_all | solution.py:778
  234.9 0.9 reduce_sum.9
  235.8 3.7 %collective-permute-start.8 = (f32[3,8,128]{2,1,0:T(8,128)S(1)}, f32[3,8,128]{2,1,0:T(8,128)S(1)}, u32[]{:S(2)}, u32[]{:S(2)}) collective-permute-start(f32[3,8,128]{2,1,0:T(8,128)S(1)} %reduce_sum.9), channel_id=1, source_target_pairs={{0,16},{16,0},{32,48},{48,32},{64,80},{80,64},{96,112},{112,96},{1... | collective-permute-start | bytes 36872 | tf_op jit(solution)/shard_map/ppermute | solution.py:585
  239.5 0.8 collective-permute-done.8
  240.4 0.6 reshape.171
  (82 shorter events, 0.5 us)
Async XLA Ops:
  0.6 1.2 copy-start.12
  1.9 0.7 copy-start.23
  2.5 0.7 copy-start.24
  6.1 19.4 %copy-start.28 = (f32[64,8,128]{2,1,0:T(8,128)S(1)}, f32[64,8,128]{2,1,0:T(8,128)}, u32[]{:S(2)}) copy-start(f32[64,8,128]{2,1,0:T(8,128)} %param.16) | copy-start | bytes 786436
  6.1 136.0 %all-to-all-start = ((bf16[32,272,128]{2,1,0:T(8,128)(2,1)}), bf16[32,272,128]{2,1,0:T(8,128)(2,1)}, u32[]{:S(2)}, u32[]{:S(2)}) async-start(bf16[32,272,128]{2,1,0:T(8,128)(2,1)} %pack.1), calls=%async_computation | async-start | bytes 4456448 | tf_op jit(solution)/shard_map/all_to_all | solution.py:617
  25.5 1.0 copy-start.25
  25.7 2.4 %copy-start.26 = (f32[64,8,128]{2,0,1:T(8,128)}, f32[64,8,128]{2,0,1:T(8,128)S(1)}, u32[]{:S(2)}) copy-start(f32[64,8,128]{2,0,1:T(8,128)S(1)} %copy.91) | copy-start | bytes 786436
  28.1 10.6 %copy-start.34 = (s32[3]{0:T(128)S(1)}, s32[3]{0:T(128)}, u32[]{:S(2)}) copy-start(s32[3]{0:T(128)} %param.25) | copy-start | bytes 40
  28.2 11.9 %copy-start.32 = (bf16[64,8,128]{2,1,0:T(8,128)(2,1)S(1)}, bf16[64,8,128]{2,1,0:T(8,128)(2,1)}, u32[]{:S(2)}) copy-start(bf16[64,8,128]{2,1,0:T(8,128)(2,1)} %param.17) | copy-start | bytes 393220
  28.2 11.9 %copy-start.30 = (bf16[3,64,8,128]{3,2,1,0:T(8,128)(2,1)S(1)}, bf16[3,64,8,128]{3,2,1,0:T(8,128)(2,1)}, u32[]{:S(2)}) copy-start(bf16[3,64,8,128]{3,2,1,0:T(8,128)(2,1)} %param.18) | copy-start | bytes 1179652
  29.2 30.3 %collective-permute-start.1 = (bf16[21,64,128]{2,1,0:T(8,128)(2,1)}, bf16[21,64,128]{2,1,0:T(8,128)(2,1)}, u32[]{:S(2)}, u32[]{:S(2)}) collective-permute-start(bf16[21,64,128]{2,1,0:T(8,128)(2,1)} %get-tuple-element.52), channel_id=1, source_target_pairs={{0,16},{16,0},{32,48},{48,32},{64,80},{80,64},{96,112},{112,96},{1... | collective-permute-start | bytes 1032200 | tf_op jit(solution)/shard_map/ppermute | solution.py:585
  31.4 110.8 %collective-permute-start = (bf16[21,64,128]{2,1,0:T(8,128)(2,1)}, bf16[21,64,128]{2,1,0:T(8,128)(2,1)}, u32[]{:S(2)}, u32[]{:S(2)}) collective-permute-start(bf16[21,64,128]{2,1,0:T(8,128)(2,1)} %get-tuple-element.53), channel_id=1, source_target_pairs={{16,32},{48,64},{80,96},{112,128},{144,160},{176,192},{208,224},{2... | collective-permute-start | bytes 1032200 | tf_op jit(solution)/shard_map/ppermute | solution.py:579
  40.3 10.6 %copy-start = (f32[4,8,64,128]{3,2,1,0:T(8,128)}, f32[4,8,64,128]{3,2,1,0:T(8,128)S(1)}, u32[]{:S(2)}) copy-start(f32[4,8,64,128]{3,2,1,0:T(8,128)S(1)} %maximum_bitcast_fusion.coef.refs_6_.refs_3_.refs_5_.refs_4_) | copy-start | bytes 3145732
  40.3 1.4 copy-start.29
  40.4 2.9 %copy-start.31 = (f32[64,8,128]{2,1,0:T(8,128)S(1)}, f32[64,8,128]{2,1,0:T(8,128)}, u32[]{:S(2)}) copy-start(f32[64,8,128]{2,1,0:T(8,128)} %param.15) | copy-start | bytes 786436
  41.8 1.6 copy-start.20
  41.8 1.6 copy-start.21
  41.8 1.6 copy-start.22
  43.3 7.6 %copy-start.17 = (s32[4]{0:T(128)}, s32[4]{0:T(128)S(1)}, u32[]{:S(2)}) copy-start(s32[4]{0:T(128)S(1)} %pad_add_fusion.src.refs_0_) | copy-start | bytes 52
  49.8 0.6 copy-start.14
  49.8 1.0 copy-start.27
  50.8 0.9 copy-start.11
  50.8 0.9 copy-start.19
  57.6 1.1 copy-start.10
  58.7 0.7 copy-start.16
  142.2 15.1 %copy-start.1 = (f32[4,8,64,128]{3,2,1,0:T(8,128)S(1)}, f32[4,8,64,128]{3,2,1,0:T(8,128)}, u32[]{:S(2)}) copy-start(f32[4,8,64,128]{3,2,1,0:T(8,128)} %copy-done) | copy-start | bytes 3145732
  142.2 15.2 %copy-start.15 = (s32[8,256]{1,0:T(8,128)S(1)}, s32[8,256]{1,0:T(8,128)}, u32[]{:S(2)}) copy-start(s32[8,256]{1,0:T(8,128)} %copy-done.14) | copy-start | bytes 24580
  142.2 15.2 %copy-start.18 = (s32[4]{0:T(128)S(1)}, s32[4]{0:T(128)}, u32[]{:S(2)}) copy-start(s32[4]{0:T(128)} %copy-done.17) | copy-start | bytes 52
  150.4 20.8 %collective-permute-start.2 = (bf16[25,64,128]{2,1,0:T(8,128)(2,1)}, bf16[25,64,128]{2,1,0:T(8,128)(2,1)S(1)}, u32[]{:S(2)}, u32[]{:S(2)}) collective-permute-start(bf16[25,64,128]{2,1,0:T(8,128)(2,1)} %get-tuple-element.33), channel_id=1, source_target_pairs={{16,32},{48,64},{80,96},{112,128},{144,160},{176,192},{208,224},{2... | collective-permute-start | bytes 1228808 | tf_op jit(solution)/shard_map/ppermute | solution.py:579
  155.4 15.8 %collective-permute-start.3 = (bf16[25,64,128]{2,1,0:T(8,128)(2,1)}, bf16[25,64,128]{2,1,0:T(8,128)(2,1)S(1)}, u32[]{:S(2)}, u32[]{:S(2)}) collective-permute-start(bf16[25,64,128]{2,1,0:T(8,128)(2,1)} %get-tuple-element.34), channel_id=1, source_target_pairs={{0,16},{16,0},{32,48},{48,32},{64,80},{80,64},{96,112},{112,96},{1... | collective-permute-start | bytes 1228808 | tf_op jit(solution)/shard_map/ppermute | solution.py:585
  157.4 1.2 copy-start.2
  158.6 1.3 copy-start.4
  159.9 11.3 %copy-start.3 = (f32[4,8,64,128]{3,2,1,0:T(8,128)S(1)}, f32[4,8,64,128]{3,2,1,0:T(8,128)}, u32[]{:S(2)}) copy-start(f32[4,8,64,128]{3,2,1,0:T(8,128)} %get-tuple-element.30.refs_5_.refs_6_.refs_4_) | copy-start | bytes 3145732
  171.2 7.8 %copy-start.33 = (f32[2,8,128]{2,1,0:T(8,128)S(1)}, f32[2,8,128]{2,1,0:T(8,128)}, u32[]{:S(2)}) copy-start(f32[2,8,128]{2,1,0:T(8,128)} %get-tuple-element.41) | copy-start | bytes 24580
  171.2 7.8 %copy-start.5 = (f32[5,8,64,128]{3,2,1,0:T(8,128)S(1)}, f32[5,8,64,128]{3,2,1,0:T(8,128)}, u32[]{:S(2)}) copy-start(f32[5,8,64,128]{3,2,1,0:T(8,128)} %get-tuple-element.29.refs_1_.prev) | copy-start | bytes 3932164
  173.2 21.6 %collective-permute-start.4 = (bf16[26,64,128]{2,1,0:T(8,128)(2,1)S(1)}, bf16[26,64,128]{2,1,0:T(8,128)(2,1)S(1)}, u32[]{:S(2)}, u32[]{:S(2)}) collective-permute-start(bf16[26,64,128]{2,1,0:T(8,128)(2,1)S(1)} %get-tuple-element.39), channel_id=1, source_target_pairs={{16,32},{48,64},{80,96},{112,128},{144,160},{176,192},{208,224},{2... | collective-permute-start | bytes 1277960 | tf_op jit(solution)/shard_map/ppermute | solution.py:579
  177.1 17.7 %collective-permute-start.5 = (bf16[26,64,128]{2,1,0:T(8,128)(2,1)S(1)}, bf16[26,64,128]{2,1,0:T(8,128)(2,1)S(1)}, u32[]{:S(2)}, u32[]{:S(2)}) collective-permute-start(bf16[26,64,128]{2,1,0:T(8,128)(2,1)S(1)} %get-tuple-element.40), channel_id=1, source_target_pairs={{0,16},{16,0},{32,48},{48,32},{64,80},{80,64},{96,112},{112,96},{1... | collective-permute-start | bytes 1277960 | tf_op jit(solution)/shard_map/ppermute | solution.py:585
  197.6 13.5 %copy-start.8 = (f32[5,8,64,128]{3,2,1,0:T(8,128)}, f32[5,8,64,128]{3,2,1,0:T(8,128)S(1)}, u32[]{:S(2)}) copy-start(f32[5,8,64,128]{3,2,1,0:T(8,128)S(1)} %get-tuple-element.45.refs_1_.cur) | copy-start | bytes 3932164
  197.6 13.5 %collective-permute-start.6 = (bf16[27,64,128]{2,1,0:T(8,128)(2,1)S(1)}, bf16[27,64,128]{2,1,0:T(8,128)(2,1)S(1)}, u32[]{:S(2)}, u32[]{:S(2)}) collective-permute-start(bf16[27,64,128]{2,1,0:T(8,128)(2,1)S(1)} %get-tuple-element.43), channel_id=1, source_target_pairs={{0,16},{16,0},{32,48},{48,32},{64,80},{80,64},{96,112},{112,96},{1... | collective-permute-start | bytes 1327112 | tf_op jit(solution)/shard_map/ppermute | solution.py:585
  199.5 25.6 %collective-permute-start.7 = (bf16[25,64,128]{2,1,0:T(8,128)(2,1)}, bf16[25,64,128]{2,1,0:T(8,128)(2,1)}, u32[]{:S(2)}, u32[]{:S(2)}) collective-permute-start(bf16[25,64,128]{2,1,0:T(8,128)(2,1)} %get-tuple-element.49), channel_id=1, source_target_pairs={{16,32},{48,64},{80,96},{112,128},{144,160},{176,192},{208,224},{2... | collective-permute-start | bytes 1228808 | tf_op jit(solution)/shard_map/ppermute | solution.py:579
  211.6 0.8 copy-start.6
  212.4 0.7 copy-start.13
  213.1 21.8 %all-to-all-start.1 = ((f32[16,3,8,128]{3,2,1,0:T(8,128)}), f32[16,3,8,128]{3,2,1,0:T(8,128)}, u32[]{:S(2)}, u32[]{:S(2)}) async-start(f32[16,3,8,128]{3,2,1,0:T(8,128)} %copy-done.13), calls=%async_computation.1 | async-start | bytes 393216 | tf_op jit(solution)/shard_map/all_to_all | solution.py:778
  217.8 1.3 copy-start.9
  219.1 6.0 %copy-start.7 = (bf16[27,64,128]{2,1,0:T(8,128)(2,1)S(1)}, bf16[27,64,128]{2,1,0:T(8,128)(2,1)}, u32[]{:S(2)}) copy-start(bf16[27,64,128]{2,1,0:T(8,128)(2,1)} %copy-done.6) | copy-start | bytes 1327108
  235.8 4.5 %collective-permute-start.8 = (f32[3,8,128]{2,1,0:T(8,128)S(1)}, f32[3,8,128]{2,1,0:T(8,128)S(1)}, u32[]{:S(2)}, u32[]{:S(2)}) collective-permute-start(f32[3,8,128]{2,1,0:T(8,128)S(1)} %reduce_sum.9), channel_id=1, source_target_pairs={{0,16},{16,0},{32,48},{48,32},{64,80},{80,64},{96,112},{112,96},{1... | collective-permute-start | bytes 36872 | tf_op jit(solution)/shard_map/ppermute | solution.py:585

commit v6 on v5

--- a/solution.py
+++ b/solution.py
@@ -506,7 +506,7 @@
 
         return c
 
-    lax.fori_loop(0, incoming.shape[0] * CAP, add, 0)
+    lax.fori_loop(0, incoming.shape[0] * CAP, add, 0, unroll=8)
     for load in loads[:5]:
         load.wait()
 

time: 245 us -> 247 us (level)
  the two profiles are of different devices: /device:TPU:1 before, /device:TPU:73 now
where the time goes in v6:
time: 247 us; the launch traced here: 246 us
  waiting for transfers between devices  89.2 us (36%)
  starting transfers between devices  80.7 us (33%)
  Pallas kernels  54 us (22%)
  local copies, waits for them, and re-layouts  16.3 us (7%)
  other arithmetic  4.11 us (2%)
    ppermute x4, waiting for transfers between devices, exchange(): there = lax.ppermute(away, 'tile', pairs + [(b, a) for a, b in pairs])  80.2 us
    pallas_call x10, Pallas kernels, call(): pl.pallas_call(kernel, out_shape=out_shape, in_specs=[sspec()] * len(scal...  44.6 us
    ppermute x4, starting transfers between devices, exchange(): there = lax.ppermute(away, 'tile', pairs + [(b, a) for a, b in pairs])  35.7 us
    all_to_all x1, starting transfers between devices, local(): incoming = lax.all_to_all(packed, 'tile', 0, 0, tiled=True)  16.8 us
    ppermute x5, starting transfers between devices, swap(): return lax.ppermute(value, 'tile', [(i, i ^ 1) for i in range(count)])  14.9 us
    unnamed x85, local copies, waits for them, and re-layouts  13.7 us
    all_to_all x1, starting transfers between devices, local(): lax.all_to_all(sent, 'tile', 0, 0, axis_index_groups=groups, tiled=True)  13.3 us
    pallas_call x1, Pallas kernels, list_receivers(): pl.pallas_call(list_kernel, out_shape=jax.ShapeDtypeStruct((8, n), jnp.in...  6.43 us
  transfers between devices with their start and end apart: 11, of which 5 were waited for; matrix products, arithmetic and copies ran while one was open for 2% of the time, Pallas kernels for 15%

profile of v6, /device:TPU:73, one launch (start us, length us, event | category | flops | bytes accessed | tf_op | source)
XLA Modules:
  0.0 246.3 jit_solution(14588872975374290638)
XLA Ops:
  0.6 1.2 copy-done.12
  1.9 0.7 copy-done.23
  2.5 0.7 copy-done.24
  3.2 3.0 %pack.1 = bf16[32,272,128]{2,1,0:T(8,128)(2,1)} custom-call(s32[32]{0:T(128)S(1)} %bitcast.103, s32[32]{0:T(128)S(1)} %copy-done.24, bf16[4,32,32,128]{3,2,1,0:T(8,128)(2,1)S(1)} %copy-done.12), custom_call_target="tpu_custom_call" | custom-call | tf_op jit(solution)/shard_map/pack/pallas_call | solution.py:85
  6.1 16.8 %all-to-all-start = ((bf16[32,272,128]{2,1,0:T(8,128)(2,1)}), bf16[32,272,128]{2,1,0:T(8,128)(2,1)}, u32[]{:S(2)}, u32[]{:S(2)}) async-start(bf16[32,272,128]{2,1,0:T(8,128)(2,1)} %pack.1), calls=%async_computation | async-start | bytes 4456448 | tf_op jit(solution)/shard_map/all_to_all | solution.py:617
  22.9 0.0 copy-start.25
  22.9 0.1 copy.80
  23.0 0.1 copy.91
  23.1 0.9 copy-done.25
  24.0 1.2 fusion.5
  25.5 0.0 copy-start.34
  25.5 0.0 copy-start.32
  25.6 0.1 constant_dynamic-update-slice_fusion
  25.7 0.9 broadcast_select_fusion
  26.6 2.2 collective-permute-start.1
  28.8 7.3 %collective-permute-start = (bf16[21,64,128]{2,1,0:T(8,128)(2,1)}, bf16[21,64,128]{2,1,0:T(8,128)(2,1)}, u32[]{:S(2)}, u32[]{:S(2)}) collective-permute-start(bf16[21,64,128]{2,1,0:T(8,128)(2,1)} %get-tuple-element.53), channel_id=1, source_target_pairs={{16,32},{48,64},{80,96},{112,128},{144,160},{176,192},{208,224},{2... | collective-permute-start | bytes 1032200 | tf_op jit(solution)/shard_map/ppermute | solution.py:579
  36.1 0.6 fusion.7
  37.4 0.1 pad_add_fusion.1.where
  37.5 0.1 convert_multiply_fusion
  37.6 0.1 maximum_bitcast_fusion.coef.refs_6_.refs_3_.refs_5_.refs_4_
  37.7 0.0 copy-start
  37.7 0.1 convert_bitcast_fusion.1
  37.9 1.3 copy-done.29
  39.1 0.1 convert_bitcast_fusion
  39.3 1.4 pad_add_fusion.src.refs_0_
  40.6 0.1 copy.82
  40.7 6.4 %receivers.1.refs_1_.refs_0_ = s32[8,256]{1,0:T(8,128)S(1)} custom-call(s32[256]{0:T(256)S(1)} %copy-done.20, s32[256]{0:T(256)S(1)} %copy-done.21, s32[256]{0:T(256)S(1)} %copy-done.22, s32[3]{0:T(128)S(1)} %pad_add_fusion.1.where), custom_call_target="tpu_custom_call" | custom-call | tf_op jit(solution)/shard_map/receivers/pallas_call | solution.py:125
  47.2 0.1 pad_maximum_fusion.1.prev
  47.3 0.5 copy-done.14
  47.8 0.4 copy-done.27
  48.1 0.1 pad_maximum_fusion.cur.refs_2_
  48.3 0.7 copy-done.11
  49.0 6.0 %own1.1 = (f32[5,8,64,128]{3,2,1,0:T(8,128)S(1)}, f32[8,64,128]{2,1,0:T(8,128)S(1)}) custom-call(f32[4]{0:T(128)S(1)} %copy-done.19, s32[4]{0:T(128)S(1)} %pad_add_fusion.src.refs_0_, f32[5,8,64,128]{3,2,1,0:T(8,128)S(1)} %pad_maximum_fusion.cur.refs_2_, f32[5,8,64,128]{3,2,1,0:T(8,128)S(1)} %pad_maximum_fusion.1.prev, ...), custom_call_target="tpu_custom_call" | custom-call | flops 26214400 | bytes 5242880 | tf_op jit(solution)/shard_map/own1/pallas_call | solution.py:662
  55.0 1.1 copy-done.10
  56.1 0.7 copy-done.16
  56.8 73.1 %collective-permute-done.refs_4_ = bf16[21,64,128]{2,1,0:T(8,128)(2,1)} collective-permute-done((bf16[21,64,128]{2,1,0:T(8,128)(2,1)}, bf16[21,64,128]{2,1,0:T(8,128)(2,1)}, u32[]{:S(2)}, u32[]{:S(2)}) %collective-permute-start) | collective-permute-done | bytes 344096 | tf_op jit(solution)/shard_map/ppermute | solution.py:579
  130.0 2.9 %all-to-all-done.refs_7_ = bf16[32,272,128]{2,1,0:T(8,128)(2,1)} async-done(((bf16[32,272,128]{2,1,0:T(8,128)(2,1)}), bf16[32,272,128]{2,1,0:T(8,128)(2,1)}, u32[]{:S(2)}, u32[]{:S(2)}) %all-to-all-start) | async-done | bytes 2228256 | tf_op jit(solution)/shard_map/all_to_all | solution.py:617
  132.9 8.1 %finish1.1 = (f32[5,8,64,128]{3,2,1,0:T(8,128)}, f32[4,8,64,128]{3,2,1,0:T(8,128)}, bf16[25,64,128]{2,1,0:T(8,128)(2,1)}, bf16[25,64,128]{2,1,0:T(8,128)(2,1)}, f32[2,8,128]{2,1,0:T(8,128)}) custom-call(s32[4]{0:T(128)} %copy-done.17, s32[8,256]{1,0:T(8,128)} %copy-done.14, f32[5,8,64,128]{3,2,1,0:T(8,128)} %copy-done.10, f32[8,64,128]{2,1,0:T(8,128)} %copy-done.16, ...), custom_call_target="tpu_custom_call" | custom-call | flops 6553600 | bytes 5242880 | tf_op jit(solution)/shard_map/finish1/pallas_call | solution.py:662
  141.0 2.6 %collective-permute-start.2 = (bf16[25,64,128]{2,1,0:T(8,128)(2,1)}, bf16[25,64,128]{2,1,0:T(8,128)(2,1)S(1)}, u32[]{:S(2)}, u32[]{:S(2)}) collective-permute-start(bf16[25,64,128]{2,1,0:T(8,128)(2,1)} %get-tuple-element.33), channel_id=1, source_target_pairs={{16,32},{48,64},{80,96},{112,128},{144,160},{176,192},{208,224},{2... | collective-permute-start | bytes 1228808 | tf_op jit(solution)/shard_map/ppermute | solution.py:579
  143.7 7.0 %collective-permute-start.3 = (bf16[25,64,128]{2,1,0:T(8,128)(2,1)}, bf16[25,64,128]{2,1,0:T(8,128)(2,1)S(1)}, u32[]{:S(2)}, u32[]{:S(2)}) collective-permute-start(bf16[25,64,128]{2,1,0:T(8,128)(2,1)} %get-tuple-element.34), channel_id=1, source_target_pairs={{0,16},{16,0},{32,48},{48,32},{64,80},{80,64},{96,112},{112,96},{1... | collective-permute-start | bytes 1228808 | tf_op jit(solution)/shard_map/ppermute | solution.py:585
  150.7 1.2 copy-done.2
  151.9 1.3 copy-done.4
  153.2 6.7 %own2.1 = (f32[5,8,64,128]{3,2,1,0:T(8,128)S(1)}, f32[8,64,128]{2,1,0:T(8,128)S(1)}, bf16[64,128]{1,0:T(8,128)(2,1)S(1)}) custom-call(f32[4]{0:T(128)S(1)} %copy-done.19, s32[4]{0:T(128)S(1)} %copy-done.18, s32[8,256]{1,0:T(8,128)S(1)} %copy-done.15, f32[5,8,64,128]{3,2,1,0:T(8,128)S(1)} %copy-done.4, f32[5,8,64,128]{3,2,1,0:T(8,128)S(1)} %pad_maximum_fusion.cur.refs_2_, ...), custom_call_target="tpu_custom_call" | custom-call | flops 26214400 | bytes 5242880 | tf_op jit(solution)/shard_map/own2/pallas_call | solution.py:662
  159.9 2.2 finish2.1
  162.1 10.3 %collective-permute-start.4 = (bf16[26,64,128]{2,1,0:T(8,128)(2,1)S(1)}, bf16[26,64,128]{2,1,0:T(8,128)(2,1)S(1)}, u32[]{:S(2)}, u32[]{:S(2)}) collective-permute-start(bf16[26,64,128]{2,1,0:T(8,128)(2,1)S(1)} %get-tuple-element.39), channel_id=1, source_target_pairs={{16,32},{48,64},{80,96},{112,128},{144,160},{176,192},{208,224},{2... | collective-permute-start | bytes 1277960 | tf_op jit(solution)/shard_map/ppermute | solution.py:579
  172.4 1.9 collective-permute-start.5
  174.4 6.0 %own3.1 = (f32[5,8,64,128]{3,2,1,0:T(8,128)S(1)}, f32[8,64,128]{2,1,0:T(8,128)S(1)}) custom-call(f32[4]{0:T(128)S(1)} %copy-done.19, s32[4]{0:T(128)S(1)} %copy-done.18, f32[5,8,64,128]{3,2,1,0:T(8,128)S(1)} %get-tuple-element.36.cur.refs_2_.prev, f32[5,8,64,128]{3,2,1,0:T(8,128)S(1)} %copy-done.5, f32[4,8,64,128]{3,2,1,0:T(8,128)S(1)} %copy-done.1, ...), custom_call_target="tpu_custom_call" | custom-call | flops 26214400 | bytes 5242880 | tf_op jit(solution)/shard_map/own3/pallas_call | solution.py:662
  180.4 7.1 %collective-permute-done.4.refs_3_ = bf16[26,64,128]{2,1,0:T(8,128)(2,1)S(1)} collective-permute-done((bf16[26,64,128]{2,1,0:T(8,128)(2,1)S(1)}, bf16[26,64,128]{2,1,0:T(8,128)(2,1)S(1)}, u32[]{:S(2)}, u32[]{:S(2)}) %collective-permute-start.4) | collective-permute-done | bytes 426016 | tf_op jit(solution)/shard_map/ppermute | solution.py:579
  187.5 2.9 %finish3.1 = (f32[5,8,64,128]{3,2,1,0:T(8,128)S(1)}, bf16[25,64,128]{2,1,0:T(8,128)(2,1)}, bf16[27,64,128]{2,1,0:T(8,128)(2,1)S(1)}, f32[2,8,128]{2,1,0:T(8,128)S(1)}, f32[16,128]{1,0:T(8,128)S(1)}) custom-call(s32[4]{0:T(128)S(1)} %copy-done.18, s32[8,256]{1,0:T(8,128)S(1)} %copy-done.15, f32[5,8,64,128]{3,2,1,0:T(8,128)S(1)} %get-tuple-element.37.refs_1_, ...), custom_call_target="tpu_custom_call" | custom-call | flops 6553600 | bytes 5242880 | tf_op jit(solution)/shard_map/finish3/pallas_call | solution.py:662
  190.4 1.9 collective-permute-start.6
  192.3 15.5 %collective-permute-start.7 = (bf16[25,64,128]{2,1,0:T(8,128)(2,1)}, bf16[25,64,128]{2,1,0:T(8,128)(2,1)}, u32[]{:S(2)}, u32[]{:S(2)}) collective-permute-start(bf16[25,64,128]{2,1,0:T(8,128)(2,1)} %get-tuple-element.49), channel_id=1, source_target_pairs={{16,32},{48,64},{80,96},{112,128},{144,160},{176,192},{208,224},{2... | collective-permute-start | bytes 1228808 | tf_op jit(solution)/shard_map/ppermute | solution.py:579
  207.8 3.5 %share.1.mine = f32[8,128]{1,0:T(8,128)S(1)} custom-call(s32[8,256]{1,0:T(8,128)S(1)} %copy-done.15, f32[5,8,64,128]{3,2,1,0:T(8,128)S(1)} %get-tuple-element.45.refs_1_.cur, f32[5,8,64,128]{3,2,1,0:T(8,128)S(1)} %get-tuple-element.36.cur.refs_2_.prev, f32[4,8,64,128]{3,2,1,0:T(8,128)S(1)} %copy-done.1, f32[4,8,64,128]{3,2,1,0:T(8,128)S(1)} %copy-done.3, ...), custom_call_target="tpu_custom_call" | custom-call | flops 6553600 | bytes 5242880 | tf_op jit(solution)/shard_map/share/pallas_call | solution.py:662
  211.3 0.6 message.1
  211.9 0.8 copy-done.6
  212.7 0.7 copy-done.13
  213.3 13.3 %all-to-all-start.1 = ((f32[16,3,8,128]{3,2,1,0:T(8,128)}), f32[16,3,8,128]{3,2,1,0:T(8,128)}, u32[]{:S(2)}, u32[]{:S(2)}) async-start(f32[16,3,8,128]{3,2,1,0:T(8,128)} %copy-done.13), calls=%async_computation.1 | async-start | bytes 393216 | tf_op jit(solution)/shard_map/all_to_all | solution.py:778
  226.7 1.3 copy-done.9
  228.0 6.0 %own4.1 = (f32[5,8,64,128]{3,2,1,0:T(8,128)S(1)}, f32[8,64,128]{2,1,0:T(8,128)S(1)}) custom-call(f32[4]{0:T(128)S(1)} %copy-done.19, s32[4]{0:T(128)S(1)} %copy-done.18, f32[5,8,64,128]{3,2,1,0:T(8,128)S(1)} %copy-done.9, f32[5,8,64,128]{3,2,1,0:T(8,128)S(1)} %get-tuple-element.36.cur.refs_2_.prev, f32[4,8,64,128]{3,2,1,0:T(8,128)S(1)} %copy-done.1, ...), custom_call_target="tpu_custom_call" | custom-call | flops 26214400000 | bytes 5242880 | tf_op jit(solution)/shard_map/own4/pallas_call | solution.py:662
  234.0 2.8 %finish4.1 = f32[4,512,128]{2,1,0:T(8,128)} custom-call(s32[4]{0:T(128)S(1)} %copy-done.18, f32[5,8,64,128]{3,2,1,0:T(8,128)S(1)} %get-tuple-element.47.refs_0_, f32[8,64,128]{2,1,0:T(8,128)S(1)} %get-tuple-element.48.refs_1_, bf16[25,64,128]{2,1,0:T(8,128)(2,1)} %collective-permute-done.7.refs_2_, bf16[27,64,128]{2,1,0:T(8,128)(2,1)S(1)} %copy-done.7, ...), custom_call_target="tpu_custom_call" | custom-call | flops 6553600 | bytes 5242880 | tf_op jit(solution)/shard_map/finish4/pallas_call | solution.py:662
  236.8 4.8 %all-to-all-done.1 = f32[16,3,8,128]{3,2,1,0:T(8,128)} async-done(((f32[16,3,8,128]{3,2,1,0:T(8,128)}), f32[16,3,8,128]{3,2,1,0:T(8,128)}, u32[]{:S(2)}, u32[]{:S(2)}) %all-to-all-start.1) | async-done | bytes 196640 | tf_op jit(solution)/shard_map/all_to_all | solution.py:778
  241.6 0.9 reduce_sum.9
  242.6 1.9 collective-permute-start.8
  244.5 1.1 collective-permute-done.8
  245.7 0.6 reshape.171
  (82 shorter events, 0.5 us)
Async XLA Ops:
  0.6 1.2 copy-start.12
  1.9 0.7 copy-start.23
  2.5 0.7 copy-start.24
  6.1 16.8 %copy-start.28 = (f32[64,8,128]{2,1,0:T(8,128)S(1)}, f32[64,8,128]{2,1,0:T(8,128)}, u32[]{:S(2)}) copy-start(f32[64,8,128]{2,1,0:T(8,128)} %param.16) | copy-start | bytes 786436
  6.1 126.8 %all-to-all-start = ((bf16[32,272,128]{2,1,0:T(8,128)(2,1)}), bf16[32,272,128]{2,1,0:T(8,128)(2,1)}, u32[]{:S(2)}, u32[]{:S(2)}) async-start(bf16[32,272,128]{2,1,0:T(8,128)(2,1)} %pack.1), calls=%async_computation | async-start | bytes 4456448 | tf_op jit(solution)/shard_map/all_to_all | solution.py:617
  22.9 1.0 copy-start.25
  23.1 2.4 copy-start.26
  25.5 10.6 %copy-start.34 = (s32[3]{0:T(128)S(1)}, s32[3]{0:T(128)}, u32[]{:S(2)}) copy-start(s32[3]{0:T(128)} %param.25) | copy-start | bytes 40
  25.5 11.9 %copy-start.32 = (bf16[64,8,128]{2,1,0:T(8,128)(2,1)S(1)}, bf16[64,8,128]{2,1,0:T(8,128)(2,1)}, u32[]{:S(2)}) copy-start(bf16[64,8,128]{2,1,0:T(8,128)(2,1)} %param.17) | copy-start | bytes 393220
  25.6 11.9 %copy-start.30 = (bf16[3,64,8,128]{3,2,1,0:T(8,128)(2,1)S(1)}, bf16[3,64,8,128]{3,2,1,0:T(8,128)(2,1)}, u32[]{:S(2)}) copy-start(bf16[3,64,8,128]{3,2,1,0:T(8,128)(2,1)} %param.18) | copy-start | bytes 1179652
  26.6 30.3 %collective-permute-start.1 = (bf16[21,64,128]{2,1,0:T(8,128)(2,1)}, bf16[21,64,128]{2,1,0:T(8,128)(2,1)}, u32[]{:S(2)}, u32[]{:S(2)}) collective-permute-start(bf16[21,64,128]{2,1,0:T(8,128)(2,1)} %get-tuple-element.52), channel_id=1, source_target_pairs={{0,16},{16,0},{32,48},{48,32},{64,80},{80,64},{96,112},{112,96},{1... | collective-permute-start | bytes 1032200 | tf_op jit(solution)/shard_map/ppermute | solution.py:585
  28.8 101.2 %collective-permute-start = (bf16[21,64,128]{2,1,0:T(8,128)(2,1)}, bf16[21,64,128]{2,1,0:T(8,128)(2,1)}, u32[]{:S(2)}, u32[]{:S(2)}) collective-permute-start(bf16[21,64,128]{2,1,0:T(8,128)(2,1)} %get-tuple-element.53), channel_id=1, source_target_pairs={{16,32},{48,64},{80,96},{112,128},{144,160},{176,192},{208,224},{2... | collective-permute-start | bytes 1032200 | tf_op jit(solution)/shard_map/ppermute | solution.py:579
  37.7 10.6 %copy-start = (f32[4,8,64,128]{3,2,1,0:T(8,128)}, f32[4,8,64,128]{3,2,1,0:T(8,128)S(1)}, u32[]{:S(2)}) copy-start(f32[4,8,64,128]{3,2,1,0:T(8,128)S(1)} %maximum_bitcast_fusion.coef.refs_6_.refs_3_.refs_5_.refs_4_) | copy-start | bytes 3145732
  37.7 1.4 copy-start.29
  37.7 2.9 %copy-start.31 = (f32[64,8,128]{2,1,0:T(8,128)S(1)}, f32[64,8,128]{2,1,0:T(8,128)}, u32[]{:S(2)}) copy-start(f32[64,8,128]{2,1,0:T(8,128)} %param.15) | copy-start | bytes 786436
  39.1 1.6 copy-start.20
  39.1 1.6 copy-start.21
  39.1 1.6 copy-start.22
  40.6 7.6 %copy-start.17 = (s32[4]{0:T(128)}, s32[4]{0:T(128)S(1)}, u32[]{:S(2)}) copy-start(s32[4]{0:T(128)S(1)} %pad_add_fusion.src.refs_0_) | copy-start | bytes 52
  47.2 0.6 copy-start.14
  47.2 1.0 copy-start.27
  48.1 0.9 copy-start.11
  48.1 0.9 copy-start.19
  55.0 1.1 copy-start.10
  56.1 0.7 copy-start.16
  132.9 17.7 %copy-start.1 = (f32[4,8,64,128]{3,2,1,0:T(8,128)S(1)}, f32[4,8,64,128]{3,2,1,0:T(8,128)}, u32[]{:S(2)}) copy-start(f32[4,8,64,128]{3,2,1,0:T(8,128)} %copy-done) | copy-start | bytes 3145732
  132.9 17.7 %copy-start.15 = (s32[8,256]{1,0:T(8,128)S(1)}, s32[8,256]{1,0:T(8,128)}, u32[]{:S(2)}) copy-start(s32[8,256]{1,0:T(8,128)} %copy-done.14) | copy-start | bytes 24580
  132.9 17.7 %copy-start.18 = (s32[4]{0:T(128)S(1)}, s32[4]{0:T(128)}, u32[]{:S(2)}) copy-start(s32[4]{0:T(128)} %copy-done.17) | copy-start | bytes 52
  141.0 18.8 %collective-permute-start.2 = (bf16[25,64,128]{2,1,0:T(8,128)(2,1)}, bf16[25,64,128]{2,1,0:T(8,128)(2,1)S(1)}, u32[]{:S(2)}, u32[]{:S(2)}) collective-permute-start(bf16[25,64,128]{2,1,0:T(8,128)(2,1)} %get-tuple-element.33), channel_id=1, source_target_pairs={{16,32},{48,64},{80,96},{112,128},{144,160},{176,192},{208,224},{2... | collective-permute-start | bytes 1228808 | tf_op jit(solution)/shard_map/ppermute | solution.py:579
  143.7 16.2 %collective-permute-start.3 = (bf16[25,64,128]{2,1,0:T(8,128)(2,1)}, bf16[25,64,128]{2,1,0:T(8,128)(2,1)S(1)}, u32[]{:S(2)}, u32[]{:S(2)}) collective-permute-start(bf16[25,64,128]{2,1,0:T(8,128)(2,1)} %get-tuple-element.34), channel_id=1, source_target_pairs={{0,16},{16,0},{32,48},{48,32},{64,80},{80,64},{96,112},{112,96},{1... | collective-permute-start | bytes 1228808 | tf_op jit(solution)/shard_map/ppermute | solution.py:585
  150.7 1.2 copy-start.2
  151.9 1.3 copy-start.4
  153.2 6.7 %copy-start.3 = (f32[4,8,64,128]{3,2,1,0:T(8,128)S(1)}, f32[4,8,64,128]{3,2,1,0:T(8,128)}, u32[]{:S(2)}) copy-start(f32[4,8,64,128]{3,2,1,0:T(8,128)} %get-tuple-element.30.refs_5_.refs_6_.refs_4_) | copy-start | bytes 3145732
  159.9 14.5 %copy-start.33 = (f32[2,8,128]{2,1,0:T(8,128)S(1)}, f32[2,8,128]{2,1,0:T(8,128)}, u32[]{:S(2)}) copy-start(f32[2,8,128]{2,1,0:T(8,128)} %get-tuple-element.41) | copy-start | bytes 24580
  159.9 14.5 %copy-start.5 = (f32[5,8,64,128]{3,2,1,0:T(8,128)S(1)}, f32[5,8,64,128]{3,2,1,0:T(8,128)}, u32[]{:S(2)}) copy-start(f32[5,8,64,128]{3,2,1,0:T(8,128)} %get-tuple-element.29.refs_1_.prev) | copy-start | bytes 3932164
  162.1 25.4 %collective-permute-start.4 = (bf16[26,64,128]{2,1,0:T(8,128)(2,1)S(1)}, bf16[26,64,128]{2,1,0:T(8,128)(2,1)S(1)}, u32[]{:S(2)}, u32[]{:S(2)}) collective-permute-start(bf16[26,64,128]{2,1,0:T(8,128)(2,1)S(1)} %get-tuple-element.39), channel_id=1, source_target_pairs={{16,32},{48,64},{80,96},{112,128},{144,160},{176,192},{208,224},{2... | collective-permute-start | bytes 1277960 | tf_op jit(solution)/shard_map/ppermute | solution.py:579
  172.4 15.0 %collective-permute-start.5 = (bf16[26,64,128]{2,1,0:T(8,128)(2,1)S(1)}, bf16[26,64,128]{2,1,0:T(8,128)(2,1)S(1)}, u32[]{:S(2)}, u32[]{:S(2)}) collective-permute-start(bf16[26,64,128]{2,1,0:T(8,128)(2,1)S(1)} %get-tuple-element.40), channel_id=1, source_target_pairs={{0,16},{16,0},{32,48},{48,32},{64,80},{80,64},{96,112},{112,96},{1... | collective-permute-start | bytes 1277960 | tf_op jit(solution)/shard_map/ppermute | solution.py:585
  190.4 20.9 %copy-start.8 = (f32[5,8,64,128]{3,2,1,0:T(8,128)}, f32[5,8,64,128]{3,2,1,0:T(8,128)S(1)}, u32[]{:S(2)}) copy-start(f32[5,8,64,128]{3,2,1,0:T(8,128)S(1)} %get-tuple-element.45.refs_1_.cur) | copy-start | bytes 3932164
  190.4 20.9 %collective-permute-start.6 = (bf16[27,64,128]{2,1,0:T(8,128)(2,1)S(1)}, bf16[27,64,128]{2,1,0:T(8,128)(2,1)S(1)}, u32[]{:S(2)}, u32[]{:S(2)}) collective-permute-start(bf16[27,64,128]{2,1,0:T(8,128)(2,1)S(1)} %get-tuple-element.43), channel_id=1, source_target_pairs={{0,16},{16,0},{32,48},{48,32},{64,80},{80,64},{96,112},{112,96},{1... | collective-permute-start | bytes 1327112 | tf_op jit(solution)/shard_map/ppermute | solution.py:585
  192.3 41.7 %collective-permute-start.7 = (bf16[25,64,128]{2,1,0:T(8,128)(2,1)}, bf16[25,64,128]{2,1,0:T(8,128)(2,1)}, u32[]{:S(2)}, u32[]{:S(2)}) collective-permute-start(bf16[25,64,128]{2,1,0:T(8,128)(2,1)} %get-tuple-element.49), channel_id=1, source_target_pairs={{16,32},{48,64},{80,96},{112,128},{144,160},{176,192},{208,224},{2... | collective-permute-start | bytes 1228808 | tf_op jit(solution)/shard_map/ppermute | solution.py:579
  211.9 0.8 copy-start.6
  212.7 0.7 copy-start.13
  213.3 28.3 %all-to-all-start.1 = ((f32[16,3,8,128]{3,2,1,0:T(8,128)}), f32[16,3,8,128]{3,2,1,0:T(8,128)}, u32[]{:S(2)}, u32[]{:S(2)}) async-start(f32[16,3,8,128]{3,2,1,0:T(8,128)} %copy-done.13), calls=%async_computation.1 | async-start | bytes 393216 | tf_op jit(solution)/shard_map/all_to_all | solution.py:778
  226.7 1.3 copy-start.9
  228.0 6.0 %copy-start.7 = (bf16[27,64,128]{2,1,0:T(8,128)(2,1)S(1)}, bf16[27,64,128]{2,1,0:T(8,128)(2,1)}, u32[]{:S(2)}) copy-start(bf16[27,64,128]{2,1,0:T(8,128)(2,1)} %copy-done.6) | copy-start | bytes 1327108
  242.6 3.1 %collective-permute-start.8 = (f32[3,8,128]{2,1,0:T(8,128)S(1)}, f32[3,8,128]{2,1,0:T(8,128)S(1)}, u32[]{:S(2)}, u32[]{:S(2)}) collective-permute-start(f32[3,8,128]{2,1,0:T(8,128)S(1)} %reduce_sum.9), channel_id=1, source_target_pairs={{0,16},{16,0},{32,48},{48,32},{64,80},{80,64},{96,112},{112,96},{1... | collective-permute-start | bytes 36872 | tf_op jit(solution)/shard_map/ppermute | solution.py:585
